TPU v7x, 32 devices: a whole 2x2x4 slice. The times are simulated.
32 devices in a mesh: seq: 8 (over y, x, core), dp: 4 (over z).
Axes of the slice: x: 2, y: 2, z: 4, core: 2. Of those that a mesh axis runs over, the one named last changes fastest.
Arguments:
- tokens: bfloat16 [4, 6144, 1024], P('dp', 'seq'), may hold values from -6 to 6
- cotangent: bfloat16 [4, 6144, 1024], P('dp', 'seq'), may hold values from -6 to 6
- lengths: int32 [4, 4], P('dp'), may hold values from 768 to 3072, as said below
- attend_weight: float32 [1024, 3072], P('seq'), may hold values from -0.1875 to 0.1875
- merge_weight: float32 [1024, 1024], P('seq'), may hold values from -0.75 to 0.75
- expand_weight: float32 [1024, 4096], P('seq'), may hold values from -0.1875 to 0.1875
- shrink_weight: float32 [4096, 1024], P('seq'), may hold values from -0.09375 to 0.09375
- gains_biases: float32 [13312], P('seq'), may hold values from -0.8 to 2.25
- attend_first: float32 [1024, 3072], P('seq'), may hold values from -10 to 10
- attend_second: float32 [1024, 3072], P('seq'), may hold values from 0.24576 to 0.98304
- merge_first: float32 [1024, 1024], P('seq'), may hold values from -32 to 32
- merge_second: float32 [1024, 1024], P('seq'), may hold values from 2.21184 to 8.84736
- expand_first: float32 [1024, 4096], P('seq'), may hold values from -32 to 32
- expand_second: float32 [1024, 4096], P('seq'), may hold values from 2.21184 to 8.84736
- shrink_first: float32 [4096, 1024], P('seq'), may hold values from -64 to 64
- shrink_second: float32 [4096, 1024], P('seq'), may hold values from 8.84736 to 35.38944
- vector_first: float32 [13312], P('seq'), may hold values from -112 to 112
- vector_second: float32 [13312], P('seq'), may hold values from 24.576 to 98.304
Outputs:
- block_output: bfloat16 [4, 6144, 1024], P('dp', 'seq')
- input_grad: bfloat16 [4, 6144, 1024], P('dp', 'seq')
- attend_new: float32 [1024, 3072], P('seq')
- attend_mean: float32 [1024, 3072], P('seq')
- attend_square: float32 [1024, 3072], P('seq')
- merge_new: float32 [1024, 1024], P('seq')
- merge_mean: float32 [1024, 1024], P('seq')
- merge_square: float32 [1024, 1024], P('seq')
- expand_new: float32 [1024, 4096], P('seq')
- expand_mean: float32 [1024, 4096], P('seq')
- expand_square: float32 [1024, 4096], P('seq')
- shrink_new: float32 [4096, 1024], P('seq')
- shrink_mean: float32 [4096, 1024], P('seq')
- shrink_square: float32 [4096, 1024], P('seq')
- vector_new: float32 [13312], P('seq')
- vector_mean: float32 [13312], P('seq')
- vector_square: float32 [13312], P('seq')
- trust_norms: float32 [10], replicated
Inputs may be any that keep to these rules, and one draw needn't show every extreme that they name: Each row lists the lengths of its group's 4 sequences in order; they sum to 6144, and every row has one entry of exactly 768 and one of exactly 3072.
All inputs are finite; a program needn't handle non-finite values.
Results may differ from a plain program's by a relative error of at most 0.006.
The roundings to bfloat16 on the way count: a program that leaves them out, or rounds other values in their place, can miss the bound.
Values may be sent and summed in bfloat16 or wider, within the bound.
No kernel may reach another device: no remote copies, remote signals or barrier semaphores. Data moves between devices by JAX's collectives and lax.ppermute only.
A program may use at most 384 MiB of HBM per device.

v0:
```python
import math

import jax
import jax.numpy as jnp
import numpy as np
from jax import lax
from jax.sharding import PartitionSpec as P

D = 1024
FF = 4096
H = 16
HEAD = 64
ROT = 16
FEAT = 64
SPAN = 64
STEP = 10


precise = lax.Precision.HIGHEST
SCALE = 0.25
BASE = 10000.0
BETA_ONE = 0.9
BETA_TWO = 0.999
EPSILON = 1e-06
DECAY = 0.01
RATE = 0.25


def carried_in(part, axis, combine, identity, reverse):
    count = lax.axis_size(axis)
    place = lax.axis_index(axis)
    ahead = count - 1 - place if reverse else place
    gathered = jax.tree.map(lambda a: lax.all_gather(a, axis), part)
    state = jax.tree.map(lambda a, e: jnp.zeros_like(a) + jnp.asarray(e, a.dtype), part, identity)

    def one(lap, state):
        source = count - 1 - lap if reverse else lap
        return combine(
            state, jax.tree.map(lambda a: lax.dynamic_index_in_dim(a, source, 0, False), gathered)
        )

    return lax.fori_loop(0, ahead, one, state)


def feature_tables(head, feats):
    row_index = np.arange(head)[:, None]
    col_index = np.arange(head)[None, :]
    cosine = np.sqrt(2.0 / head) * np.cos(np.pi * (2 * col_index + 1) * row_index / (2.0 * head))
    cosine[0, :] = cosine[0, :] / np.sqrt(2.0)
    entry = np.arange(head)[:, None] + 1.0
    column = np.arange(feats)[None, :] + 0.5
    first_point = np.clip(np.mod(column / feats + entry * 0.7548776662, 1.0), 0.01, 0.99)
    second_point = np.mod(column * 0.569840291 + entry * 0.6180339887, 1.0)
    omega = np.sqrt(-2.0 * np.log(first_point)) * np.cos(2.0 * np.pi * second_point)
    matrix = cosine.T @ omega * SCALE
    weighting = (1.5 + np.cos(2.0 * np.pi * column[0] / feats)) / (1.5 * feats)
    return (matrix.astype(np.float32), weighting.astype(np.float32))


def features(heads_in):
    matrix, weighting = feature_tables(HEAD, FEAT)
    project = jnp.einsum("...e,ef->...f", heads_in, jnp.asarray(matrix), precision=precise)
    squares = SCALE * SCALE * jnp.sum(heads_in * heads_in, -1, keepdims=True)
    return jnp.asarray(weighting) * jnp.exp(project - 0.5 * squares)


def layer_norm(inputs, gain, shift):
    center = inputs - jnp.mean(inputs, -1, keepdims=True)
    spread = jnp.mean(center * center, -1, keepdims=True)
    return center * lax.rsqrt(spread + 1e-05) * gain + shift


def rotate(heads_in, offset):
    halfway = ROT // 2
    inverse = jnp.exp(jnp.arange(halfway, dtype=jnp.float32) * (-2.0 * math.log(BASE) / ROT))
    angles = offset.astype(jnp.float32)[..., None] * inverse
    cosine = jnp.cos(angles)[..., None, :]
    sines = jnp.sin(angles)[..., None, :]
    first_half = heads_in[..., :halfway]
    second_half = heads_in[..., halfway:ROT]
    return jnp.concatenate(
        [
            first_half * cosine - second_half * sines,
            second_half * cosine + first_half * sines,
            heads_in[..., ROT:],
        ],
        -1,
    )


def attend_local(qkv, state_in, total_in, offset, segment, previous):
    count = qkv.shape[0]
    number = count // SPAN
    pieces = qkv.reshape(number, SPAN, 3, H, HEAD)
    turns = offset.reshape(number, SPAN)
    query_feat = features(rotate(pieces[:, :, 0], turns))
    key_feat = features(rotate(pieces[:, :, 1], turns))
    value_rows = pieces[:, :, 2]
    labels = segment.reshape(number, SPAN)
    inner = jnp.arange(SPAN)[:, None] >= jnp.arange(SPAN)[None, :]

    def advance(carry, block):
        state, key_total, before = carry
        query_part, key_part, value_part, label_part = block
        causal = (inner & (label_part[:, None] == label_part[None, :])).astype(jnp.float32)
        scores = jnp.einsum("thf,shf->hts", query_part, key_part, precision=precise) * causal[None]
        reach = (label_part == before).astype(jnp.float32)
        weighted = jnp.einsum("hts,she->the", scores, value_part, precision=precise)
        weighted = weighted + reach[:, None, None] * jnp.einsum(
            "thf,hfe->the", query_part, state, precision=precise
        )
        totals = jnp.transpose(jnp.sum(scores, -1)) + reach[:, None] * jnp.einsum(
            "thf,hf->th", query_part, key_total, precision=precise
        )
        final = label_part[-1]
        keeping = (final == before).astype(jnp.float32)
        tailing = (label_part == final).astype(jnp.float32)
        kept = key_part * tailing[:, None, None]
        state = keeping * state + jnp.einsum("thf,the->hfe", kept, value_part, precision=precise)
        key_total = keeping * key_total + jnp.sum(kept, 0)
        return ((state, key_total, final), weighted / totals[..., None])

    start = (state_in, total_in, previous)
    _, outcome = lax.scan(
        jax.checkpoint(advance), start, (query_feat, key_feat, value_rows, labels)
    )
    return outcome.reshape(count, D)


def summary_state(qkv, offset, tailing):
    count = qkv.shape[0]
    pieces = qkv.reshape(count, 3, H, HEAD)
    key_feat = features(rotate(pieces[:, 1], offset)) * tailing[:, None, None]
    state = jnp.einsum("thf,the->hfe", key_feat, pieces[:, 2], precision=precise)
    return (state, jnp.sum(key_feat, 0))


def join_state(earlier, later):
    keeping = 1.0 - later[2]
    return (
        later[0] + keeping * earlier[0],
        later[1] + keeping * earlier[1],
        jnp.maximum(earlier[2], later[2]),
    )


def lamb_update(master, first, second, grad, decay):
    first = BETA_ONE * first + (1.0 - BETA_ONE) * grad
    second = BETA_TWO * second + (1.0 - BETA_TWO) * grad * grad
    update = (
        first / (1.0 - BETA_ONE**STEP) / (jnp.sqrt(second / (1.0 - BETA_TWO**STEP)) + EPSILON)
        + decay * master
    )
    return (first, second, update)


def per_device(
    tokens,
    cotangent,
    lengths,
    attend_weight,
    merge_weight,
    expand_weight,
    shrink_weight,
    gains_biases,
    attend_first,
    attend_second,
    merge_first,
    merge_second,
    expand_first,
    expand_second,
    shrink_first,
    shrink_second,
    vector_first,
    vector_second,
):
    local_rows = tokens.shape[1]
    inputs = tokens[0].astype(jnp.float32)
    grad_out = cotangent[0]
    grad_float = grad_out.astype(jnp.float32)
    masters = (attend_weight, merge_weight, expand_weight, shrink_weight, gains_biases)
    gathered = (
        lax.all_gather(attend_weight.astype(jnp.bfloat16), "seq", axis=0, tiled=True),
        lax.all_gather(merge_weight.astype(jnp.bfloat16), "seq", axis=0, tiled=True),
        lax.all_gather(expand_weight.astype(jnp.bfloat16), "seq", axis=0, tiled=True),
        lax.all_gather(shrink_weight.astype(jnp.bfloat16), "seq", axis=0, tiled=True),
        lax.all_gather(gains_biases.astype(jnp.bfloat16), "seq", axis=0, tiled=True),
    )
    attend, merge, expand, shrink, packed = gathered
    vector = packed.astype(jnp.float32)
    gain_one = vector[0:D]
    shift_one = vector[D : 2 * D]
    gain_two = vector[2 * D : 3 * D]
    shift_two = vector[3 * D : 4 * D]
    bias_attend = vector[4 * D : 7 * D]
    bias_merge = vector[7 * D : 8 * D]
    bias_expand = vector[8 * D : 8 * D + FF]
    bias_shrink = vector[8 * D + FF :]
    device = lax.axis_index("seq")
    positions = device * local_rows + jnp.arange(local_rows, dtype=jnp.int32)
    bounds = jnp.cumsum(lengths[0])
    passed = bounds[None, :] <= positions[:, None]
    segment = jnp.sum(passed.astype(jnp.int32), -1)
    starts = jnp.sum(jnp.where(passed, lengths[0][None, :], 0), -1)
    offset = positions - starts
    previous = jnp.sum((bounds <= device * local_rows - 1).astype(jnp.int32))
    tailing = (segment == segment[-1]).astype(jnp.float32)
    starting = (segment[-1] != previous).astype(jnp.float32)
    normed_one, norm_pull_one = jax.vjp(layer_norm, inputs, gain_one, shift_one)
    normed_two, norm_pull_two = jax.vjp(layer_norm, inputs, gain_two, shift_two)
    low_one = normed_one.astype(jnp.bfloat16)
    low_two = normed_two.astype(jnp.bfloat16)
    qkv = jnp.dot(low_one, attend, preferred_element_type=jnp.float32) + bias_attend
    state_loc, total_loc = summary_state(qkv, offset, tailing)
    identity = (jnp.zeros_like(state_loc), jnp.zeros_like(total_loc), jnp.zeros((), jnp.float32))
    state_in, total_in, _ = carried_in(
        (state_loc, total_loc, starting), "seq", join_state, identity, False
    )

    def attend_part(qkv_in, state_arg, total_arg):
        return attend_local(qkv_in, state_arg, total_arg, offset, segment, previous)

    mixed, attend_pull = jax.vjp(attend_part, qkv, state_in, total_in)
    mixed_low = mixed.astype(jnp.bfloat16)
    before_act = jnp.dot(low_two, expand, preferred_element_type=jnp.float32) + bias_expand
    active, gelu_pull = jax.vjp(lambda value: jax.nn.gelu(value, approximate=False), before_act)
    active_low = active.astype(jnp.bfloat16)
    result = inputs + jnp.dot(mixed_low, merge, preferred_element_type=jnp.float32) + bias_merge
    result = result + jnp.dot(active_low, shrink, preferred_element_type=jnp.float32) + bias_shrink
    block_output = result.astype(jnp.bfloat16)[None]
    grad_merge = jnp.einsum("td,te->de", mixed_low, grad_out, preferred_element_type=jnp.float32)
    grad_mixed = jnp.einsum("te,de->td", grad_out, merge, preferred_element_type=jnp.float32)
    grad_shrink = jnp.einsum("tf,td->fd", active_low, grad_out, preferred_element_type=jnp.float32)
    grad_active = jnp.einsum("td,fd->tf", grad_out, shrink, preferred_element_type=jnp.float32)
    grad_pre = gelu_pull(grad_active)[0].astype(jnp.bfloat16)
    grad_expand = jnp.einsum("td,tf->df", low_two, grad_pre, preferred_element_type=jnp.float32)
    grad_two = jnp.einsum("tf,df->td", grad_pre, expand, preferred_element_type=jnp.float32)
    grad_bias_out = jnp.sum(grad_float, 0)
    grad_bias_expand = jnp.sum(grad_pre.astype(jnp.float32), 0)
    grad_qkv, grad_state_in, grad_total_in = attend_pull(grad_mixed)
    grad_state_loc, grad_total_loc, _ = carried_in(
        (grad_state_in, grad_total_in, starting), "seq", join_state, identity, True
    )
    _, summary_pull = jax.vjp(lambda qkv_in: summary_state(qkv_in, offset, tailing), qkv)
    grad_qkv = grad_qkv + summary_pull((grad_state_loc, grad_total_loc))[0]
    grad_qkv_low = grad_qkv.astype(jnp.bfloat16)
    grad_attend = jnp.einsum("td,te->de", low_one, grad_qkv_low, preferred_element_type=jnp.float32)
    grad_one = jnp.einsum("te,de->td", grad_qkv_low, attend, preferred_element_type=jnp.float32)
    grad_bias_attend = jnp.sum(grad_qkv_low.astype(jnp.float32), 0)
    input_one, gain_grad_one, shift_grad_one = norm_pull_one(grad_one)
    input_two, gain_grad_two, shift_grad_two = norm_pull_two(grad_two)
    input_grad = (grad_float + input_one + input_two).astype(jnp.bfloat16)[None]
    grad_vector = jnp.concatenate(
        [
            gain_grad_one,
            shift_grad_one,
            gain_grad_two,
            shift_grad_two,
            grad_bias_attend,
            grad_bias_out,
            grad_bias_expand,
            grad_bias_out,
        ]
    )
    shares = (
        lax.psum_scatter(grad_attend, "seq", scatter_dimension=0, tiled=True),
        lax.psum_scatter(grad_merge, "seq", scatter_dimension=0, tiled=True),
        lax.psum_scatter(grad_expand, "seq", scatter_dimension=0, tiled=True),
        lax.psum_scatter(grad_shrink, "seq", scatter_dimension=0, tiled=True),
        lax.psum_scatter(grad_vector, "seq", scatter_dimension=0, tiled=True),
    )
    summed = lax.psum((shares[0], shares[1], shares[2], shares[3], shares[4]), "dp")
    firsts = (attend_first, merge_first, expand_first, shrink_first, vector_first)
    seconds = (attend_second, merge_second, expand_second, shrink_second, vector_second)
    decays = (DECAY, DECAY, DECAY, DECAY, 0.0)
    sectioned = []
    weight_squares = []
    update_squares = []
    for master, first, second, grad, decay in zip(masters, firsts, seconds, summed, decays):
        first, second, update = lamb_update(master, first, second, grad, decay)
        sectioned.append((master, first, second, update))
        weight_squares.append(jnp.sum(master * master))
        update_squares.append(jnp.sum(update * update))
    squares = lax.psum(jnp.stack(weight_squares + update_squares), "seq")
    roots = jnp.sqrt(squares)
    results = []
    for index_value in range(5):
        master, first, second, update = sectioned[index_value]
        fresh = master - RATE * (roots[index_value] / (roots[index_value + 5] + EPSILON)) * update
        results.extend([fresh, first, second])
    return (
        block_output,
        input_grad,
        results[0],
        results[1],
        results[2],
        results[3],
        results[4],
        results[5],
        results[6],
        results[7],
        results[8],
        results[9],
        results[10],
        results[11],
        results[12],
        results[13],
        results[14],
        roots,
    )


def solution(mesh):
    placed = (
        P("dp", "seq", None),
        P("dp", "seq", None),
        P("dp", None),
        P("seq", None),
        P("seq", None),
        P("seq", None),
        P("seq", None),
        P("seq"),
        P("seq", None),
        P("seq", None),
        P("seq", None),
        P("seq", None),
        P("seq", None),
        P("seq", None),
        P("seq", None),
        P("seq", None),
        P("seq"),
        P("seq"),
    )
    return jax.shard_map(
        per_device,
        mesh=mesh,
        in_specs=placed,
        out_specs=(
            P("dp", "seq", None),
            P("dp", "seq", None),
            P("seq", None),
            P("seq", None),
            P("seq", None),
            P("seq", None),
            P("seq", None),
            P("seq", None),
            P("seq", None),
            P("seq", None),
            P("seq", None),
            P("seq", None),
            P("seq", None),
            P("seq", None),
            P("seq"),
            P("seq"),
            P("seq"),
            P(),
        ),
        check_vma=False,
    )
```

profile of v0, /device:TPU:0, one launch (start us, length us, event | category | flops | bytes accessed | tf_op | source)
XLA Modules:
  0.0 1869.4 jit_solution(8323115967165696601)
XLA Ops:
  16.0 15.3 all-reduce.14
  55.6 33.8 %all-gather.12.cloned.1.call-done = bf16[1024,3072]{1,0:T(8,128)(2,1)} async-done(((bf16[128,3072]{1,0:T(8,128)(2,1)}), bf16[1024,3072]{1,0:T(8,128)(2,1)}) %all-gather.12.cloned.1.call-update) | async-done | bytes 6291472 | tf_op jit(solution)/shard_map/all_gather | solution.py:183
  100.1 14.3 reshape.391
  174.6 19.4 %multiply_subtract_fusion = (f32[12,64,16,8]{3,1,2,0:T(8,128)}, f32[12,64,16,8]{3,1,2,0:T(8,128)}, f32[12,64,16,8]{3,1,2,0:T(8,128)}, f32[12,64,16,8]{3,1,2,0:T(8,128)}) fusion(f32[12,64,16,64]{3,1,2,0:T(8,128)} %copy-done.1, f32[12,64,8]{2,1,0:T(8,128)S(1)} %copy-done.28, f32[12,64,8]{2,1,0:T(8,128)S(1)} %get-tuple-element.937, ...), kind=kLoop, calls=%fused_computation.142 | loop fusion | flops 1179648 | bytes 3194880 | tf_op jit(solution)/shard_map/jvp()/sub | solution.py:83
  213.7 18.1 fusion.164
  231.8 22.2 %fusion.63 = (f32[12,64,16,64]{1,3,2,0:T(8,128)}, f32[12,64,16,64]{1,3,2,0:T(8,128)}, f32[12,64,16,64]{1,3,2,0:T(8,128)}) fusion(f32[12,64,16]{1,2,0:T(8,128)S(1)} %broadcast_multiply_fusion.1, f32[64]{0:T(128)S(1)} %copy-done.94, f32[12,64,16,64]{1,3,2,0:T(8,128)S(1)} %fusion.164, f32[12,64,16]{1,2,0:T(8,128)S(1)} %broadcast_multiply_fusion.2, ...), kind=kOutput, calls=%fused_computation.148 | convolution fusion | flops 607125504 | bytes 15843584 | tf_op jit(solution)/shard_map/jvp(...e,ef->...f)/dot_general | solution.py:62
  284.3 209.0 %while.78 = (s32[]{:T(128)}, f32[16,64,64]{2,1,0:T(8,128)S(1)}, f32[16,64]{1,0:T(8,128)S(1)}, s32[]{:T(128)}, bf16[12,64,16,64]{1,3,2,0:T(8,128)(2,1)}, /*index=...) while((s32[]{:T(128)}, f32[16,64,64]{2,1,0:T(8,128)S(1)}, ...), condition=%wide.region_15.16_spmd.clone, body=%wide.region_12.15_spmd.clone.sunk | while | flops 202787072 | bytes 7175871 | solution.py:124
  503.8 451.3 %while.79 = (s32[]{:T(128)}, f32[16,64,64]{2,1,0:T(8,128)S(1)}, f32[16,64]{1,0:T(8,128)}, f32[12,64,16,64]{1,3,2,0:T(8,128)}, f32[12,64,16,64]{1,3,2,0:T(8,128)}...) while((s32[]{:T(128)}, f32[16,64,64]{2,1,0:T(8,128)S(1)}, ...), condition=%wide.region_19.20_spmd.clone, body=%wide.region_16.19_spmd.clone.sunk | while | flops 556949760 | bytes 18178236 | solution.py:124
  970.7 15.8 multiply_add_fusion.3
  991.1 15.3 multiply_add_fusion.2
  1020.7 26.3 %all-gather.3 = f32[128,64]{1,0:T(8,128)S(1)} all-gather(f32[16,64]{1,0:T(8,128)S(1)} %copy-done.72), channel_id=5, replica_groups=mesh['seq'=8,'dp'=4] {'seq'}, dimensions={0}, use_global_device_ids=true | all-gather | bytes 36864 | tf_op jit(solution)/shard_map/all_gather | solution.py:33
  1052.3 19.8 %multiply_add_fusion.7 = (f32[12,64,16,8]{3,1,2,0:T(8,128)}, f32[12,64,16,8]{3,1,2,0:T(8,128)}, f32[12,64,16,8]{3,1,2,0:T(8,128)}, f32[12,64,16,8]{3,1,2,0:T(8,128)}) fusion(f32[12,64,16,64]{3,1,2,0:T(8,128)} %copy-done.2, f32[12,64,8]{2,1,0:T(8,128)S(1)} %copy-done.29, f32[12,64,8]{2,1,0:T(8,128)S(1)} %get-tuple-element.937, f32[12,64,16,64]{3,1,2,0:T(8,128)} %copy-done.3), kind=kLoop, calls=%fused_computation.137 | loop fusion | flops 1376256 | bytes 3194880 | tf_op jit(solution)/shard_map/transpose(jvp())/add_any | solution.py:83
  1092.2 17.8 while.77
  1131.2 18.0 reshape.394
  1149.2 23.3 %copy.207 = f32[12,64,3,16,64]{4,1,3,0,2:T(8,128)} copy(f32[12,64,3,16,64]{1,0,4,3,2:T(8,128)} %reshape.394) | data formatting | bytes 18874368 | tf_op jit(solution)/shard_map/transpose(jvp())/reshape | solution.py:132
  1172.5 23.5 %convert_reduce_fusion = (f32[3,16,64]{2,1,0:T(8,128)}, bf16[12,64,3,16,64]{4,1,3,0,2:T(8,128)(2,1)}, f32[12,64,3,16,64]{4,1,3,0,2:T(8,128)}) fusion(f32[12,64,3,16,64]{4,1,3,0,2:T(8,128)} %copy.207, f32[12,64,1,16,64]{4,1,3,0,2:T(8,128)} %add_bitcast_fusion.2, f32[12,64,1,16,64]{4,1,3,0,2:T(8,128)} %add_bitcast_fusion.3, f32[12,64,1,16,64]{4,1,3,0,2:T(8,128)} %bitcast.534), kind=kLoop, calls=%fused_computation.102 | loop fusion | flops 14152704 | bytes 33042432 | tf_op jit(solution)/shard_map/reduce_sum | solution.py:249
  1196.0 14.6 copy.208
  1235.0 38.8 %multiply_convert_fusion = (bf16[768,4096]{1,0:T(8,128)(2,1)}, f32[768,4096]{1,0:T(8,128)}, f32[768,4096]{1,0:T(8,128)}) fusion(f32[4096]{0:T(1024)S(1)} %slice.173, bf16[1024,4096]{1,0:T(8,128)(2,1)} %all-gather.16.cloned.1.call-done, bf16[1,768,1024]{2,1,0:T(8,128)(2,1)S(1)} %copy-done.5, f32[1024]{0:T(1024)S(1)} %copy-done.69, f32[1024]{0:T(1024)S(1)} %copy-done.68, ...), kind=kOutput, calls=%fused_computation.108 | convolution fusion | flops 6654787584 | bytes 41449472 | tf_op jit(solution)/shard_map/dot_general | solution.py:225
  1273.8 21.5 %convert_reduce_fusion.1 = (f32[4096]{0:T(1024)S(1)}, bf16[768,4096]{1,0:T(8,128)(2,1)}) fusion(f32[768,4096]{1,0:T(8,128)} %get-tuple-element.898, bf16[4096,1024]{1,0:T(8,128)(2,1)} %all-gather.18.cloned.1.call-done, bf16[1,768,1024]{2,1,0:T(8,128)(2,1)} %param.35, f32[768,4096]{1,0:T(8,128)} %get-tuple-element.957, f32[4096]{0:T(1024)S(1)} %slice.173), kind=kOutput, calls=%fused_computation.106 | convolution fusion | flops 6495924224 | bytes 41451520 | tf_op jit(solution)/shard_map/td,fd->tf/dot_general | solution.py:234
  1326.2 120.0 %reduce-scatter.9.cloned.1.call-done = f32[128,4096]{1,0:T(8,128)} async-done(((f32[1024,4096]{1,0:T(8,128)}), f32[128,4096]{1,0:T(8,128)}) %reduce-scatter.9.cloned.1.call-update) | async-done | bytes 2097168 | tf_op jit(solution)/shard_map/reduce_scatter | solution.py:268
  1446.1 119.8 %reduce-scatter.11.cloned.1.call-done = f32[512,1024]{1,0:T(8,128)} async-done(((f32[4096,1024]{1,0:T(8,128)}), f32[512,1024]{1,0:T(8,128)}) %reduce-scatter.11.cloned.1.call-update) | async-done | bytes 2097168 | tf_op jit(solution)/shard_map/reduce_scatter | solution.py:269
  1595.5 15.6 reshape.392
  1641.8 25.1 %all-reduce.15 = f32[13312]{0:T(1024)S(1)} all-reduce(f32[13312]{0:T(1024)S(1)} %constant_dynamic-update-slice_fusion.2), channel_id=10, replica_groups=mesh['seq'=8,'dp'=4] {'seq'}, use_global_device_ids=true, to_apply=%region_53.54.clone | all-reduce | flops 13312 | bytes 106496
  1680.3 112.9 %all-reduce.19.cloned.1.call-done = (f32[128,3072]{1,0:T(8,128)}, f32[128,1024]{1,0:T(8,128)}, f32[128,4096]{1,0:T(8,128)}, f32[512,1024]{1,0:T(8,128)}) async-done(((f32[128,3072]{1,0:T(8,128)}, f32[128,1024]{1,0:T(8,128)}, f32[128,4096]{1,0:T(8,128)}, f32[512,1024]{1,0:T(8,128)}), (f32[128,3072]{1,0:T(8,128)}, f32[128,1024]{1,0:T(8,128)}, f32[128,4096]{1,0:T(8,128)}, ...) | async-done | bytes 6291472 | tf_op jit(solution)/shard_map/psum | solution.py:272
  (1272 shorter events, 1073.6 us)
Async XLA Ops:
  7.2 33.0 %copy-start.4 = (bf16[1,768,1024]{2,1,0:T(8,128)(2,1)S(1)}, bf16[1,768,1024]{2,1,0:T(8,128)(2,1)}, u32[]{:S(2)}) copy-start(bf16[1,768,1024]{2,1,0:T(8,128)(2,1)} %param.34) | copy-start | bytes 4718596
  7.2 41.3 %all-gather.14.cloned.1.call-start = ((), (), s32[]{:S(2)}) async-start(), calls=%async_computation.5 | async-start | bytes 2359296 | tf_op jit(solution)/shard_map/all_gather | solution.py:184
  9.2 80.3 %all-gather.12.cloned.1.call-start = ((), (), s32[]{:S(2)}) async-start(), calls=%async_computation.4 | async-start | bytes 7077888 | tf_op jit(solution)/shard_map/all_gather | solution.py:183
  11.7 272.0 %all-gather.20.cloned.1.call-start = ((), (), s32[]{:S(2)}) async-start(), calls=%async_computation.12 | async-start | bytes 4718592 | tf_op jit(solution)/shard_map/all_gather | solution.py:33
  43.6 125.0 %copy-start.85 = (f32[768]{0:T(1024)}, f32[768]{0:T(1024)S(1)}, u32[]{:S(2)}) copy-start(f32[768]{0:T(1024)S(1)} %compare_convert_fusion.5) | copy-start | bytes 9220
  43.6 45.8 %copy-start.41 = (f32[768]{0:T(1024)}, f32[768]{0:T(1024)S(1)}, u32[]{:S(2)}) copy-start(f32[768]{0:T(1024)S(1)} %broadcast_multiply_fusion.4) | copy-start | bytes 9220
  44.8 44.7 %copy-start.54 = (f32[768]{0:T(1024)}, f32[768]{0:T(1024)S(1)}, u32[]{:S(2)}) copy-start(f32[768]{0:T(1024)S(1)} %fusion.137) | copy-start | bytes 9220
  45.4 44.1 %copy-start.65 = (f32[1024]{0:T(1024)}, f32[1024]{0:T(1024)S(1)}, u32[]{:S(2)}) copy-start(f32[1024]{0:T(1024)S(1)} %get-tuple-element.931) | copy-start | bytes 12292
  45.4 44.1 %copy-start.70 = (f32[1024]{0:T(1024)}, f32[1024]{0:T(1024)S(1)}, u32[]{:S(2)}) copy-start(f32[1024]{0:T(1024)S(1)} %get-tuple-element.936) | copy-start | bytes 12292
  46.2 117.9 %copy-start.73 = (f32[768,8]{0,1:T(8,128)}, f32[768,8]{0,1:T(8,128)S(1)}, u32[]{:S(2)}) copy-start(f32[768,8]{0,1:T(8,128)S(1)} %get-tuple-element.939) | copy-start | bytes 73732
  174.6 917.6 %all-gather.22.cloned.1.call-start = ((), (), s32[]{:S(2)}) async-start(), calls=%async_computation.13 | async-start | bytes 4718592 | tf_op jit(solution)/shard_map/all_gather | solution.py:33
  955.9 279.0 %all-gather.16.cloned.1.call-start = ((), (), s32[]{:S(2)}) async-start(), calls=%async_computation.6 | async-start | bytes 9437184 | tf_op jit(solution)/shard_map/all_gather | solution.py:185
  958.7 315.1 %all-gather.18.cloned.1.call-start = ((), (), s32[]{:S(2)}) async-start(), calls=%async_computation.7 | async-start | bytes 9437184 | tf_op jit(solution)/shard_map/all_gather | solution.py:186
  959.9 364.0 %reduce-scatter.7.cloned.1.call-start = ((), (), s32[]{:S(2)}) async-start(), calls=%async_computation.9 | async-start | bytes 4718592 | tf_op jit(solution)/shard_map/reduce_scatter | solution.py:267
  1015.1 31.9 %copy-start.47 = (bf16[1,768,1024]{2,1,0:T(8,128)(2,1)S(1)}, bf16[1,768,1024]{2,1,0:T(8,128)(2,1)}, u32[]{:S(2)}) copy-start(bf16[1,768,1024]{2,1,0:T(8,128)(2,1)} %param.35) | copy-start | bytes 4718596
  1072.1 254.1 %reduce-scatter.5.cloned.1.call-start = ((), (), s32[]{:S(2)}) async-start(), calls=%async_computation.8 | async-start | bytes 14155776 | tf_op jit(solution)/shard_map/reduce_scatter | solution.py:266
  1234.2 211.9 %reduce-scatter.9.cloned.1.call-start = ((), (), s32[]{:S(2)}) async-start(), calls=%async_computation.10 | async-start | bytes 18874368 | tf_op jit(solution)/shard_map/reduce_scatter | solution.py:268
  1308.9 257.1 %reduce-scatter.11.cloned.1.call-start = ((), (), s32[]{:S(2)}) async-start(), calls=%async_computation.11 | async-start | bytes 18874368 | tf_op jit(solution)/shard_map/reduce_scatter | solution.py:269
  1323.3 469.9 %all-reduce.19.cloned.1.call-start = ((), (), s32[]{:S(2)}) async-start(), calls=%async_computation.14 | async-start | bytes 12582912 | tf_op jit(solution)/shard_map/psum | solution.py:272
  1638.4 41.2 %copy-start.84 = (f32[1664]{0:T(1024)S(1)}, f32[1664]{0:T(1024)}, u32[]{:S(2)}) copy-start(f32[1664]{0:T(1024)} %param.41) | copy-start | bytes 19972
  1638.5 41.2 %copy-start.96 = (f32[1664]{0:T(1024)S(1)}, f32[1664]{0:T(1024)}, u32[]{:S(2)}) copy-start(f32[1664]{0:T(1024)} %param.50) | copy-start | bytes 19972
  1638.5 41.2 %copy-start.97 = (f32[1664]{0:T(1024)S(1)}, f32[1664]{0:T(1024)}, u32[]{:S(2)}) copy-start(f32[1664]{0:T(1024)} %param.51) | copy-start | bytes 19972
  1680.3 170.7 %copy-start.92 = (f32[1664]{0:T(1024)}, f32[1664]{0:T(1024)S(1)}, u32[]{:S(2)}) copy-start(f32[1664]{0:T(1024)S(1)} %get-tuple-element.881) | copy-start | bytes 19972
  1680.3 170.7 %copy-start.93 = (f32[1664]{0:T(1024)}, f32[1664]{0:T(1024)S(1)}, u32[]{:S(2)}) copy-start(f32[1664]{0:T(1024)S(1)} %get-tuple-element.882) | copy-start | bytes 19972
  (237 other events, 1490.8 us)
Sparse Core Ops, SparseCore 0:
  10.5 30.8 all-gather.13
  43.9 45.5 all-gather.11
  174.7 36.7 all-gather.19
  956.0 54.4 all-gather.21
  1012.8 54.5 all-gather.15
  1069.8 54.3 all-gather.17
  1127.5 51.3 reduce-scatter.6
  1234.3 91.8 reduce-scatter.4
  1330.2 115.9 reduce-scatter.8
  1450.0 115.9 reduce-scatter.10
  1568.7 224.4 all-reduce.18
where the time goes:
time: 1890 us; the launch traced here: 1870 us
  matrix products  580 us (31%)
  local copies, waits for them, and re-layouts  465 us (25%)
  waiting for transfers between devices  389 us (21%)
  other arithmetic  262 us (14%)
  blocking collectives  110 us (6%)
  loops' own time  38.5 us (2%)
  between operations  24 us (1%)
    reduce_scatter x1, waiting for transfers between devices, per_device(): lax.psum_scatter(grad_expand, 'seq', scatter_dimension=0, tiled=True)  120 us
    reduce_scatter x1, waiting for transfers between devices, per_device(): lax.psum_scatter(grad_shrink, 'seq', scatter_dimension=0, tiled=True)  120 us
    psum x1, waiting for transfers between devices, per_device(): lax.psum((shares[0], shares[1], shares[2], shares[3], shares[4]), 'dp')  113 us
    dot_general x48, matrix products, advance(): jnp.einsum('thf,hfe->the', query_part, state, precision=precise)  92.3 us
    squeeze x72, local copies, waits for them, and re-layouts, attend_local(): lax.scan(jax.checkpoint(advance), start, (query_feat, key_feat, value_row...  86.7 us
    dot_general x6, matrix products, features(): jnp.einsum('...e,ef->...f', heads_in, jnp.asarray(matrix), precision=prec...  78.6 us
    dynamic_update_slice x84, local copies, waits for them, and re-layouts, attend_local(): lax.scan(jax.checkpoint(advance), start, (query_feat, key_feat, value_row...  78.5 us
    dot_general x48, matrix products, advance(): weighted = jnp.einsum('hts,she->the', scores, value_part, precision=precise)  65.8 us
  transfers between devices with their start and end apart: 11, of which 5 were waited for; matrix products, arithmetic and copies ran while one was open for 28% of the time, Pallas kernels for 0%

commit v1 on v0

v1 whole, which is shorter than its diff:
```python
import math

import jax
import jax.numpy as jnp
import ml_dtypes
import numpy as np
from jax import lax
from jax.experimental import pallas as pl
from jax.experimental.pallas import tpu as pltpu
from jax.sharding import PartitionSpec as P

D = 1024
FF = 4096
H = 16
HEAD = 64
ROT = 16
FEAT = 64
STEP = 10

SCALE = 0.25
BASE = 10000.0
BETA_ONE = 0.9
BETA_TWO = 0.999
EPSILON = 1e-06
DECAY = 0.01
RATE = 0.25

CHUNK = 256
LANES = 256
EACH = LANES // HEAD
NGROUP = D // LANES
STATE = HEAD + 8
ROOM = 56 * 1024 * 1024
f32 = jnp.float32
bf16 = jnp.bfloat16


def feature_tables(head, feats):
    row_index = np.arange(head)[:, None]
    col_index = np.arange(head)[None, :]
    cosine = np.sqrt(2.0 / head) * np.cos(np.pi * (2 * col_index + 1) * row_index / (2.0 * head))
    cosine[0, :] = cosine[0, :] / np.sqrt(2.0)
    entry = np.arange(head)[:, None] + 1.0
    column = np.arange(feats)[None, :] + 0.5
    first_point = np.clip(np.mod(column / feats + entry * 0.7548776662, 1.0), 0.01, 0.99)
    second_point = np.mod(column * 0.569840291 + entry * 0.6180339887, 1.0)
    omega = np.sqrt(-2.0 * np.log(first_point)) * np.cos(2.0 * np.pi * second_point)
    matrix = cosine.T @ omega * SCALE
    weighting = (1.5 + np.cos(2.0 * np.pi * column[0] / feats)) / (1.5 * feats)
    return (matrix.astype(np.float32), weighting.astype(np.float32))


def group_tables():
    matrix, weighting = feature_tables(HEAD, FEAT)
    eye = np.eye(EACH, dtype=np.float32)
    wide = np.kron(eye, matrix)
    high = wide.astype(ml_dtypes.bfloat16)
    low = (wide - high.astype(np.float32)).astype(ml_dtypes.bfloat16)
    ones = np.kron(eye, np.ones((HEAD, HEAD), np.float32)).astype(ml_dtypes.bfloat16)
    return np.stack([high, low, ones]), np.tile(weighting, EACH)[None, :]


def dot_nn(a, b):
    return lax.dot_general(a, b, (((1,), (0,)), ((), ())), preferred_element_type=f32)


def dot_nt(a, b):
    return lax.dot_general(a, b, (((1,), (1,)), ((), ())), preferred_element_type=f32)


def dot_tn(a, b):
    return lax.dot_general(a, b, (((0,), (0,)), ((), ())), preferred_element_type=f32)


def halves(value):
    high = value.astype(bf16)
    return high, (value - high.astype(f32)).astype(bf16)


def dot_three(dot, high, low, other_high, other_low):
    return dot(high, other_high) + dot(low, other_high) + dot(high, other_low)


def twice(table):
    return jnp.concatenate([table, table], axis=1)


def flat(value):
    return value.reshape(-1, value.shape[-1])


def head_mask(index, dtype):
    lane = lax.broadcasted_iota(jnp.int32, (1, LANES), 1)
    inside = (lane >= index * HEAD) & (lane < (index + 1) * HEAD)
    return jnp.where(inside, 1.0, 0.0).astype(dtype)


def turn(value, table_ref):
    cosine, first, second = (twice(table_ref[i]) for i in range(3))
    half = ROT // 2
    return (
        value * cosine
        + pltpu.roll(value, LANES - half, 1) * first
        + pltpu.roll(value, half, 1) * second
    )


def turn_back(grad, table_ref):
    cosine, first, second = (twice(table_ref[i]) for i in range(3))
    half = ROT // 2
    return (
        grad * cosine
        + pltpu.roll(grad * first, half, 1)
        + pltpu.roll(grad * second, LANES - half, 1)
    )


def phi(value, const_ref, weight_ref):
    high, low = halves(value)
    project = (
        dot_nn(high, const_ref[0]) + dot_nn(low, const_ref[0]) + dot_nn(high, const_ref[1])
    )
    top, rest = halves(value * value)
    squares = dot_nn(top, const_ref[2]) + dot_nn(rest, const_ref[2])
    return weight_ref[...] * jnp.exp(project - (0.5 * SCALE * SCALE) * squares)


def phi_back(grad, feats, value, const_ref):
    high, low = halves(grad * feats)
    project = (
        dot_nt(high, const_ref[0]) + dot_nt(low, const_ref[0]) + dot_nt(high, const_ref[1])
    )
    total = dot_nn(high, const_ref[2]) + dot_nn(low, const_ref[2])
    return project - (SCALE * SCALE) * value * total


def spread(state_ref, const_ref):
    packed = state_ref[0:HEAD, :]
    tall = jnp.concatenate([packed] * EACH, axis=0)
    return tall * const_ref[2].astype(f32)


def squeeze_state(state):
    total = state[0:HEAD]
    for index in range(1, EACH):
        total = total + state[index * HEAD : (index + 1) * HEAD]
    return total


def qkv_kernel(
    h_ref, wq_ref, wk_ref, wv_ref, b_ref, table_ref, marks_ref, const_ref, weight_ref,
    q_ref, k_ref, v_ref, vl_ref, uq_ref, uk_ref, s_ref,
):
    rows = h_ref[...]
    query = turn(dot_nn(rows, flat(wq_ref[...])) + b_ref[0:1, :], table_ref)
    uq_ref[...] = query.astype(bf16)
    q_ref[...] = phi(query, const_ref, weight_ref).astype(bf16)
    key = turn(dot_nn(rows, flat(wk_ref[...])) + b_ref[1:2, :], table_ref)
    uk_ref[...] = key.astype(bf16)
    feats = phi(key, const_ref, weight_ref).astype(bf16)
    k_ref[...] = feats
    value, value_low = halves(dot_nn(rows, flat(wv_ref[...])) + b_ref[2:3, :])
    v_ref[...] = value
    vl_ref[...] = value_low
    segment = twice(table_ref[3])
    tail = jnp.where(segment == marks_ref[15:16, :], 1.0, 0.0)
    kept = feats.astype(f32) * tail
    kept_low = kept.astype(bf16)
    state = (dot_tn(kept_low, value) + dot_tn(kept_low, value_low)) * const_ref[2].astype(f32)
    s_ref[0:HEAD, :] = squeeze_state(state)
    s_ref[HEAD:STATE, :] = jnp.broadcast_to(jnp.sum(kept, 0, keepdims=True), (8, LANES))


def attend_kernel(
    q_ref, k_ref, v_ref, vl_ref, uq_ref, s_ref, g_ref, wm_ref, table_ref, row_ref, marks_ref, const_ref, core_ref,
    mixed_ref, dq_ref, dk_ref, dv_ref, ds_ref, bias_ref, out_ref, send_ref, keep_ref,
    dnum_ref, dlow_ref, dden_ref,
):
    count = q_ref.shape[0] // CHUNK
    merge = flat(wm_ref[...])
    state = spread(s_ref, const_ref)
    total = s_ref[HEAD : HEAD + 1, :]
    blocks = const_ref[2].astype(f32)
    masks = [head_mask(index, bf16) for index in range(EACH)]
    lower = lax.broadcasted_iota(jnp.int32, (CHUNK, CHUNK), 0) >= lax.broadcasted_iota(
        jnp.int32, (CHUNK, CHUNK), 1
    )
    bias = jnp.zeros((1, LANES), f32)
    for c in range(count):
        here = pl.ds(c * CHUNK, CHUNK)
        query, key = q_ref[here, :], k_ref[here, :]
        value, value_low = v_ref[here, :], vl_ref[here, :]
        segment = twice(table_ref[3, here, :])
        before, final = marks_ref[c : c + 1, :], marks_ref[8 + c : 9 + c, :]
        reach = jnp.where(segment == before, 1.0, 0.0)
        tail = jnp.where(segment == final, 1.0, 0.0)
        keep = jnp.where(final == before, 1.0, 0.0)
        causal = lower & (segment == row_ref[0:1, c * CHUNK : (c + 1) * CHUNK])
        grad_mixed = dot_nt(g_ref[here, :], merge)
        state_high, state_low = halves(state)
        reached = query * reach.astype(bf16)
        number = dot_nn(reached, state_high) + dot_nn(reached, state_low)
        top, rest = halves(reached.astype(f32) * total)
        totals = dot_nn(top, const_ref[2]) + dot_nn(rest, const_ref[2])
        scores = []
        for index in range(EACH):
            mask = masks[index]
            score = jnp.where(causal, dot_nt(query, key * mask), 0.0)
            totals = totals + jnp.sum(score, 1, keepdims=True) * mask.astype(f32)
            high, low = halves(score)
            scores.append((high, low))
            number = number + dot_three(dot_nn, high, low, value * mask, value_low * mask)
        mixed = number / totals
        mixed_ref[here, :] = mixed.astype(bf16)
        slope_number = grad_mixed / totals
        dnum, dlow = halves(slope_number)
        dnum_ref[here, :] = dnum
        dlow_ref[here, :] = dlow
        top, rest = halves(slope_number * mixed)
        dden = -(dot_nn(top, const_ref[2]) + dot_nn(rest, const_ref[2]))
        dden_ref[here, :] = dden
        grad_query = reach * (
            dot_three(dot_nt, dnum, dlow, state_high, state_low) + dden * total
        )
        grad_key = jnp.zeros((CHUNK, LANES), f32)
        grad_value = jnp.zeros((CHUNK, LANES), f32)
        for index in range(EACH):
            mask = masks[index]
            column = dden[:, index * HEAD : index * HEAD + 1]
            slope = dot_three(dot_nt, dnum, dlow, value * mask, value_low * mask) + column
            high, low = halves(jnp.where(causal, slope, 0.0))
            grad_query = grad_query + dot_nn(high, key * mask) + dot_nn(low, key * mask)
            grad_key = grad_key + dot_tn(high, query * mask) + dot_tn(low, query * mask)
            high, low = scores[index]
            grad_value = grad_value + dot_three(dot_tn, high, low, dnum * mask, dlow * mask)
        dk_ref[here, :] = grad_key
        dv_ref[here, :] = grad_value
        grad = phi_back(grad_query, query.astype(f32), uq_ref[here, :].astype(f32), const_ref)
        grad = turn_back(grad, table_ref.at[:, here, :]).astype(bf16)
        dq_ref[here, :] = grad
        bias = bias + jnp.sum(grad.astype(f32), 0, keepdims=True)
        if c < count - 1:
            kept = key.astype(f32) * tail
            kept_low = kept.astype(bf16)
            state = keep * state + blocks * (dot_tn(kept_low, value) + dot_tn(kept_low, value_low))
            total = keep * total + jnp.sum(kept, 0, keepdims=True)
    bias_ref[...] = jnp.broadcast_to(bias, (8, LANES))
    grad_state = jnp.zeros((LANES, LANES), f32)
    grad_total = jnp.zeros((1, LANES), f32)
    for c in reversed(range(count)):
        here = pl.ds(c * CHUNK, CHUNK)
        segment = twice(table_ref[3, here, :])
        before, final = marks_ref[c : c + 1, :], marks_ref[8 + c : 9 + c, :]
        reach = jnp.where(segment == before, 1.0, 0.0)
        tail = jnp.where(segment == final, 1.0, 0.0)
        keep = jnp.where(final == before, 1.0, 0.0)
        if c < count - 1:
            high, low = halves(grad_state)
            dk_ref[here, :] += tail * (
                dot_three(dot_nt, v_ref[here, :], vl_ref[here, :], high, low) + grad_total
            )
            dv_ref[here, :] += tail * (dot_nn(k_ref[here, :], high) + dot_nn(k_ref[here, :], low))
        reached = q_ref[here, :].astype(f32) * reach
        low_reached = reached.astype(bf16)
        grad_state = keep * grad_state + blocks * (
            dot_tn(low_reached, dnum_ref[here, :]) + dot_tn(low_reached, dlow_ref[here, :])
        )
        grad_total = keep * grad_total + jnp.sum(reached * dden_ref[here, :], 0, keepdims=True)
    ds_ref[0:HEAD, :] = squeeze_state(grad_state)
    ds_ref[HEAD:STATE, :] = jnp.broadcast_to(grad_total, (8, LANES))
    mixed = mixed_ref[...]
    accumulate(out_ref, dot_nn(mixed, merge))
    part_owners(dot_tn(mixed, g_ref[...]), core_ref, send_ref, keep_ref)


def accumulate(ref, value):
    first = pl.program_id(0) == 0

    @pl.when(first)
    def _():
        ref[...] = value

    @pl.when(jnp.logical_not(first))
    def _():
        ref[...] += value


def part_owners(value, core_ref, send_ref, keep_ref):
    held = send_ref.shape
    pairs = value.reshape((held[0], 2) + held[1:]).astype(send_ref.dtype)
    even, odd = pairs[:, 0], pairs[:, 1]
    first = core_ref[0] == 0
    keep, send = jnp.where(first, even, odd), jnp.where(first, odd, even)
    keep_ref[...], send_ref[...] = keep, send


def finish_kernel(
    k_ref, v_ref, vl_ref, uk_ref, dq_ref, dk_ref, dv_ref, ds_ref, table_ref, marks_ref, const_ref,
    wq_ref, wk_ref, wv_ref, ht_ref, core_ref, sent_ref, kept_ref, done_ref,
    bias_ref, dh_ref, send_ref, keep_ref,
):
    segment = twice(table_ref[3])
    tail = jnp.where(segment == marks_ref[15:16, :], 1.0, 0.0)
    high, low = halves(spread(ds_ref, const_ref))
    key, value = k_ref[...], v_ref[...]
    grad_key = dk_ref[...] + tail * (
        dot_three(dot_nt, value, vl_ref[...], high, low) + ds_ref[HEAD : HEAD + 1, :]
    )
    grad_value = dv_ref[...] + tail * (dot_nn(key, high) + dot_nn(key, low))
    grad = phi_back(grad_key, key.astype(f32), uk_ref[...].astype(f32), const_ref)
    grad = turn_back(grad, table_ref).astype(bf16)
    low_value = grad_value.astype(bf16)
    bias_ref[0:8, :] = jnp.broadcast_to(jnp.sum(grad.astype(f32), 0, keepdims=True), (8, LANES))
    bias_ref[8:16, :] = jnp.broadcast_to(
        jnp.sum(low_value.astype(f32), 0, keepdims=True), (8, LANES)
    )
    grads = (dq_ref[...], grad, low_value)
    weights = (flat(wq_ref[...]), flat(wk_ref[...]), flat(wv_ref[...]))
    accumulate(dh_ref, sum(dot_nt(g, w) for g, w in zip(grads, weights)))
    first = core_ref[0] == 0
    for index, value in enumerate(grads):
        pairs = dot_nn(ht_ref[...], value).reshape(-1, 2, send_ref.shape[2], LANES)
        keep_ref[:, index] = jnp.where(first, pairs[:, 0], pairs[:, 1])
        send_ref[:, index] = jnp.where(first, pairs[:, 1], pairs[:, 0])


def normal_cdf(value):
    bell = jnp.exp(-0.5 * value * value)
    near = jnp.abs(value) * (0.3275911 * math.sqrt(0.5)) + 1.0
    guess = pl.reciprocal(near, approx=True)
    t = guess * (2.0 - near * guess)
    poly = 0.5 * 1.061405429
    for factor in (-1.453152027, 1.421413741, -0.284496736, 0.254829592):
        poly = poly * t + 0.5 * factor
    tail = poly * t * bell
    return jnp.where(value >= 0.0, 1.0 - tail, tail), bell


def feed_kernel(
    h_ref, ht_ref, g_ref, we_ref, ws_ref, be_ref, core_ref, done_ref,
    out_ref, dh_ref, bias_ref, *grad_refs,
):
    step = pl.program_id(0)
    grad_out = g_ref[...]
    expand, shrink = flat(we_ref[...]), flat(ws_ref[...])
    width = expand.shape[1]
    pre = dot_nn(h_ref[...], expand) + be_ref[...]
    cdf, bell = normal_cdf(pre)
    active = (pre * cdf).astype(bf16)
    slope = cdf + pre * bell * (1.0 / math.sqrt(2.0 * math.pi))
    grad = (dot_nt(grad_out, shrink) * slope).astype(bf16)
    bias_ref[...] = jnp.broadcast_to(
        jnp.sum(grad.astype(f32), 0, keepdims=True), bias_ref.shape
    )
    _, blocks, rows, _ = grad_refs[0].shape
    where = lax.rem(step, D // width)
    block = step // (D // width)
    lanes = pl.ds(pl.multiple_of(where * width, width), width)
    wide = dot_nn(ht_ref[...], grad).astype(bf16)
    tall = dot_tn(active, grad_out).astype(bf16).reshape(2, blocks // 2, rows, D)
    if len(grad_refs) == 1:
        grad_refs[0][:, block, :, lanes] = wide.reshape(-1, rows, width)
        grad_refs[0][pl.ds(2 * step, 2), blocks // 2 :] = tall
    else:
        send_ref, keep_ref = grad_refs
        first = core_ref[0] == 0
        pairs = wide.reshape(-1, 2, rows, width)
        keep_ref[:, block, :, lanes] = jnp.where(first, pairs[:, 0], pairs[:, 1])
        send_ref[:, block, :, lanes] = jnp.where(first, pairs[:, 1], pairs[:, 0])
        keep_ref[step, blocks // 2 :] = jnp.where(first, tall[0], tall[1])
        send_ref[step, blocks // 2 :] = jnp.where(first, tall[1], tall[0])
    accumulate(out_ref, dot_nn(active, shrink))
    accumulate(dh_ref, dot_nt(grad, expand))


def lamb_step(master, first, second, grad, mean_ref, square_ref, update_ref, norms_ref):
    first, second, update = lamb_update(master, first, second, grad, DECAY)
    mean_ref[...], square_ref[...], update_ref[...] = first, second, update
    for index, value in enumerate((master, update)):
        squares = jnp.sum((value * value).reshape(-1, 8, value.shape[-1]), 0)
        accumulate(norms_ref.at[index], squares)


def lamb_feed_kernel(
    ep_ref, em_ref, es_ref, eg_ref, sp_ref, sm_ref, ss_ref, sg_ref, *refs
):
    enorm_ref, snorm_ref, *outs = refs[-8:]
    lamb_step(ep_ref[...], em_ref[...], es_ref[...], eg_ref[0].astype(f32), *outs[:3], enorm_ref)
    lamb_step(sp_ref[...], sm_ref[...], ss_ref[...], sg_ref[...].astype(f32), *outs[3:], snorm_ref)


def lamb_attend_kernel(
    ap_ref, am_ref, as_ref, mp_ref, mm_ref, ms_ref, grad_ref,
    anorm_ref, mnorm_ref, *outs,
):
    step = pl.program_id(0)
    grad = grad_ref[step].astype(f32)
    grad = grad + jnp.where(step < 2, grad_ref[jnp.minimum(4 + step, 5)].astype(f32), 0.0)
    lamb_step(ap_ref[...], am_ref[...], as_ref[...], grad, *outs[:3], anorm_ref)

    @pl.when(step == 0)
    def _():
        grad = grad_ref[3].astype(f32)
        lamb_step(mp_ref[...], mm_ref[...], ms_ref[...], grad, *outs[3:], mnorm_ref)


def renew_kernel(squares_ref, *refs):
    count = len(refs) // 3
    for index in range(count):
        master_ref, update_ref, fresh_ref = refs[2 * index], refs[2 * index + 1], refs[2 * count + index]
        lanes = (1, master_ref.shape[-1])
        weight = jnp.sqrt(jnp.full(lanes, squares_ref[2 * index], f32))
        change = jnp.sqrt(jnp.full(lanes, squares_ref[2 * index + 1], f32))
        ratio = RATE * (weight / (change + EPSILON))
        fresh_ref[...] = master_ref[...] - ratio * update_ref[...]


def whole(shape):
    return pl.BlockSpec(shape, lambda g: (0,) * len(shape), pipeline_mode=pl.Buffered(1))


def total_of(shape):
    return pl.BlockSpec(shape, lambda g: (0,) * len(shape))


def scalar():
    return pl.BlockSpec(memory_space=pltpu.SMEM)


def columns(rows, width=LANES, offset=0):
    return pl.BlockSpec((rows, width), lambda g: (0, g + offset))


def shaped(shape, dtype):
    return jax.ShapeDtypeStruct(shape, dtype)


def params():
    return pltpu.CompilerParams(vmem_limit_bytes=ROOM, dimension_semantics=("arbitrary",))


def layer_parts(inputs):
    center = inputs - jnp.mean(inputs, -1, keepdims=True)
    spread_of = jnp.mean(center * center, -1, keepdims=True)
    root = lax.rsqrt(spread_of + 1e-05)
    return center * root, root


def lamb_update(master, first, second, grad, decay):
    first = BETA_ONE * first + (1.0 - BETA_ONE) * grad
    second = BETA_TWO * second + (1.0 - BETA_TWO) * grad * grad
    update = (
        first / (1.0 - BETA_ONE**STEP) / (jnp.sqrt(second / (1.0 - BETA_TWO**STEP)) + EPSILON)
        + decay * master
    )
    return (first, second, update)


def per_device(
    tokens,
    cotangent,
    lengths,
    attend_weight,
    merge_weight,
    expand_weight,
    shrink_weight,
    gains_biases,
    attend_first,
    attend_second,
    merge_first,
    merge_second,
    expand_first,
    expand_second,
    shrink_first,
    shrink_second,
    vector_first,
    vector_second,
):
    rows = tokens.shape[1]
    count = rows // CHUNK
    n = lax.axis_size("seq")
    device = lax.axis_index("seq")
    grad_out = cotangent[0]
    own = D // n
    parts = 2 if FF // n >= 256 else 1
    sub = FF // n // parts
    tall = FF // D // parts
    core = lax.rem(device, 2)
    core_ref = core[None].astype(jnp.int32)

    def gather(blocks):
        shard = jnp.concatenate([block.astype(bf16) for block in blocks], 0)
        full = lax.all_gather(shard, "seq", axis=0, tiled=False)
        return full.reshape(n, shard.shape[0] // own, own, D)

    def of_part(array, index):
        return jnp.concatenate(
            [array[:, (j * parts + index) * sub : (j * parts + index + 1) * sub] for j in range(n)], 1
        )

    attend = gather(
        [attend_weight[:, :D], attend_weight[:, D : 2 * D], attend_weight[:, 2 * D :], merge_weight]
    )
    feeds = []
    for index in range(parts):
        wide = of_part(expand_weight, index)
        feeds.append(
            gather(
                [wide[:, c * D : (c + 1) * D] for c in range(tall)]
                + [shrink_weight[index * sub : (index + 1) * sub]]
            )
        )
    packed = lax.all_gather(gains_biases.astype(bf16), "seq", axis=0, tiled=True)
    vector = packed.astype(f32)
    gain_one = vector[0:D]
    shift_one = vector[D : 2 * D]
    gain_two = vector[2 * D : 3 * D]
    shift_two = vector[3 * D : 4 * D]
    bias_attend = vector[4 * D : 7 * D]
    bias_merge = vector[7 * D : 8 * D]
    bias_expand = vector[8 * D : 8 * D + FF]
    bias_shrink = vector[8 * D + FF :]

    bounds = jnp.cumsum(lengths[0])

    def label(place):
        return jnp.sum((bounds <= place[..., None]).astype(jnp.int32), -1)

    positions = device * rows + jnp.arange(rows, dtype=jnp.int32)
    segment = label(positions)
    starts = jnp.sum(jnp.where(bounds[None, :] <= positions[:, None], lengths[0][None, :], 0), -1)
    offset = positions - starts
    edges = device * rows + jnp.arange(count, dtype=jnp.int32) * CHUNK
    before = jnp.zeros((8,), jnp.int32).at[:count].set(label(edges - 1))
    final = jnp.zeros((8,), jnp.int32).at[:count].set(label(edges + CHUNK - 1))
    final = final.at[7].set(segment[-1])
    marks = jnp.broadcast_to(jnp.concatenate([before, final])[:, None], (16, LANES)).astype(f32)
    halfway = ROT // 2
    inverse = jnp.exp(jnp.arange(halfway, dtype=f32) * (-2.0 * math.log(BASE) / ROT))
    angles = offset.astype(f32)[:, None] * inverse
    cosine, sines = jnp.cos(angles), jnp.sin(angles)
    rest = jnp.ones((rows, HEAD - ROT), f32)
    none = jnp.zeros((rows, HEAD - ROT), f32)
    part = jnp.zeros((rows, halfway), f32)
    table = jnp.stack(
        [
            jnp.tile(jnp.concatenate([cosine, cosine, rest], 1), (1, 2)),
            jnp.tile(jnp.concatenate([-sines, part, none], 1), (1, 2)),
            jnp.tile(jnp.concatenate([part, sines, none], 1), (1, 2)),
            jnp.broadcast_to(segment.astype(f32)[:, None], (rows, 2 * HEAD)),
        ]
    )
    row_table = jnp.broadcast_to(segment.astype(f32)[None, :], (8, rows))
    const_np, weight_np = group_tables()
    const, weighting = jnp.asarray(const_np), jnp.asarray(weight_np)

    inputs = tokens[0].astype(f32)
    normed, root = layer_parts(inputs)
    low_one = (normed * gain_one + shift_one).astype(bf16)
    low_two = (normed * gain_two + shift_two).astype(bf16)

    flipped_one = lax.optimization_barrier(low_one.T)
    flipped_two = lax.optimization_barrier(low_two.T)

    def feed(index, done, parted):
        width = 2 * sub
        per = D // width
        held = (n // 2 if parted else n, 2 * tall, own, D)
        many = 2 if parted else 1
        return pl.pallas_call(
            feed_kernel,
            grid=(n // 2,),
            in_specs=[
                whole((rows, D)),
                whole((D, rows)),
                whole((rows, D)),
                pl.BlockSpec((n, 1, own, width), lambda g: (0, g // per, 0, g % per)),
                pl.BlockSpec((2, tall, own, D), lambda g: (g, 1, 0, 0)),
                pl.BlockSpec((1, width), lambda g: (0, g)),
                scalar(),
                pl.BlockSpec(memory_space=pl.ANY),
            ],
            out_specs=[
                total_of((rows, D)),
                total_of((rows, D)),
                pl.BlockSpec((8, width), lambda g: (0, g)),
                *[total_of(held)] * many,
            ],
            out_shape=[
                shaped((rows, D), f32),
                shaped((rows, D), f32),
                shaped((8, FF // parts), f32),
                *[shaped(held, bf16)] * many,
            ],
            compiler_params=params(),
            cost_estimate=pl.CostEstimate(
                flops=24 * rows * D * FF // parts,
                bytes_accessed=10 * D * FF // parts,
                transcendentals=rows * FF // parts,
            ),
            name="feed",
        )(
            low_two, flipped_two, grad_out, feeds[index], feeds[index],
            of_part(bias_expand[None, :], index), core_ref, done,
        )

    def projection(index):
        return pl.BlockSpec((n, 1, own, LANES), lambda g: (0, index, 0, g))

    constants = [whole((3, LANES, LANES)), whole((1, LANES))]
    tables = [whole((4, rows, 2 * HEAD)), whole((16, LANES))]
    query, key, value, value_low, turned_query, turned_key, summary = pl.pallas_call(
        qkv_kernel,
        grid=(NGROUP,),
        in_specs=[
            whole((rows, D)),
            *[projection(index) for index in range(3)],
            columns(3),
            *tables,
            *constants,
        ],
        out_specs=[columns(rows)] * 6 + [columns(STATE)],
        out_shape=[shaped((rows, D), bf16)] * 6 + [shaped((STATE, D), f32)],
        compiler_params=params(),
        cost_estimate=pl.CostEstimate(
            flops=6 * rows * D * D + 22 * rows * D * LANES,
            bytes_accessed=20 * rows * D,
            transcendentals=2 * rows * D,
        ),
        name="qkv",
    )(low_one, attend, attend, attend, bias_attend.reshape(3, D), table, marks, const, weighting)

    reaches = range(1, n // 2 + 1)
    own_before, own_final = label(device * rows - 1), segment[-1]
    carried = jnp.zeros_like(summary)
    for far in reaches:
        came = lax.ppermute(summary, "seq", [(e, e + far) for e in range(n - far)])
        same = (device >= far) & (label((device - far + 1) * rows - 1) == own_before)
        carried = carried + jnp.where(same, came, 0.0)

    _, grad_query, part_key, part_value, grad_carried, query_bias, attend_out, send, keep = pl.pallas_call(
        attend_kernel,
        grid=(NGROUP,),
        in_specs=[
            *[columns(rows)] * 5,
            columns(STATE),
            whole((rows, D)),
            pl.BlockSpec((LANES // own, 1, own, D), lambda g: (g, 3, 0, 0)),
            whole((4, rows, 2 * HEAD)),
            whole((8, rows)),
            whole((16, LANES)),
            whole((3, LANES, LANES)),
            scalar(),
        ],
        out_specs=[columns(rows)] * 4
        + [columns(STATE), columns(8), total_of((rows, D))]
        + [pl.BlockSpec((LANES // own // 2, 1, own, D), lambda g: (g, 3, 0, 0))] * 2,
        out_shape=[
            shaped((rows, D), bf16),
            shaped((rows, D), bf16),
            shaped((rows, D), f32),
            shaped((rows, D), f32),
            shaped((STATE, D), f32),
            shaped((8, D), f32),
            shaped((rows, D), f32),
            shaped((n // 2, 4, own, D), f32),
            shaped((n // 2, 4, own, D), f32),
        ],
        scratch_shapes=[pltpu.VMEM((rows, LANES), kind) for kind in (bf16, bf16, f32)],
        compiler_params=params(),
        cost_estimate=pl.CostEstimate(
            flops=2 * rows * D * D + 150 * rows * D * LANES,
            bytes_accessed=24 * rows * D,
            transcendentals=0,
        ),
        name="attend",
    )(
        query, key, value, value_low, turned_query, carried,
        grad_out, attend, table, row_table, marks, const, core_ref,
    )

    fed = [feed(0, grad_carried, False)]

    returned = jnp.zeros_like(summary)
    for far in reaches:
        came = lax.ppermute(grad_carried, "seq", [(e + far, e) for e in range(n - far)])
        same = (device + far < n) & (label((device + far) * rows - 1) == own_final)
        returned = returned + jnp.where(same, came, 0.0)

    sides = pl.BlockSpec((n // 2, 3, own, LANES), lambda g: (0, 0, 0, g))
    rest_bias, grad_one, send, keep = pl.pallas_call(
        finish_kernel,
        grid=(NGROUP,),
        in_specs=[columns(rows)] * 7
        + [columns(STATE), *tables, whole((3, LANES, LANES))]
        + [projection(index) for index in range(3)]
        + [whole((D, rows)), scalar()]
        + [pl.BlockSpec(memory_space=pl.ANY)] * 3,
        out_specs=[columns(16), total_of((rows, D)), sides, sides],
        out_shape=[
            shaped((16, D), f32),
            shaped((rows, D), f32),
            shaped((n // 2, 4, own, D), f32),
            shaped((n // 2, 4, own, D), f32),
        ],
        input_output_aliases={16: 2, 17: 3},
        compiler_params=params(),
        cost_estimate=pl.CostEstimate(
            flops=12 * rows * D * D + 24 * rows * D * LANES,
            bytes_accessed=18 * rows * D,
            transcendentals=0,
        ),
        name="finish",
    )(
        key, value, value_low, turned_key, grad_query, part_key, part_value, returned,
        table, marks, const, attend, attend, attend, flipped_one, core_ref, send, keep, fed[0][2],
    )

    for index in range(1, parts):
        fed.append(feed(index, rest_bias, True))

    bits = n.bit_length() - 1

    def exchange(array, bit):
        return lax.ppermute(array, "seq", [(i, i ^ (1 << bit)) for i in range(n)])

    def scatter(send, keep):
        came = exchange(send, 0)
        middle = keep.shape[1] // 2
        order = list(range(1, bits))
        turned = (bits - 1) // 2
        orders = order, order[turned:] + order[:turned]
        places = order[::-1]
        deep = keep.reshape((2,) * (bits - 1) + keep.shape[1:])
        came = came.reshape(deep.shape)
        sides = [[(deep, places, side * middle), (came, places, side * middle)] for side in range(2)]

        def pick(terms, fixed):
            total = 0.0
            for array, axes, start in terms:
                starts = [fixed.get(bit, 0) for bit in axes] + [start, 0, 0]
                sizes = [1 if bit in fixed else 2 for bit in axes] + [middle, own, D]
                value = lax.dynamic_slice(array, starts, sizes).astype(f32)
                kept = [2 for bit in places if bit not in fixed]
                total = total + value.reshape(kept + [middle, own, D])
            return total

        for place in range(bits - 1):
            for side in range(2):
                bit, earlier = orders[side][place], orders[side][:place]
                fixed = {b: (device >> b) & 1 for b in earlier}
                fixed[bit] = 1 - ((device >> bit) & 1)
                other = pick(sides[side], fixed).astype(bf16)
                left = [b for b in places if b not in fixed]
                sides[side].append((exchange(other, bit), left, 0))
        fixed = {b: (device >> b) & 1 for b in order}
        return [pick(terms, fixed) for terms in sides]

    groups = lax.axis_size("dp")
    group = lax.axis_index("dp")

    def sum_groups(value, fine):
        blocks = value.shape[0]
        shares = value.reshape(blocks, groups, own // groups, D)
        rolls = {far: [(i, (i + far) % groups) for i in range(groups)] for far in range(1, groups)}

        def share(which):
            return lax.dynamic_index_in_dim(shares, which % groups, 1, False)

        total = share(group)
        for far, pairs in rolls.items():
            total = total + lax.ppermute(share(group + far).astype(bf16), "dp", pairs).astype(f32)
        high = lax.reduce_precision(total, 8, 7)
        total = jnp.concatenate([high, (total - high)[:fine]], 0).astype(bf16)
        result = jnp.zeros((blocks + fine,) + shares.shape[1:], bf16)
        result = lax.dynamic_update_index_in_dim(result, total, group, 1)
        for far, pairs in rolls.items():
            came = lax.ppermute(total, "dp", pairs)
            result = lax.dynamic_update_index_in_dim(result, came, (group - far) % groups, 1)
        return result.reshape(blocks + fine, own, D)

    def sum_all(value):
        for bit in range(bits):
            value = value + exchange(value, bit)
        for bit in range(groups.bit_length() - 1):
            pairs = [(i, i ^ (1 << bit)) for i in range(groups)]
            value = value + lax.ppermute(value, "dp", pairs)
        return value

    first_part = lax.psum_scatter(fed[0][3], "seq", scatter_dimension=0, tiled=False)
    feed_sums = [lax.psum([first_part[:tall], first_part[tall:]], "dp")]
    attend_sum = sum_groups(jnp.concatenate(scatter(send, keep), 0), 2)
    for index in range(1, parts):
        pieces = [piece.astype(bf16) for piece in scatter(*fed[index][3:])]
        feed_sums.append(lax.psum(pieces, "dp"))

    grad_float = grad_out.astype(f32)
    result = inputs + attend_out + bias_merge + bias_shrink + sum(f[0] for f in fed)
    block_output = result.astype(bf16)[None]
    grad_two = sum(f[1] for f in fed)
    grad_bias_out = jnp.sum(grad_float, 0)
    pulled = grad_one * gain_one + grad_two * gain_two
    drop = jnp.mean(pulled, -1, keepdims=True)
    lean = jnp.mean(pulled * normed, -1, keepdims=True)
    input_grad = (grad_float + root * (pulled - drop - normed * lean)).astype(bf16)[None]
    feed_bias = jnp.concatenate(
        [fed[p][2][0, j * sub : (j + 1) * sub] for j in range(n) for p in range(parts)]
    )
    grad_vector = jnp.concatenate(
        [
            jnp.sum(grad_one * normed, 0),
            jnp.sum(grad_one, 0),
            jnp.sum(grad_two * normed, 0),
            jnp.sum(grad_two, 0),
            query_bias[0],
            rest_bias[0],
            rest_bias[8],
            grad_bias_out,
            feed_bias,
            grad_bias_out,
        ]
    )
    vector_sum = sum_all(grad_vector.reshape(-1, 128)).reshape(-1)
    share = gains_biases.shape[0]
    own_vector = lax.dynamic_slice(vector_sum, (device * share,), (share,))

    strips = 8

    wide_cols = FF // parts // strips
    per = D // wide_cols
    held = None
    expand_sums, shrink_sums = [], []
    for index in range(parts):
        of_expand = pl.BlockSpec((own, wide_cols), lambda g: (0, g * parts + index))
        of_shrink = pl.BlockSpec((sub // strips, D), lambda g: (index * strips + g, 0))
        before_specs = [] if held is None else [pl.BlockSpec(memory_space=pl.ANY)] * 6
        expand_norm, shrink_norm, *held = pl.pallas_call(
            lamb_feed_kernel,
            grid=(strips,),
            in_specs=[of_expand] * 3
            + [pl.BlockSpec((1, own, wide_cols), lambda g: (g // per, 0, g % per))]
            + [of_shrink] * 3
            + [pl.BlockSpec((sub // strips, D), lambda g: (g, 0))]
            + before_specs,
            out_specs=[total_of((2, 8, wide_cols)), total_of((2, 8, D))]
            + [of_expand] * 3
            + [of_shrink] * 3,
            out_shape=[shaped((2, 8, wide_cols), f32), shaped((2, 8, D), f32)]
            + [shaped((own, FF), f32)] * 3
            + [shaped((FF // n, D), f32)] * 3,
            input_output_aliases={} if held is None else {8 + i: 2 + i for i in range(6)},
            compiler_params=params(),
            name="lamb_feed",
        )(
            expand_weight, expand_first, expand_second, feed_sums[index][0],
            shrink_weight, shrink_first, shrink_second, flat(feed_sums[index][1]),
            *([] if held is None else held),
        )
        expand_sums.append(jnp.sum(expand_norm, (1, 2)))
        shrink_sums.append(jnp.sum(shrink_norm, (1, 2)))
    expand_mean, expand_square, expand_update, shrink_mean, shrink_square, shrink_update = held
    block_of = pl.BlockSpec((own, D), lambda g: (0, g))
    attend_norm, merge_norm, *held = pl.pallas_call(
        lamb_attend_kernel,
        grid=(3,),
        in_specs=[block_of] * 3 + [whole((own, D))] * 3 + [whole((6, own, D))],
        out_specs=[total_of((2, 8, D))] * 2 + [block_of] * 3 + [total_of((own, D))] * 3,
        out_shape=[shaped((2, 8, D), f32)] * 2
        + [shaped((own, 3 * D), f32)] * 3
        + [shaped((own, D), f32)] * 3,
        compiler_params=params(),
        name="lamb_attend",
    )(
        attend_weight, attend_first, attend_second, merge_weight, merge_first, merge_second,
        attend_sum,
    )
    attend_mean, attend_square, attend_update, merge_mean, merge_square, merge_update = held
    vector_mean, vector_square, vector_update = lamb_update(
        gains_biases, vector_first, vector_second, own_vector, 0.0
    )
    local = jnp.concatenate(
        [
            jnp.sum(attend_norm, (1, 2)),
            jnp.sum(merge_norm, (1, 2)),
            sum(expand_sums),
            sum(shrink_sums),
            jnp.stack([jnp.sum(gains_biases * gains_biases), jnp.sum(vector_update * vector_update)]),
        ]
    )
    squares = lax.psum(local, "seq")
    fresh = pl.pallas_call(
        renew_kernel,
        grid=(strips,),
        in_specs=[scalar()]
        + [pl.BlockSpec((own, 3 * D // strips), lambda g: (0, g))] * 2
        + [pl.BlockSpec((own, D // strips), lambda g: (0, g))] * 2
        + [pl.BlockSpec((own, FF // strips), lambda g: (0, g))] * 2
        + [pl.BlockSpec((FF // n // strips, D), lambda g: (g, 0))] * 2,
        out_specs=[
            pl.BlockSpec((own, 3 * D // strips), lambda g: (0, g)),
            pl.BlockSpec((own, D // strips), lambda g: (0, g)),
            pl.BlockSpec((own, FF // strips), lambda g: (0, g)),
            pl.BlockSpec((FF // n // strips, D), lambda g: (g, 0)),
        ],
        out_shape=[
            shaped((own, 3 * D), f32),
            shaped((own, D), f32),
            shaped((own, FF), f32),
            shaped((FF // n, D), f32),
        ],
        compiler_params=params(),
        name="renew",
    )(
        squares, attend_weight, attend_update, merge_weight, merge_update,
        expand_weight, expand_update, shrink_weight, shrink_update,
    )
    roots = jnp.sqrt(squares.reshape(5, 2).T.reshape(10))
    vector_fresh = gains_biases - RATE * (roots[4] / (roots[9] + EPSILON)) * vector_update
    return (
        block_output, input_grad,
        fresh[0], attend_mean, attend_square,
        fresh[1], merge_mean, merge_square,
        fresh[2], expand_mean, expand_square,
        fresh[3], shrink_mean, shrink_square,
        vector_fresh, vector_mean, vector_square,
        roots,
    )


def solution(mesh):
    matrix, line = P("seq", None), P("seq")
    stream = P("dp", "seq", None)
    return jax.shard_map(
        per_device,
        mesh=mesh,
        in_specs=(stream, stream, P("dp", None))
        + (matrix,) * 4
        + (line,)
        + (matrix,) * 8
        + (line,) * 2,
        out_specs=(stream, stream) + (matrix,) * 12 + (line,) * 3 + (P(),),
        check_vma=False,
    )
```

time: 1890 us -> 606 us (0.32)
  matrix products: 580 us -> 0 us
  local copies, waits for them, and re-layouts: 465 us -> 20.1 us
  Pallas kernels: 0 us -> 232 us
  waiting for transfers between devices: 389 us -> 162 us
  other arithmetic: 262 us -> 51.2 us
  blocking collectives: 110 us -> 24.2 us
  starting transfers between devices: 0.46 us -> 83.2 us
  loops' own time: 38.5 us -> 0 us
    dot_general x237 -> x0, matrix products: 580 us -> none  [the longest x48 92.3 us: advance(): jnp.einsum('thf,hfe->the', query_part, state, precision=precise)]
    reduce_scatter x4 -> x1, waiting for transfers between devices: 242 us -> 0.01 us  [per_device(): lax.psum_scatter(fed[0][3], 'seq', scatter_dimension=0, tiled=False)]
    pallas_call x0 -> x9, Pallas kernels: none -> 232 us  [the longest x1 76.3 us: per_device(): pl.pallas_call(attend_kernel, grid=(NGROUP,), in_specs=[*[columns(rows)]...]
    squeeze x74 -> x0, local copies, waits for them, and re-layouts: 99 us -> none  [the longest x72 86.7 us: attend_local(): lax.scan(jax.checkpoint(advance), start, (query_feat, key_feat, value_row...]
    ppermute x0 -> x29, waiting for transfers between devices: none -> 96.3 us  [the longest x13 45.3 us: exchange(): return lax.ppermute(array, 'seq', [(i, i ^ 1 << bit) for i in range(n)])]
    ppermute x0 -> x29, starting transfers between devices: none -> 83 us  [the longest x3 30.9 us: sum_groups(): came = lax.ppermute(total, 'dp', pairs)]
    psum x1, waiting for transfers between devices: 113 us -> 30.4 us  [per_device(): feed_sums = [lax.psum([first_part[:tall], first_part[tall:]], 'dp')]]
    reshape x6 -> x0, local copies, waits for them, and re-layouts: 81.6 us -> none  [the longest x3 51.1 us: summary_state(): pieces = qkv.reshape(count, 3, H, HEAD)]
  transfers between devices with their start and end apart: 11 -> 34, of which waited for: 5 -> 15; matrix products, arithmetic and copies ran while one was open for 28% -> 10% of each run, Pallas kernels for 0% -> 34%
where the time goes in v1:
time: 606 us; the launch traced here: 598 us
  Pallas kernels  232 us (38%)
  waiting for transfers between devices  162 us (27%)
  starting transfers between devices  83.2 us (14%)
  other arithmetic  51.2 us (8%)
  between operations  25.7 us (4%)
  blocking collectives  24.2 us (4%)
  local copies, waits for them, and re-layouts  20.1 us (3%)
    pallas_call x1, Pallas kernels, per_device(): pl.pallas_call(attend_kernel, grid=(NGROUP,), in_specs=[*[columns(rows)]...  76.3 us
    pallas_call x2, Pallas kernels, feed(): pl.pallas_call(feed_kernel, grid=(n // 2,), in_specs=[whole((rows, D)), w...  74.6 us
    ppermute x13, waiting for transfers between devices, exchange(): return lax.ppermute(array, 'seq', [(i, i ^ 1 << bit) for i in range(n)])  45.3 us
    ppermute x3, waiting for transfers between devices, sum_groups(): came = lax.ppermute(total, 'dp', pairs)  35.5 us
    all_gather x3, waiting for transfers between devices, gather(): full = lax.all_gather(shard, 'seq', axis=0, tiled=False)  34.8 us
    ppermute x3, starting transfers between devices, sum_groups(): came = lax.ppermute(total, 'dp', pairs)  30.9 us
    psum x1, waiting for transfers between devices, per_device(): feed_sums = [lax.psum([first_part[:tall], first_part[tall:]], 'dp')]  30.4 us
    ppermute x13, starting transfers between devices, exchange(): return lax.ppermute(array, 'seq', [(i, i ^ 1 << bit) for i in range(n)])  27.7 us
  transfers between devices with their start and end apart: 34, of which 15 were waited for; matrix products, arithmetic and copies ran while one was open for 10% of the time, Pallas kernels for 34%

profile of v1, /device:TPU:0, one launch (start us, length us, event | category | flops | bytes accessed | tf_op | source)
XLA Modules:
  0.0 597.5 jit_solution(11623206395150279802)
XLA Ops:
  14.9 10.6 %all-gather.3 = bf16[8,1,1664]{2,1,0:T(2,128)(2,1)S(1)} all-gather(bf16[1,1,1664]{2,1,0:T(2,128)(2,1)S(1)} %reshape.438), channel_id=1, replica_groups=mesh['seq'=8,'dp'=4] {'seq'}, dimensions={0}, use_global_device_ids=true | all-gather | bytes 29952 | tf_op jit(solution)/shard_map/all_gather | solution.py:513
  32.9 34.7 %all-gather.8.cloned.1.call-done = bf16[4096,1024]{1,0:T(8,128)(2,1)} async-done(((bf16[512,1024]{1,0:T(8,128)(2,1)}), bf16[4096,1024]{1,0:T(8,128)(2,1)}) %all-gather.8.cloned.1.call-update) | async-done | bytes 8388624 | tf_op jit(solution)/shard_map/all_gather | solution.py:493
  68.3 20.1 %qkv.1 = (bf16[768,1024]{1,0:T(8,128)(2,1)}, bf16[768,1024]{1,0:T(8,128)(2,1)}, bf16[768,1024]{1,0:T(8,128)(2,1)}, bf16[768,1024]{1,0:T(8,128)(2,1)}, bf16[768,1...) custom-call(bf16[768,1024]{1,0:T(8,128)(2,1)} %get-tuple-element.207.h_ref, ...), custom_call_target="tpu_custom_call" | custom-call | flops 9261023232 | bytes 15728640 | tf_op jit(solution)/shard_map/qkv/pallas_call | solution.py:612
  90.6 4.1 collective-permute-start.1
  120.7 76.3 %attend.1 = (bf16[768,1024]{1,0:T(8,128)(2,1)}, bf16[768,1024]{1,0:T(8,128)(2,1)}, f32[768,1024]{1,0:T(8,128)}, f32[768,1024]{1,0:T(8,128)}, f32[72,1024]{1,0:T(...) custom-call(bf16[768,1024]{1,0:T(8,128)(2,1)} %get-tuple-element.110, ...), custom_call_target="tpu_custom_call" | custom-call | flops 31809601536 | bytes 18874368 | tf_op jit(solution)/shard_map/attend/pallas_call | solution.py:641
  202.3 36.9 %feed.2 = (f32[768,1024]{1,0:T(8,128)}, f32[768,1024]{1,0:T(8,128)}, f32[8,2048]{1,0:T(8,128)}, bf16[8,4,128,1024]{3,2,1,0:T(8,128)(2,1)}) custom-call(bf16[768,1024]{1,0:T(8,128)(2,1)} %copy-done.2, bf16[1024,768]{1,0:T(8,128)(2,1)} %copy.86.ht_ref, bf16[768,1024]{1,0:T(8,128)(2,1)} %bitcast.260, bf16[8,4,128,1024]{3,2,1,0:T(8,128)(2,1)} %bitcast.301, ...), custom_call_target="tpu_custom_call" | custom-call | flops 38654705664 | bytes 20971520 | tf_op jit(solution)/shard_map/feed/pallas_call | solution.py:570
  240.1 24.2 %finish.1 = (f32[16,1024]{1,0:T(8,128)}, f32[768,1024]{1,0:T(8,128)}, f32[4,4,128,1024]{3,2,1,0:T(8,128)}, f32[4,4,128,1024]{3,2,1,0:T(8,128)}) custom-call(bf16[768,1024]{1,0:T(8,128)(2,1)} %get-tuple-element.111.k_ref, bf16[768,1024]{1,0:T(8,128)(2,1)} %get-tuple-element.112.v_ref, ...), custom_call_target="tpu_custom_call", output_to_operand_aliasing={{2}: (16, {}), {3}: (17, {})} | custom-call | flops 14495514624 | bytes 14155776 | tf_op jit(solution)/shard_map/finish/pallas_call | solution.py:691
  264.3 9.3 %collective-permute-start.8 = (f32[4,4,128,1024]{3,2,1,0:T(8,128)}, f32[4,4,128,1024]{3,2,1,0:T(8,128)}, u32[]{:S(2)}, u32[]{:S(2)}) collective-permute-start(f32[4,4,128,1024]{3,2,1,0:T(8,128)} %get-tuple-element.132), channel_id=1, source_target_pairs={{0,4},{4,0},{8,12},{12,8},{16,20},{20,16},{24,28},{28,24},{1,5},{5... | collective-permute-start | bytes 25165832 | tf_op jit(solution)/shard_map/ppermute | solution.py:725
  275.2 37.7 %feed.3 = (f32[768,1024]{1,0:T(8,128)}, f32[768,1024]{1,0:T(8,128)}, f32[8,2048]{1,0:T(8,128)}, bf16[4,4,128,1024]{3,2,1,0:T(8,128)(2,1)}, bf16[4,4,128,1024]{3,2,1,0:T(8,128)(2,1)}) custom-call(bf16[768,1024]{1,0:T(8,128)(2,1)} %copy-done.2, bf16[1024,768]{1,0:T(8,128)(2,1)} %copy.86.ht_ref, bf16[768,1024]{1,0:T(8,128)(2,1)} %bitcast.261, ...), custom_call_target="tpu_custom_call" | custom-call | flops 38654705664 | bytes 20971520 | tf_op jit(solution)/shard_map/feed/pallas_call | solution.py:570
  312.9 5.1 add_reduce_fusion
  336.6 16.4 %collective-permute-done.9 = bf16[2,2,128,1024]{3,2,1,0:T(8,128)(2,1)S(1)} collective-permute-done((bf16[2,2,128,1024]{3,2,1,0:T(8,128)(2,1)S(1)}, bf16[2,2,128,1024]{3,2,1,0:T(8,128)(2,1)S(1)}, u32[]{:S(2)}, u32[]{:S(2)}) %collective-permute-start.9) | collective-permute-done | bytes 1048608 | tf_op jit(solution)/shard_map/ppermute | solution.py:725
  366.6 12.4 %collective-permute-done.11 = bf16[2,2,128,1024]{3,2,1,0:T(8,128)(2,1)S(1)} collective-permute-done((bf16[2,2,128,1024]{3,2,1,0:T(8,128)(2,1)}, bf16[2,2,128,1024]{3,2,1,0:T(8,128)(2,1)S(1)}, u32[]{:S(2)}, u32[]{:S(2)}) %collective-permute-start.11) | collective-permute-done | bytes 1048608 | tf_op jit(solution)/shard_map/ppermute | solution.py:725
  380.0 10.0 %collective-permute-done.10 = bf16[2,128,1024]{2,1,0:T(8,128)(2,1)} collective-permute-done((bf16[2,128,1024]{2,1,0:T(8,128)(2,1)}, bf16[2,128,1024]{2,1,0:T(8,128)(2,1)}, u32[]{:S(2)}, u32[]{:S(2)}) %collective-permute-start.10) | collective-permute-done | bytes 524320 | tf_op jit(solution)/shard_map/ppermute | solution.py:725
  425.4 7.5 %collective-permute-done.14 = bf16[4,32,1024]{2,1,0:T(8,128)(2,1)S(1)} collective-permute-done((bf16[4,32,1024]{2,1,0:T(8,128)(2,1)S(1)}, bf16[4,32,1024]{2,1,0:T(8,128)(2,1)S(1)}, u32[]{:S(2)}, u32[]{:S(2)}) %collective-permute-start.14) | collective-permute-done | bytes 262176 | tf_op jit(solution)/shard_map/ppermute | solution.py:772
  433.2 28.5 %collective-permute-start.16 = (bf16[6,32,1024]{2,1,0:T(8,128)(2,1)S(1)}, bf16[6,32,1024]{2,1,0:T(8,128)(2,1)S(1)}, u32[]{:S(2)}, u32[]{:S(2)}) collective-permute-start(bf16[6,32,1024]{2,1,0:T(8,128)(2,1)S(1)} %pad_maximum_fusion.5), channel_id=1, source_target_pairs={{0,1},{1,2},{2,3},{3,0},{4,5},{5,6},{6,7},{7,4},{8,9},{9,10},{10,1... | collective-permute-start | bytes 1179656 | tf_op jit(solution)/shard_map/ppermute | solution.py:778
  465.2 10.8 %collective-permute-done.16 = bf16[6,32,1024]{2,1,0:T(8,128)(2,1)S(1)} collective-permute-done((bf16[6,32,1024]{2,1,0:T(8,128)(2,1)S(1)}, bf16[6,32,1024]{2,1,0:T(8,128)(2,1)S(1)}, u32[]{:S(2)}, u32[]{:S(2)}) %collective-permute-start.16) | collective-permute-done | bytes 393248 | tf_op jit(solution)/shard_map/ppermute | solution.py:778
  476.0 20.7 %collective-permute-done.17 = bf16[6,32,1024]{2,1,0:T(8,128)(2,1)S(1)} collective-permute-done((bf16[6,32,1024]{2,1,0:T(8,128)(2,1)S(1)}, bf16[6,32,1024]{2,1,0:T(8,128)(2,1)S(1)}, u32[]{:S(2)}, u32[]{:S(2)}) %collective-permute-start.17) | collective-permute-done | bytes 393248 | tf_op jit(solution)/shard_map/ppermute | solution.py:778
  496.7 4.0 collective-permute-done.18
  501.9 8.8 %lamb_attend.1 = (f32[2,8,1024]{2,1,0:T(8,128)}, f32[2,8,1024]{2,1,0:T(8,128)}, f32[128,3072]{1,0:T(8,128)}, f32[128,3072]{1,0:T(8,128)}, f32[128,3072]{1,0:T(8,...) custom-call(f32[128,3072]{1,0:T(8,128)} %refs_0_.1, f32[128,3072]{1,0:T(8,128)} %am_ref.1, ...), custom_call_target="tpu_custom_call" | custom-call | tf_op jit(solution)/shard_map/lamb_attend/pallas_call | solution.py:863
  512.6 30.4 %all-reduce.5.cloned.1.call-done = (bf16[2,128,1024]{2,1,0:T(8,128)(2,1)}, bf16[256,1024]{1,0:T(8,128)(2,1)}, bf16[2,128,1024]{2,1,0:T(8,128)(2,1)}, bf16[256,1024]{1,0:T(8,128)(2,1)}) async-done(((bf16[2,128,1024]{2,1,0:T(8,128)(2,1)}, bf16[256,1024]{1,0:T(8,128)(2,1)}, bf16[2,128,1024]{2,1,0:T(8,128)(2,1)}, bf16[256,1024]{1,0:T(8,128)(2,1)}), (bf16[2,128,1024]{2,1,0:T(8,128)(2,1)}, ...) | async-done | bytes 2097168 | tf_op jit(solution)/shard_map/psum | solution.py:791
  543.0 9.3 %lamb_feed.2 = (f32[2,8,256]{2,1,0:T(8,128)}, f32[2,8,1024]{2,1,0:T(8,128)}, f32[128,4096]{1,0:T(8,128)}, f32[128,4096]{1,0:T(8,128)}, f32[128,4096]{1,0:T(8,128...) custom-call(f32[128,4096]{1,0:T(8,128)} %refs_4_.1, f32[128,4096]{1,0:T(8,128)} %em_ref.3, ...), custom_call_target="tpu_custom_call" | custom-call | tf_op jit(solution)/shard_map/lamb_feed/pallas_call | solution.py:837
  552.3 9.3 %lamb_feed.3 = (f32[2,8,256]{2,1,0:T(8,128)}, f32[2,8,1024]{2,1,0:T(8,128)}, f32[128,4096]{1,0:T(8,128)}, f32[128,4096]{1,0:T(8,128)}, f32[128,4096]{1,0:T(8,128...) custom-call(f32[128,4096]{1,0:T(8,128)} %refs_4_.1, ...), custom_call_target="tpu_custom_call", output_to_operand_aliasing={{2}: (8, {}), {3}: (9, {}), {4}: (10, {}), {5}: (11, {}), {... | custom-call | tf_op jit(solution)/shard_map/lamb_feed/pallas_call | solution.py:837
  565.0 13.6 %psum.39.squares_ref = f32[10]{0:T(128)S(1)} all-reduce(f32[10]{0:T(128)S(1)} %concatenate.97), channel_id=1, replica_groups=mesh['seq'=8,'dp'=4] {'seq'}, use_global_device_ids=true, to_apply=%region_35.36 | all-reduce | flops 10 | bytes 80 | tf_op jit(solution)/shard_map/psum | solution.py:890
  581.4 9.2 %renew.1 = (f32[128,3072]{1,0:T(8,128)}, f32[128,1024]{1,0:T(8,128)}, f32[128,4096]{1,0:T(8,128)}, f32[512,1024]{1,0:T(8,128)}) custom-call(f32[10]{0:T(128)} %copy-done.25, f32[128,3072]{1,0:T(8,128)} %refs_0_.1, f32[128,3072]{1,0:T(8,128)} %get-tuple-element.150.refs_1_, f32[128,1024]{1,0:T(8,128)} %refs_2_.1, f32[128,1024]{1,0:T(8,128)} %get-tuple-element.151.refs_3_, ...), custom_call_target="tpu_custom_call" | custom-call | tf_op jit(solution)/shard_map/renew/pallas_call | solution.py:891
  (262 shorter events, 121.9 us)
Async XLA Ops:
  7.2 60.5 %all-gather.8.cloned.1.call-start = ((), (), s32[]{:S(2)}) async-start(), calls=%async_computation.2 | async-start | bytes 9437184 | tf_op jit(solution)/shard_map/all_gather | solution.py:493
  10.0 192.3 %all-gather.10.cloned.1.call-start = ((), (), s32[]{:S(2)}) async-start(), calls=%async_computation.3 | async-start | bytes 9437184 | tf_op jit(solution)/shard_map/all_gather | solution.py:493
  13.6 261.6 %all-gather.12.cloned.1.call-start = ((), (), s32[]{:S(2)}) async-start(), calls=%async_computation.4 | async-start | bytes 9437184 | tf_op jit(solution)/shard_map/all_gather | solution.py:493
  14.8 408.3 %reduce-scatter.2.cloned.1.call-start = ((), (), s32[]{:S(2)}) async-start(), calls=%async_computation.1 | async-start | bytes 9437184 | tf_op jit(solution)/shard_map/reduce_scatter | solution.py:790
  88.4 25.5 %collective-permute-start = (f32[72,1024]{1,0:T(8,128)}, f32[72,1024]{1,0:T(8,128)S(1)}, u32[]{:S(2)}, u32[]{:S(2)}) collective-permute-start(f32[72,1024]{1,0:T(8,128)} %get-tuple-element.115), channel_id=1, source_target_pairs={{0,4},{4,8},{8,12},{12,16},{16,20},{20,24},{24,28},{1,5},{5,9},{9,... | collective-permute-start | bytes 884744 | tf_op jit(solution)/shard_map/ppermute | solution.py:637
  90.6 23.4 %collective-permute-start.1 = (f32[72,1024]{1,0:T(8,128)}, f32[72,1024]{1,0:T(8,128)}, u32[]{:S(2)}, u32[]{:S(2)}) collective-permute-start(f32[72,1024]{1,0:T(8,128)} %get-tuple-element.115), channel_id=1, source_target_pairs={{0,8},{4,12},{8,16},{12,20},{16,24},{20,28},{1,9},{5,13},{9,17},{1... | collective-permute-start | bytes 884744 | tf_op jit(solution)/shard_map/ppermute | solution.py:637
  97.8 21.4 %collective-permute-start.3 = (f32[72,1024]{1,0:T(8,128)}, f32[72,1024]{1,0:T(8,128)}, u32[]{:S(2)}, u32[]{:S(2)}) collective-permute-start(f32[72,1024]{1,0:T(8,128)} %get-tuple-element.115), channel_id=1, source_target_pairs={{0,16},{4,20},{8,24},{12,28},{1,17},{5,21},{9,25},{13,29},{2,18},{... | collective-permute-start | bytes 884744 | tf_op jit(solution)/shard_map/ppermute | solution.py:637
  197.0 42.2 %collective-permute-start.4 = (f32[72,1024]{1,0:T(8,128)}, f32[72,1024]{1,0:T(8,128)S(1)}, u32[]{:S(2)}, u32[]{:S(2)}) collective-permute-start(f32[72,1024]{1,0:T(8,128)} %get-tuple-element.117.done_ref), channel_id=1, source_target_pairs={{4,0},{8,4},{12,8},{16,12},{20,16},{24,20},{28,24},{5,1},{9,5},{13... | collective-permute-start | bytes 884744 | tf_op jit(solution)/shard_map/ppermute | solution.py:686
  198.3 40.9 %collective-permute-start.5 = (f32[72,1024]{1,0:T(8,128)}, f32[72,1024]{1,0:T(8,128)S(1)}, u32[]{:S(2)}, u32[]{:S(2)}) collective-permute-start(f32[72,1024]{1,0:T(8,128)} %get-tuple-element.117.done_ref), channel_id=1, source_target_pairs={{8,0},{12,4},{16,8},{20,12},{24,16},{28,20},{9,1},{13,5},{17,9},{2... | collective-permute-start | bytes 884744 | tf_op jit(solution)/shard_map/ppermute | solution.py:686
  199.6 39.6 %collective-permute-start.6 = (f32[72,1024]{1,0:T(8,128)}, f32[72,1024]{1,0:T(8,128)S(1)}, u32[]{:S(2)}, u32[]{:S(2)}) collective-permute-start(f32[72,1024]{1,0:T(8,128)} %get-tuple-element.117.done_ref), channel_id=1, source_target_pairs={{12,0},{16,4},{20,8},{24,12},{28,16},{13,1},{17,5},{21,9},{25,13},... | collective-permute-start | bytes 884744 | tf_op jit(solution)/shard_map/ppermute | solution.py:686
  200.9 38.3 %collective-permute-start.7 = (f32[72,1024]{1,0:T(8,128)}, f32[72,1024]{1,0:T(8,128)S(1)}, u32[]{:S(2)}, u32[]{:S(2)}) collective-permute-start(f32[72,1024]{1,0:T(8,128)} %get-tuple-element.117.done_ref), channel_id=1, source_target_pairs={{16,0},{20,4},{24,8},{28,12},{17,1},{21,5},{25,9},{29,13},{18,2},{... | collective-permute-start | bytes 884744 | tf_op jit(solution)/shard_map/ppermute | solution.py:686
  239.2 303.8 %all-reduce.5.cloned.1.call-start = ((), (), s32[]{:S(2)}) async-start(), calls=%async_computation.5 | async-start | bytes 4194304 | tf_op jit(solution)/shard_map/psum | solution.py:791
  264.3 59.6 %collective-permute-start.8 = (f32[4,4,128,1024]{3,2,1,0:T(8,128)}, f32[4,4,128,1024]{3,2,1,0:T(8,128)}, u32[]{:S(2)}, u32[]{:S(2)}) collective-permute-start(f32[4,4,128,1024]{3,2,1,0:T(8,128)} %get-tuple-element.132), channel_id=1, source_target_pairs={{0,4},{4,0},{8,12},{12,8},{16,20},{20,16},{24,28},{28,24},{1,5},{5... | collective-permute-start | bytes 25165832 | tf_op jit(solution)/shard_map/ppermute | solution.py:725
  326.0 27.0 %collective-permute-start.9 = (bf16[2,2,128,1024]{3,2,1,0:T(8,128)(2,1)S(1)}, bf16[2,2,128,1024]{3,2,1,0:T(8,128)(2,1)S(1)}, u32[]{:S(2)}, u32[]{:S(2)}) collective-permute-start(bf16[2,2,128,1024]{3,2,1,0:T(8,128)(2,1)S(1)} %fusion.31), channel_id=1, source_target_pairs={{0,8},{4,12},{8,0},{12,4},{16,24},{20,28},{24,16},{28,20},{1,9},{5... | collective-permute-start | bytes 3145736 | tf_op jit(solution)/shard_map/ppermute | solution.py:725
  329.7 32.7 %collective-permute-start.22 = (bf16[2,2,128,1024]{3,2,1,0:T(8,128)(2,1)S(1)}, bf16[2,2,128,1024]{3,2,1,0:T(8,128)(2,1)}, u32[]{:S(2)}, u32[]{:S(2)}) collective-permute-start(bf16[2,2,128,1024]{3,2,1,0:T(8,128)(2,1)S(1)} %fusion.30), channel_id=1, source_target_pairs={{0,16},{4,20},{8,24},{12,28},{16,0},{20,4},{24,8},{28,12},{1,17},{... | collective-permute-start | bytes 3145736 | tf_op jit(solution)/shard_map/ppermute | solution.py:725
  335.6 43.5 %collective-permute-start.11 = (bf16[2,2,128,1024]{3,2,1,0:T(8,128)(2,1)}, bf16[2,2,128,1024]{3,2,1,0:T(8,128)(2,1)S(1)}, u32[]{:S(2)}, u32[]{:S(2)}) collective-permute-start(bf16[2,2,128,1024]{3,2,1,0:T(8,128)(2,1)} %fusion.28), channel_id=1, source_target_pairs={{0,16},{4,20},{8,24},{12,28},{16,0},{20,4},{24,8},{28,12},{1,17},{... | collective-permute-start | bytes 3145736 | tf_op jit(solution)/shard_map/ppermute | solution.py:725
  355.7 34.4 %collective-permute-start.10 = (bf16[2,128,1024]{2,1,0:T(8,128)(2,1)}, bf16[2,128,1024]{2,1,0:T(8,128)(2,1)}, u32[]{:S(2)}, u32[]{:S(2)}) collective-permute-start(bf16[2,128,1024]{2,1,0:T(8,128)(2,1)} %fusion.40), channel_id=1, source_target_pairs={{0,16},{4,20},{8,24},{12,28},{16,0},{20,4},{24,8},{28,12},{1,17},{... | collective-permute-start | bytes 1572872 | tf_op jit(solution)/shard_map/ppermute | solution.py:725
  359.1 46.6 %collective-permute-start.20 = (bf16[2,2,128,1024]{3,2,1,0:T(8,128)(2,1)S(1)}, bf16[2,2,128,1024]{3,2,1,0:T(8,128)(2,1)}, u32[]{:S(2)}, u32[]{:S(2)}) collective-permute-start(bf16[2,2,128,1024]{3,2,1,0:T(8,128)(2,1)S(1)} %fusion.29), channel_id=1, source_target_pairs={{0,8},{4,12},{8,0},{12,4},{16,24},{20,28},{24,16},{28,20},{1,9},{5... | collective-permute-start | bytes 3145736 | tf_op jit(solution)/shard_map/ppermute | solution.py:725
  362.1 32.7 %collective-permute-start.25 = (f32[104,128]{1,0:T(8,128)S(1)}, f32[104,128]{1,0:T(8,128)S(1)}, u32[]{:S(2)}, u32[]{:S(2)}) collective-permute-start(f32[104,128]{1,0:T(8,128)S(1)} %bitcast_add_fusion.2), channel_id=1, source_target_pairs={{0,8},{4,12},{8,0},{12,4},{16,24},{20,28},{24,16},{28,20},{1,9},{5... | collective-permute-start | bytes 159752 | tf_op jit(solution)/shard_map/ppermute | solution.py:725
  364.9 40.8 %collective-permute-start.23 = (bf16[2,128,1024]{2,1,0:T(8,128)(2,1)}, bf16[2,128,1024]{2,1,0:T(8,128)(2,1)}, u32[]{:S(2)}, u32[]{:S(2)}) collective-permute-start(bf16[2,128,1024]{2,1,0:T(8,128)(2,1)} %fusion.32), channel_id=1, source_target_pairs={{0,8},{4,12},{8,0},{12,4},{16,24},{20,28},{24,16},{28,20},{1,9},{5... | collective-permute-start | bytes 1572872 | tf_op jit(solution)/shard_map/ppermute | solution.py:725
  403.3 58.5 %collective-permute-start.28 = (f32[104,128]{1,0:T(8,128)S(1)}, f32[104,128]{1,0:T(8,128)S(1)}, u32[]{:S(2)}, u32[]{:S(2)}) collective-permute-start(f32[104,128]{1,0:T(8,128)S(1)} %add.553), channel_id=1, source_target_pairs={{0,2},{1,3},{2,0},{3,1},{4,6},{5,7},{6,4},{7,5},{8,10},{9,11},{10,... | collective-permute-start | bytes 159752 | tf_op jit(solution)/shard_map/ppermute | solution.py:787
  433.2 42.7 %collective-permute-start.16 = (bf16[6,32,1024]{2,1,0:T(8,128)(2,1)S(1)}, bf16[6,32,1024]{2,1,0:T(8,128)(2,1)S(1)}, u32[]{:S(2)}, u32[]{:S(2)}) collective-permute-start(bf16[6,32,1024]{2,1,0:T(8,128)(2,1)S(1)} %pad_maximum_fusion.5), channel_id=1, source_target_pairs={{0,1},{1,2},{2,3},{3,0},{4,5},{5,6},{6,7},{7,4},{8,9},{9,10},{10,1... | collective-permute-start | bytes 1179656 | tf_op jit(solution)/shard_map/ppermute | solution.py:778
  461.8 34.9 %collective-permute-start.17 = (bf16[6,32,1024]{2,1,0:T(8,128)(2,1)S(1)}, bf16[6,32,1024]{2,1,0:T(8,128)(2,1)S(1)}, u32[]{:S(2)}, u32[]{:S(2)}) collective-permute-start(bf16[6,32,1024]{2,1,0:T(8,128)(2,1)S(1)} %pad_maximum_fusion.5), channel_id=1, source_target_pairs={{0,2},{1,3},{2,0},{3,1},{4,6},{5,7},{6,4},{7,5},{8,10},{9,11},{10,... | collective-permute-start | bytes 1179656 | tf_op jit(solution)/shard_map/ppermute | solution.py:778
  462.6 38.2 %collective-permute-start.18 = (bf16[6,32,1024]{2,1,0:T(8,128)(2,1)S(1)}, bf16[6,32,1024]{2,1,0:T(8,128)(2,1)S(1)}, u32[]{:S(2)}, u32[]{:S(2)}) collective-permute-start(bf16[6,32,1024]{2,1,0:T(8,128)(2,1)S(1)} %pad_maximum_fusion.5), channel_id=1, source_target_pairs={{0,3},{1,0},{2,1},{3,2},{4,7},{5,4},{6,5},{7,6},{8,11},{9,8},{10,9... | collective-permute-start | bytes 1179656 | tf_op jit(solution)/shard_map/ppermute | solution.py:778
  (41 other events, 963.8 us)
Sparse Core Ops, SparseCore 0:
  10.5 57.1 all-gather.7
  69.6 68.1 all-gather.9
  139.7 57.3 all-gather.11
  239.3 84.6 reduce-scatter.1
  425.5 117.4 all-reduce.4

commit v2 on v1

--- a/solution.py
+++ b/solution.py
@@ -147,14 +147,11 @@
     return total
 
 
-def qkv_kernel(
-    h_ref, wq_ref, wk_ref, wv_ref, b_ref, table_ref, marks_ref, const_ref, weight_ref,
-    q_ref, k_ref, v_ref, vl_ref, uq_ref, uk_ref, s_ref,
+def key_kernel(
+    h_ref, wk_ref, wv_ref, b_ref, table_ref, marks_ref, const_ref, weight_ref,
+    k_ref, v_ref, vl_ref, uk_ref, s_ref,
 ):
     rows = h_ref[...]
-    query = turn(dot_nn(rows, flat(wq_ref[...])) + b_ref[0:1, :], table_ref)
-    uq_ref[...] = query.astype(bf16)
-    q_ref[...] = phi(query, const_ref, weight_ref).astype(bf16)
     key = turn(dot_nn(rows, flat(wk_ref[...])) + b_ref[1:2, :], table_ref)
     uk_ref[...] = key.astype(bf16)
     feats = phi(key, const_ref, weight_ref).astype(bf16)
@@ -171,8 +168,16 @@
     s_ref[HEAD:STATE, :] = jnp.broadcast_to(jnp.sum(kept, 0, keepdims=True), (8, LANES))
 
 
+def query_kernel(
+    h_ref, wq_ref, b_ref, table_ref, const_ref, weight_ref, done_ref, q_ref, uq_ref
+):
+    query = turn(dot_nn(h_ref[...], flat(wq_ref[...])) + b_ref[0:1, :], table_ref)
+    uq_ref[...] = query.astype(bf16)
+    q_ref[...] = phi(query, const_ref, weight_ref).astype(bf16)
+
+
 def attend_kernel(
-    q_ref, k_ref, v_ref, vl_ref, uq_ref, s_ref, g_ref, wm_ref, table_ref, row_ref, marks_ref, const_ref, core_ref,
+    q_ref, k_ref, v_ref, vl_ref, uq_ref, s_ref, g_ref, wm_ref, table_ref, row_ref, marks_ref, const_ref, core_ref, done_ref,
     mixed_ref, dq_ref, dk_ref, dv_ref, ds_ref, bias_ref, out_ref, send_ref, keep_ref,
     dnum_ref, dlow_ref, dden_ref,
 ):
@@ -208,7 +213,7 @@
             score = jnp.where(causal, dot_nt(query, key * mask), 0.0)
             totals = totals + jnp.sum(score, 1, keepdims=True) * mask.astype(f32)
             high, low = halves(score)
-            scores.append((high, low))
+            scores.append(high)
             number = number + dot_three(dot_nn, high, low, value * mask, value_low * mask)
         mixed = number / totals
         mixed_ref[here, :] = mixed.astype(bf16)
@@ -230,9 +235,12 @@
             slope = dot_three(dot_nt, dnum, dlow, value * mask, value_low * mask) + column
             high, low = halves(jnp.where(causal, slope, 0.0))
             grad_query = grad_query + dot_nn(high, key * mask) + dot_nn(low, key * mask)
-            grad_key = grad_key + dot_tn(high, query * mask) + dot_tn(low, query * mask)
-            high, low = scores[index]
-            grad_value = grad_value + dot_three(dot_tn, high, low, dnum * mask, dlow * mask)
+            part_query = query * mask
+            grad_key = grad_key + dot_tn(
+                jnp.concatenate([high, low], 0), jnp.concatenate([part_query, part_query], 0)
+            )
+            both = dot_tn(scores[index], jnp.concatenate([dnum * mask, dlow * mask], 1))
+            grad_value = grad_value + both[:, :LANES] + both[:, LANES:]
         dk_ref[here, :] = grad_key
         dv_ref[here, :] = grad_value
         grad = phi_back(grad_query, query.astype(f32), uq_ref[here, :].astype(f32), const_ref)
@@ -341,36 +349,61 @@
     out_ref, dh_ref, bias_ref, *grad_refs,
 ):
     step = pl.program_id(0)
-    grad_out = g_ref[...]
+    grad_out, rows_in, flipped = g_ref[...], h_ref[...], ht_ref[...]
     expand, shrink = flat(we_ref[...]), flat(ws_ref[...])
     width = expand.shape[1]
-    pre = dot_nn(h_ref[...], expand) + be_ref[...]
-    cdf, bell = normal_cdf(pre)
-    active = (pre * cdf).astype(bf16)
-    slope = cdf + pre * bell * (1.0 / math.sqrt(2.0 * math.pi))
-    grad = (dot_nt(grad_out, shrink) * slope).astype(bf16)
-    bias_ref[...] = jnp.broadcast_to(
-        jnp.sum(grad.astype(f32), 0, keepdims=True), bias_ref.shape
-    )
+    half = width // 2
     _, blocks, rows, _ = grad_refs[0].shape
-    where = lax.rem(step, D // width)
     block = step // (D // width)
-    lanes = pl.ds(pl.multiple_of(where * width, width), width)
-    wide = dot_nn(ht_ref[...], grad).astype(bf16)
-    tall = dot_tn(active, grad_out).astype(bf16).reshape(2, blocks // 2, rows, D)
-    if len(grad_refs) == 1:
-        grad_refs[0][:, block, :, lanes] = wide.reshape(-1, rows, width)
-        grad_refs[0][pl.ds(2 * step, 2), blocks // 2 :] = tall
-    else:
-        send_ref, keep_ref = grad_refs
-        first = core_ref[0] == 0
-        pairs = wide.reshape(-1, 2, rows, width)
-        keep_ref[:, block, :, lanes] = jnp.where(first, pairs[:, 0], pairs[:, 1])
-        send_ref[:, block, :, lanes] = jnp.where(first, pairs[:, 1], pairs[:, 0])
-        keep_ref[step, blocks // 2 :] = jnp.where(first, tall[0], tall[1])
-        send_ref[step, blocks // 2 :] = jnp.where(first, tall[1], tall[0])
-    accumulate(out_ref, dot_nn(active, shrink))
-    accumulate(dh_ref, dot_nt(grad, expand))
+    first = core_ref[0] == 0
+
+    def products(side):
+        cut = slice(side * half, (side + 1) * half)
+        pre = dot_nn(rows_in, expand[:, cut]) + be_ref[:, cut]
+        return pre, dot_nt(grad_out, shrink[cut])
+
+    def pointwise(side, pre, grad):
+        cdf, bell = normal_cdf(pre)
+        active = (pre * cdf).astype(bf16)
+        slope = cdf + pre * bell * (1.0 / math.sqrt(2.0 * math.pi))
+        grad = (grad * slope).astype(bf16)
+        bias_ref[:, side * half : (side + 1) * half] = jnp.broadcast_to(
+            jnp.sum(grad.astype(f32), 0, keepdims=True), (8, half)
+        )
+        return active, grad
+
+    def gradients(side, active, grad):
+        start = lax.rem(step, D // width) * width + side * half
+        lanes = pl.ds(pl.multiple_of(start, half), half)
+        wide = dot_nn(flipped, grad).astype(bf16)
+        tall = dot_tn(active, grad_out).astype(bf16).reshape(blocks // 2, rows, D)
+        if len(grad_refs) == 1:
+            grad_refs[0][:, block, :, lanes] = wide.reshape(-1, rows, half)
+            grad_refs[0][2 * step + side, blocks // 2 :] = tall
+        else:
+            send_ref, keep_ref = grad_refs
+            pairs = wide.reshape(-1, 2, rows, half)
+            keep_ref[:, block, :, lanes] = jnp.where(first, pairs[:, 0], pairs[:, 1])
+            send_ref[:, block, :, lanes] = jnp.where(first, pairs[:, 1], pairs[:, 0])
+
+            @pl.when(first == (side == 0))
+            def _():
+                keep_ref[step, blocks // 2 :] = tall
+
+            @pl.when(first != (side == 0))
+            def _():
+                send_ref[step, blocks // 2 :] = tall
+
+    left = products(0)
+    left = pointwise(0, *left)
+    right = products(1)
+    gradients(0, *left)
+    right = pointwise(1, *right)
+    forward = dot_nn(left[0], shrink[:half])
+    backward = dot_nt(left[1], expand[:, :half])
+    gradients(1, *right)
+    accumulate(out_ref, forward + dot_nn(right[0], shrink[half:]))
+    accumulate(dh_ref, backward + dot_nt(right[1], expand[:, half:]))
 
 
 def lamb_step(master, first, second, grad, mean_ref, square_ref, update_ref, norms_ref):
@@ -498,9 +531,8 @@
             [array[:, (j * parts + index) * sub : (j * parts + index + 1) * sub] for j in range(n)], 1
         )
 
-    attend = gather(
-        [attend_weight[:, :D], attend_weight[:, D : 2 * D], attend_weight[:, 2 * D :], merge_weight]
-    )
+    attend = gather([attend_weight[:, :D], attend_weight[:, D : 2 * D], attend_weight[:, 2 * D :]])
+    merge = gather([merge_weight])
     feeds = []
     for index in range(parts):
         wide = of_part(expand_weight, index)
@@ -609,26 +641,50 @@
 
     constants = [whole((3, LANES, LANES)), whole((1, LANES))]
     tables = [whole((4, rows, 2 * HEAD)), whole((16, LANES))]
-    query, key, value, value_low, turned_query, turned_key, summary = pl.pallas_call(
-        qkv_kernel,
+    biases = bias_attend.reshape(3, D)
+    key, value, value_low, turned_key, summary = pl.pallas_call(
+        key_kernel,
         grid=(NGROUP,),
         in_specs=[
             whole((rows, D)),
-            *[projection(index) for index in range(3)],
+            *[projection(index) for index in range(1, 3)],
             columns(3),
             *tables,
             *constants,
         ],
-        out_specs=[columns(rows)] * 6 + [columns(STATE)],
-        out_shape=[shaped((rows, D), bf16)] * 6 + [shaped((STATE, D), f32)],
+        out_specs=[columns(rows)] * 4 + [columns(STATE)],
+        out_shape=[shaped((rows, D), bf16)] * 4 + [shaped((STATE, D), f32)],
         compiler_params=params(),
         cost_estimate=pl.CostEstimate(
-            flops=6 * rows * D * D + 22 * rows * D * LANES,
-            bytes_accessed=20 * rows * D,
-            transcendentals=2 * rows * D,
+            flops=4 * rows * D * D + 14 * rows * D * LANES,
+            bytes_accessed=14 * rows * D,
+            transcendentals=rows * D,
         ),
-        name="qkv",
-    )(low_one, attend, attend, attend, bias_attend.reshape(3, D), table, marks, const, weighting)
+        name="keys",
+    )(low_one, attend, attend, biases, table, marks, const, weighting)
+    query, turned_query = pl.pallas_call(
+        query_kernel,
+        grid=(NGROUP,),
+        in_specs=[
+            whole((rows, D)),
+            projection(0),
+            columns(3),
+            tables[0],
+            *constants,
+            pl.BlockSpec(memory_space=pl.ANY),
+        ],
+        out_specs=[columns(rows)] * 2,
+        out_shape=[shaped((rows, D), bf16)] * 2,
+        compiler_params=params(),
+        cost_estimate=pl.CostEstimate(
+            flops=2 * rows * D * D + 8 * rows * D * LANES,
+            bytes_accessed=8 * rows * D,
+            transcendentals=rows * D,
+        ),
+        name="queries",
+    )(low_one, attend, biases, table, const, weighting, summary)
+
+    fed = [feed(0, query, False)]
 
     reaches = range(1, n // 2 + 1)
     own_before, own_final = label(device * rows - 1), segment[-1]
@@ -645,12 +701,13 @@
             *[columns(rows)] * 5,
             columns(STATE),
             whole((rows, D)),
-            pl.BlockSpec((LANES // own, 1, own, D), lambda g: (g, 3, 0, 0)),
+            pl.BlockSpec((LANES // own, 1, own, D), lambda g: (g, 0, 0, 0)),
             whole((4, rows, 2 * HEAD)),
             whole((8, rows)),
             whole((16, LANES)),
             whole((3, LANES, LANES)),
             scalar(),
+            pl.BlockSpec(memory_space=pl.ANY),
         ],
         out_specs=[columns(rows)] * 4
         + [columns(STATE), columns(8), total_of((rows, D))]
@@ -676,10 +733,11 @@
         name="attend",
     )(
         query, key, value, value_low, turned_query, carried,
-        grad_out, attend, table, row_table, marks, const, core_ref,
-    )
-
-    fed = [feed(0, grad_carried, False)]
+        grad_out, merge, table, row_table, marks, const, core_ref, fed[0][2],
+    )
+
+    for index in range(1, parts):
+        fed.append(feed(index, grad_carried, True))
 
     returned = jnp.zeros_like(summary)
     for far in reaches:
@@ -713,19 +771,15 @@
         name="finish",
     )(
         key, value, value_low, turned_key, grad_query, part_key, part_value, returned,
-        table, marks, const, attend, attend, attend, flipped_one, core_ref, send, keep, fed[0][2],
-    )
-
-    for index in range(1, parts):
-        fed.append(feed(index, rest_bias, True))
+        table, marks, const, attend, attend, attend, flipped_one, core_ref, send, keep, fed[-1][2],
+    )
 
     bits = n.bit_length() - 1
 
     def exchange(array, bit):
         return lax.ppermute(array, "seq", [(i, i ^ (1 << bit)) for i in range(n)])
 
-    def scatter(send, keep):
-        came = exchange(send, 0)
+    def scatter(keep, came):
         middle = keep.shape[1] // 2
         order = list(range(1, bits))
         turned = (bits - 1) // 2
@@ -754,7 +808,75 @@
                 left = [b for b in places if b not in fixed]
                 sides[side].append((exchange(other, bit), left, 0))
         fixed = {b: (device >> b) & 1 for b in order}
-        return [pick(terms, fixed) for terms in sides]
+        return jnp.concatenate([pick(terms, fixed) for terms in sides], 0)
+
+    spot = jnp.stack([(device >> 1) & 1, (device >> 2) & 1]).astype(jnp.int32)
+
+    def add_step(terms, outs, done, count):
+        flat_terms = [term for group in terms for term in group]
+        sizes = [len(group) for group in terms]
+
+        def kernel(spot_ref, *refs):
+            ins, out_refs = refs[: len(flat_terms)], refs[len(flat_terms) + len(done) :]
+            at = 0
+            for size, (out_ref, place) in zip(sizes, count(out_refs)):
+                shape = out_ref.at[place].shape
+                total = ins[at][...].astype(f32).reshape(shape)
+                for ref in ins[at + 1 : at + size]:
+                    total = total + ref[...].astype(f32).reshape(shape)
+                out_ref[place] = total.astype(out_ref.dtype)
+                at += size
+
+        return pl.pallas_call(
+            kernel,
+            grid_spec=pltpu.PrefetchScalarGridSpec(
+                num_scalar_prefetch=1,
+                grid=(2,),
+                in_specs=[spec for _, spec in flat_terms]
+                + [pl.BlockSpec(memory_space=pl.ANY)] * len(done),
+                out_specs=[spec for _, spec in outs],
+            ),
+            out_shape=[shape for shape, _ in outs],
+            compiler_params=params(),
+            name="add",
+        )(spot, *[array for array, _ in flat_terms], *done)
+
+    one, two = (1, 1, 1, own, D), (1, 1, 2, own, D)
+
+    def step_one(keep, came, done):
+        wide = pl.BlockSpec(two, lambda g, at: (g, 1 - at[0], 0, 0, 0))
+        tall_part = pl.BlockSpec(two, lambda g, at: (1 - at[1], g, 1, 0, 0))
+        out = shaped((2, 2, own, D), bf16), pl.BlockSpec((1, 2, own, D), lambda g, at: (g, 0, 0, 0))
+        terms = [[(keep, wide), (came, wide)], [(keep, tall_part), (came, tall_part)]]
+        first, second = add_step(terms, [out] * 2, done, lambda refs: [(ref, ...) for ref in refs])
+        return first, exchange(first, 1), exchange(second, 2)
+
+    def step_two(keep, came, first, second, done):
+        wide = pl.BlockSpec(one, lambda g, at: (1 - at[1], at[0], g, 0, 0))
+        tall_part = pl.BlockSpec(one, lambda g, at: (at[1], 1 - at[0], 2 + g, 0, 0))
+        first_of = pl.BlockSpec((1, 1, own, D), lambda g, at: (1 - at[1], g, 0, 0))
+        second_of = pl.BlockSpec((1, 1, own, D), lambda g, at: (1 - at[0], g, 0, 0))
+        out = shaped((2, own, D), bf16), pl.BlockSpec((1, own, D), lambda g, at: (g, 0, 0))
+        terms = [
+            [(keep, wide), (came, wide), (first, first_of)],
+            [(keep, tall_part), (came, tall_part), (second, second_of)],
+        ]
+        sent = add_step(terms, [out] * 2, done, lambda refs: [(ref, ...) for ref in refs])
+        return exchange(sent[0], 2), exchange(sent[1], 1)
+
+    def step_three(keep, came, first, second, last_first, last_second, kind, done):
+        wide = pl.BlockSpec(one, lambda g, at: (at[1], at[0], g, 0, 0))
+        tall_part = pl.BlockSpec(one, lambda g, at: (at[1], at[0], 2 + g, 0, 0))
+        first_of = pl.BlockSpec((1, 1, own, D), lambda g, at: (at[1], g, 0, 0))
+        second_of = pl.BlockSpec((1, 1, own, D), lambda g, at: (at[0], g, 0, 0))
+        last = pl.BlockSpec((1, own, D), lambda g, at: (g, 0, 0))
+        out = shaped((2, 2, own, D), kind), pl.BlockSpec((2, 1, own, D), lambda g, at: (0, g, 0, 0))
+        terms = [
+            [(keep, wide), (came, wide), (first, first_of), (last_first, last)],
+            [(keep, tall_part), (came, tall_part), (second, second_of), (last_second, last)],
+        ]
+        result = add_step(terms, [out], done, lambda refs: [(refs[0], 0), (refs[0], 1)])
+        return result[0].reshape(4, own, D)
 
     groups = lax.axis_size("dp")
     group = lax.axis_index("dp")
@@ -788,11 +910,29 @@
         return value
 
     first_part = lax.psum_scatter(fed[0][3], "seq", scatter_dimension=0, tiled=False)
-    feed_sums = [lax.psum([first_part[:tall], first_part[tall:]], "dp")]
-    attend_sum = sum_groups(jnp.concatenate(scatter(send, keep), 0), 2)
-    for index in range(1, parts):
-        pieces = [piece.astype(bf16) for piece in scatter(*fed[index][3:])]
-        feed_sums.append(lax.psum(pieces, "dp"))
+    feed_sums = [lax.psum(first_part, "dp")]
+    if bits == 3 and parts == 2:
+        deep = (2, 2, 4, own, D)
+        feed_send, feed_keep = (array.reshape(deep) for array in fed[1][3:])
+        feed_came = exchange(feed_send, 0)
+        send, keep = send.reshape(deep), keep.reshape(deep)
+        came = exchange(send, 0)
+        begun, *feed_first = step_one(feed_keep, feed_came, [rest_bias])
+        started, *first = step_one(keep, came, [begun, first_part])
+        feed_second = step_two(feed_keep, feed_came, *feed_first, [started])
+        second = step_two(keep, came, *first, feed_second)
+        attend_part = step_three(keep, came, *first, *second, f32, [])
+        feed_part = step_three(
+            feed_keep, feed_came, *feed_first, *feed_second, bf16, [attend_part, feed_sums[0]]
+        )
+        feed_sums.append(lax.psum(feed_part, "dp"))
+        grad_one = grad_one + 0.0 * started[0, 0, 0, 0].astype(f32)
+    else:
+        for index in range(1, parts):
+            part = scatter(fed[index][4], exchange(fed[index][3], 0))
+            feed_sums.append(lax.psum(part.astype(bf16), "dp"))
+        attend_part = scatter(keep, exchange(send, 0))
+    attend_sum = sum_groups(attend_part, 2)
 
     grad_float = grad_out.astype(f32)
     result = inputs + attend_out + bias_merge + bias_shrink + sum(f[0] for f in fed)
@@ -820,6 +960,7 @@
             grad_bias_out,
         ]
     )
+    grad_vector = grad_vector + 0.0 * attend_part[0, 0, 0].astype(f32)
     vector_sum = sum_all(grad_vector.reshape(-1, 128)).reshape(-1)
     share = gains_biases.shape[0]
     own_vector = lax.dynamic_slice(vector_sum, (device * share,), (share,))
@@ -840,7 +981,7 @@
             in_specs=[of_expand] * 3
             + [pl.BlockSpec((1, own, wide_cols), lambda g: (g // per, 0, g % per))]
             + [of_shrink] * 3
-            + [pl.BlockSpec((sub // strips, D), lambda g: (g, 0))]
+            + [pl.BlockSpec((sub // strips, D), lambda g: (strips + g, 0))]
             + before_specs,
             out_specs=[total_of((2, 8, wide_cols)), total_of((2, 8, D))]
             + [of_expand] * 3
@@ -852,8 +993,8 @@
             compiler_params=params(),
             name="lamb_feed",
         )(
-            expand_weight, expand_first, expand_second, feed_sums[index][0],
-            shrink_weight, shrink_first, shrink_second, flat(feed_sums[index][1]),
+            expand_weight, expand_first, expand_second, feed_sums[index],
+            shrink_weight, shrink_first, shrink_second, flat(feed_sums[index]),
             *([] if held is None else held),
         )
         expand_sums.append(jnp.sum(expand_norm, (1, 2)))
@@ -890,17 +1031,17 @@
     squares = lax.psum(local, "seq")
     fresh = pl.pallas_call(
         renew_kernel,
-        grid=(strips,),
+        grid=(4,),
         in_specs=[scalar()]
-        + [pl.BlockSpec((own, 3 * D // strips), lambda g: (0, g))] * 2
-        + [pl.BlockSpec((own, D // strips), lambda g: (0, g))] * 2
-        + [pl.BlockSpec((own, FF // strips), lambda g: (0, g))] * 2
-        + [pl.BlockSpec((FF // n // strips, D), lambda g: (g, 0))] * 2,
+        + [pl.BlockSpec((own, 3 * D // 4), lambda g: (0, g))] * 2
+        + [pl.BlockSpec((own, D // 4), lambda g: (0, g))] * 2
+        + [pl.BlockSpec((own, FF // 4), lambda g: (0, g))] * 2
+        + [pl.BlockSpec((FF // n // 4, D), lambda g: (g, 0))] * 2,
         out_specs=[
-            pl.BlockSpec((own, 3 * D // strips), lambda g: (0, g)),
-            pl.BlockSpec((own, D // strips), lambda g: (0, g)),
-            pl.BlockSpec((own, FF // strips), lambda g: (0, g)),
-            pl.BlockSpec((FF // n // strips, D), lambda g: (g, 0)),
+            pl.BlockSpec((own, 3 * D // 4), lambda g: (0, g)),
+            pl.BlockSpec((own, D // 4), lambda g: (0, g)),
+            pl.BlockSpec((own, FF // 4), lambda g: (0, g)),
+            pl.BlockSpec((FF // n // 4, D), lambda g: (g, 0)),
         ],
         out_shape=[
             shaped((own, 3 * D), f32),

time: 606 us -> 583 us (0.962)
  starting transfers between devices: 83.2 us -> 44.2 us
  local copies, waits for them, and re-layouts: 20.1 us -> 50.3 us
  waiting for transfers between devices: 162 us -> 146 us
  Pallas kernels: 232 us -> 246 us
  other arithmetic: 51.2 us -> 38.2 us
    pallas_call x2 -> x9, Pallas kernels: 29.2 us -> 58.4 us  [the longest x6 26 us: add_step(): pl.pallas_call(kernel, grid_spec=pltpu.PrefetchScalarGridSpec(num_scalar_...]
    ppermute x3, starting transfers between devices: 30.9 us -> 4.58 us  [sum_groups(): came = lax.ppermute(total, 'dp', pairs)]
    psum x1 -> x2, waiting for transfers between devices: 30.4 us -> 6 us  [the longest x1 6 us: per_device(): feed_sums.append(lax.psum(feed_part, 'dp'))]
    pallas_call x0 -> x6, local copies, waits for them, and re-layouts: none -> 19.9 us  [the longest x4 12.7 us: feed(): pl.pallas_call(feed_kernel, grid=(n // 2,), in_specs=[whole((rows, D)), w...]
    convert_element_type x8 -> x0, other arithmetic: 17 us -> none  [the longest x6 10.9 us: scatter(): other = pick(sides[side], fixed).astype(bf16)]
    pallas_call x1, Pallas kernels: 76.3 us -> 61.4 us  [per_device(): pl.pallas_call(attend_kernel, grid=(NGROUP,), in_specs=[*[columns(rows)]...]
    ppermute x3, waiting for transfers between devices: 35.5 us -> 48.4 us  [sum_groups(): came = lax.ppermute(total, 'dp', pairs)]
    ppermute x13, starting transfers between devices: 27.7 us -> 17.6 us  [exchange(): return lax.ppermute(array, 'seq', [(i, i ^ 1 << bit) for i in range(n)])]
  transfers between devices with their start and end apart: 34 -> 36, of which waited for: 15 -> 15; matrix products, arithmetic and copies ran while one was open for 10% -> 13% of each run, Pallas kernels for 34% -> 40%
where the time goes in v2:
time: 583 us; the launch traced here: 575 us
  Pallas kernels  246 us (42%)
  waiting for transfers between devices  146 us (25%)
  local copies, waits for them, and re-layouts  50.3 us (9%)
  starting transfers between devices  44.2 us (8%)
  other arithmetic  38.2 us (7%)
  between operations  27.1 us (5%)
  blocking collectives  24.4 us (4%)
    pallas_call x2, Pallas kernels, feed(): pl.pallas_call(feed_kernel, grid=(n // 2,), in_specs=[whole((rows, D)), w...  73.9 us
    pallas_call x1, Pallas kernels, per_device(): pl.pallas_call(attend_kernel, grid=(NGROUP,), in_specs=[*[columns(rows)]...  61.4 us
    ppermute x13, waiting for transfers between devices, exchange(): return lax.ppermute(array, 'seq', [(i, i ^ 1 << bit) for i in range(n)])  49.7 us
    ppermute x3, waiting for transfers between devices, sum_groups(): came = lax.ppermute(total, 'dp', pairs)  48.4 us
    all_gather x4, waiting for transfers between devices, gather(): full = lax.all_gather(shard, 'seq', axis=0, tiled=False)  34.5 us
    pallas_call x6, Pallas kernels, add_step(): pl.pallas_call(kernel, grid_spec=pltpu.PrefetchScalarGridSpec(num_scalar_...  26 us
    pallas_call x1, Pallas kernels, per_device(): pl.pallas_call(finish_kernel, grid=(NGROUP,), in_specs=[columns(rows)] *...  24.4 us
    pallas_call x2, Pallas kernels, per_device(): pl.pallas_call(lamb_feed_kernel, grid=(strips,), in_specs=[of_expand] * 3...  18.6 us
  transfers between devices with their start and end apart: 36, of which 15 were waited for; matrix products, arithmetic and copies ran while one was open for 13% of the time, Pallas kernels for 40%

profile of v2, /device:TPU:0, one launch (start us, length us, event | category | flops | bytes accessed | tf_op | source)
XLA Modules:
  0.0 575.2 jit_solution(9255738563043397956)
XLA Ops:
  15.5 10.6 %all-gather.4 = bf16[8,1,1664]{2,1,0:T(2,128)(2,1)S(1)} all-gather(bf16[1,1,1664]{2,1,0:T(2,128)(2,1)S(1)} %reshape.330), channel_id=1, replica_groups=mesh['seq'=8,'dp'=4] {'seq'}, dimensions={0}, use_global_device_ids=true | all-gather | bytes 29952 | tf_op jit(solution)/shard_map/all_gather | solution.py:545
  59.5 13.6 %keys.1 = (bf16[768,1024]{1,0:T(8,128)(2,1)}, bf16[768,1024]{1,0:T(8,128)(2,1)}, bf16[768,1024]{1,0:T(8,128)(2,1)}, bf16[768,1024]{1,0:T(8,128)(2,1)}, f32[72,1024]{1,0:T(8,128)}) custom-call(bf16[768,1024]{1,0:T(8,128)(2,1)} %copy.129.h_ref, bf16[8,3,128,1024]{3,2,1,0:T(8,128)(2,1)} %bitcast.189, bf16[8,3,128,1024]{3,2,1,0:T(8,128)(2,1)} %bitcast.190, ...), custom_call_target="tpu_custom_call" | custom-call | flops 6039797760 | bytes 11010048 | tf_op jit(solution)/shard_map/keys/pallas_call | solution.py:645
  83.1 11.4 %queries.1 = (bf16[768,1024]{1,0:T(8,128)(2,1)}, bf16[768,1024]{1,0:T(8,128)(2,1)}) custom-call(bf16[768,1024]{1,0:T(8,128)(2,1)} %copy.129.h_ref, bf16[8,3,128,1024]{3,2,1,0:T(8,128)(2,1)} %bitcast.191, f32[3,1024]{1,0:T(4,128)} %slice.288.b_ref, f32[4,768,128]{2,1,0:T(8,128)} %pad_maximum_fusion.table_ref, bf16[3,256,256]{2,1,0:T(8,128)(2,1)} %constant.228.clone.const_ref, ...), custom_call_target="tpu_custom_call" | custom-call | flops 3221225472 | bytes 6291456 | tf_op jit(solution)/shard_map/queries/pallas_call | solution.py:665
  94.5 6.3 %collective-permute-done.3 = f32[72,1024]{1,0:T(8,128)S(1)} collective-permute-done((f32[72,1024]{1,0:T(8,128)}, f32[72,1024]{1,0:T(8,128)S(1)}, u32[]{:S(2)}, u32[]{:S(2)}) %collective-permute-start.3) | collective-permute-done | bytes 294944 | tf_op jit(solution)/shard_map/ppermute | solution.py:693
  101.5 30.7 %all-gather.14.cloned.1.call-done = bf16[4096,1024]{1,0:T(8,128)(2,1)} async-done(((bf16[512,1024]{1,0:T(8,128)(2,1)}), bf16[4096,1024]{1,0:T(8,128)(2,1)}) %all-gather.14.cloned.1.call-update) | async-done | bytes 8388624 | tf_op jit(solution)/shard_map/all_gather | solution.py:526
  132.3 35.8 %feed.2 = (f32[768,1024]{1,0:T(8,128)}, f32[768,1024]{1,0:T(8,128)}, f32[8,2048]{1,0:T(8,128)}, bf16[8,4,128,1024]{3,2,1,0:T(8,128)(2,1)}) custom-call(bf16[768,1024]{1,0:T(8,128)(2,1)} %copy.131.h_ref, bf16[1024,768]{1,0:T(8,128)(2,1)} %bitcast.202, bf16[768,1024]{1,0:T(8,128)(2,1)} %bitcast.210, bf16[8,4,128,1024]{3,2,1,0:T(8,128)(2,1)} %bitcast.254, ...), custom_call_target="tpu_custom_call" | custom-call | flops 38654705664 | bytes 20971520 | tf_op jit(solution)/shard_map/feed/pallas_call | solution.py:602
  168.8 61.4 %attend.1 = (bf16[768,1024]{1,0:T(8,128)(2,1)}, bf16[768,1024]{1,0:T(8,128)(2,1)}, f32[768,1024]{1,0:T(8,128)}, f32[768,1024]{1,0:T(8,128)}, f32[72,1024]{1,0:T(...) custom-call(bf16[768,1024]{1,0:T(8,128)(2,1)} %get-tuple-element.119, ...), custom_call_target="tpu_custom_call" | custom-call | flops 31809601536 | bytes 18874368 | tf_op jit(solution)/shard_map/attend/pallas_call | solution.py:697
  235.6 38.1 %feed.3 = (f32[768,1024]{1,0:T(8,128)}, f32[768,1024]{1,0:T(8,128)}, f32[8,2048]{1,0:T(8,128)}, bf16[4,4,128,1024]{3,2,1,0:T(8,128)(2,1)}, bf16[4,4,128,1024]{3,2,1,0:T(8,128)(2,1)}) custom-call(bf16[768,1024]{1,0:T(8,128)(2,1)} %copy.131.h_ref, bf16[1024,768]{1,0:T(8,128)(2,1)} %bitcast.203, bf16[768,1024]{1,0:T(8,128)(2,1)} %bitcast.212, ...), custom_call_target="tpu_custom_call" | custom-call | flops 38654705664 | bytes 20971520 | tf_op jit(solution)/shard_map/feed/pallas_call | solution.py:602
  274.6 24.4 %finish.1 = (f32[16,1024]{1,0:T(8,128)}, f32[768,1024]{1,0:T(8,128)}, f32[4,4,128,1024]{3,2,1,0:T(8,128)}, f32[4,4,128,1024]{3,2,1,0:T(8,128)}) custom-call(bf16[768,1024]{1,0:T(8,128)(2,1)} %get-tuple-element.120.k_ref, bf16[768,1024]{1,0:T(8,128)(2,1)} %get-tuple-element.121.v_ref, ...), custom_call_target="tpu_custom_call", output_to_operand_aliasing={{2}: (16, {}), {3}: (17, {})} | custom-call | flops 14495514624 | bytes 14155776 | tf_op jit(solution)/shard_map/finish/pallas_call | solution.py:749
  344.0 6.2 %add_reduce_fusion.1 = (f32[1024]{0:T(1024)S(1)}, f32[1024]{0:T(1024)S(1)}, f32[768]{0:T(1024)S(1)}, f32[768]{0:T(1024)S(1)}, f32[768,1024]{0,1:T(8,128)}, /*index=5*/f32[1024]{0:T(1024)S(1)}, f32[1024]{0:T(1024)S(1)}) fusion(f32[768,1024]{0,1:T(8,128)} %copy.140, f32[768,1024]{0,1:T(8,128)} %copy.141, f32[768]{0:T(1024)S(1)} %copy-done.23, ...), kind=kLoop, calls=%fused_computation.149 | loop fusion | flops 13363712 | bytes 14192644 | tf_op jit(solution)/shard_map/reduce_sum | solution.py:954
  350.2 7.1 %collective-permute-done.13.refs_5_.refs_6_ = bf16[2,2,128,1024]{3,2,1,0:T(8,128)(2,1)S(1)} collective-permute-done((bf16[2,2,128,1024]{3,2,1,0:T(8,128)(2,1)}, bf16[2,2,128,1024]{3,2,1,0:T(8,128)(2,1)S(1)}, u32[]{:S(2)}, u32[]{:S(2)}) %collective-permute-start.13) | collective-permute-done | bytes 1048608 | tf_op jit(solution)/shard_map/ppermute | solution.py:780
  367.5 5.7 convert_reduce_fusion
  373.3 5.7 collective-permute-done.14.refs_6_.refs_3_
  379.0 13.6 %collective-permute-done.15.refs_7_ = bf16[2,128,1024]{2,1,0:T(8,128)(2,1)} collective-permute-done((bf16[2,128,1024]{2,1,0:T(8,128)(2,1)}, bf16[2,128,1024]{2,1,0:T(8,128)(2,1)}, u32[]{:S(2)}, u32[]{:S(2)}) %collective-permute-start.15) | collective-permute-done | bytes 524320 | tf_op jit(solution)/shard_map/ppermute | solution.py:780
  392.6 5.6 collective-permute-done.11.refs_5_.refs_6_
  405.8 8.5 %collective-permute-done.16.refs_3_ = bf16[2,128,1024]{2,1,0:T(8,128)(2,1)S(1)} collective-permute-done((bf16[2,128,1024]{2,1,0:T(8,128)(2,1)}, bf16[2,128,1024]{2,1,0:T(8,128)(2,1)S(1)}, u32[]{:S(2)}, u32[]{:S(2)}) %collective-permute-start.16) | collective-permute-done | bytes 524320 | tf_op jit(solution)/shard_map/ppermute | solution.py:780
  441.0 9.3 %lamb_feed.2 = (f32[2,8,256]{2,1,0:T(8,128)}, f32[2,8,1024]{2,1,0:T(8,128)}, f32[128,4096]{1,0:T(8,128)}, f32[128,4096]{1,0:T(8,128)}, f32[128,4096]{1,0:T(8,128...) custom-call(f32[128,4096]{1,0:T(8,128)} %refs_4_.1, f32[128,4096]{1,0:T(8,128)} %em_ref.3, ...), custom_call_target="tpu_custom_call" | custom-call | tf_op jit(solution)/shard_map/lamb_feed/pallas_call | solution.py:978
  463.7 37.6 %collective-permute-done.21 = bf16[6,32,1024]{2,1,0:T(8,128)(2,1)S(1)} collective-permute-done((bf16[6,32,1024]{2,1,0:T(8,128)(2,1)S(1)}, bf16[6,32,1024]{2,1,0:T(8,128)(2,1)S(1)}, u32[]{:S(2)}, u32[]{:S(2)}) %collective-permute-start.21) | collective-permute-done | bytes 393248 | tf_op jit(solution)/shard_map/ppermute | solution.py:900
  501.3 10.9 %collective-permute-done.22 = bf16[6,32,1024]{2,1,0:T(8,128)(2,1)S(1)} collective-permute-done((bf16[6,32,1024]{2,1,0:T(8,128)(2,1)S(1)}, bf16[6,32,1024]{2,1,0:T(8,128)(2,1)S(1)}, u32[]{:S(2)}, u32[]{:S(2)}) %collective-permute-start.22) | collective-permute-done | bytes 393248 | tf_op jit(solution)/shard_map/ppermute | solution.py:900
  513.4 8.8 %lamb_attend.1 = (f32[2,8,1024]{2,1,0:T(8,128)}, f32[2,8,1024]{2,1,0:T(8,128)}, f32[128,3072]{1,0:T(8,128)}, f32[128,3072]{1,0:T(8,128)}, f32[128,3072]{1,0:T(8,...) custom-call(f32[128,3072]{1,0:T(8,128)} %refs_0_.1, f32[128,3072]{1,0:T(8,128)} %am_ref.1, ...), custom_call_target="tpu_custom_call" | custom-call | tf_op jit(solution)/shard_map/lamb_attend/pallas_call | solution.py:1004
  524.1 6.0 %all-reduce.7.cloned.1.call-done.eg_ref = bf16[4,128,1024]{2,1,0:T(8,128)(2,1)} async-done(((bf16[4,128,1024]{2,1,0:T(8,128)(2,1)}), bf16[4,128,1024]{2,1,0:T(8,128)(2,1)}) %all-reduce.7.cloned.1.call-update) | async-done | bytes 1048592 | tf_op jit(solution)/shard_map/psum | solution.py:928
  530.1 9.3 %lamb_feed.3 = (f32[2,8,256]{2,1,0:T(8,128)}, f32[2,8,1024]{2,1,0:T(8,128)}, f32[128,4096]{1,0:T(8,128)}, f32[128,4096]{1,0:T(8,128)}, f32[128,4096]{1,0:T(8,128...) custom-call(f32[128,4096]{1,0:T(8,128)} %refs_4_.1, ...), custom_call_target="tpu_custom_call", output_to_operand_aliasing={{2}: (8, {}), {3}: (9, {}), {4}: (10, {}), {5}: (11, {}), {... | custom-call | tf_op jit(solution)/shard_map/lamb_feed/pallas_call | solution.py:978
  544.2 13.8 %psum.23.squares_ref = f32[10]{0:T(128)S(1)} all-reduce(f32[10]{0:T(128)S(1)} %concatenate.93), channel_id=1, replica_groups=mesh['seq'=8,'dp'=4] {'seq'}, use_global_device_ids=true, to_apply=%region_33.34 | all-reduce | flops 10 | bytes 80 | tf_op jit(solution)/shard_map/psum | solution.py:1031
  560.8 7.4 %renew.1 = (f32[128,3072]{1,0:T(8,128)}, f32[128,1024]{1,0:T(8,128)}, f32[128,4096]{1,0:T(8,128)}, f32[512,1024]{1,0:T(8,128)}) custom-call(f32[10]{0:T(128)} %copy-done.36, f32[128,3072]{1,0:T(8,128)} %refs_0_.1, f32[128,3072]{1,0:T(8,128)} %get-tuple-element.166.refs_1_, f32[128,1024]{1,0:T(8,128)} %refs_2_.1, f32[128,1024]{1,0:T(8,128)} %get-tuple-element.167.refs_3_, ...), custom_call_target="tpu_custom_call" | custom-call | tf_op jit(solution)/shard_map/renew/pallas_call | solution.py:1032
  (296 shorter events, 160.3 us)
Async XLA Ops:
  7.2 51.6 %all-gather.10.cloned.1.call-start = ((), (), s32[]{:S(2)}) async-start(), calls=%async_computation.4 | async-start | bytes 7077888 | tf_op jit(solution)/shard_map/all_gather | solution.py:526
  9.8 122.5 %all-gather.14.cloned.1.call-start = ((), (), s32[]{:S(2)}) async-start(), calls=%async_computation.6 | async-start | bytes 9437184 | tf_op jit(solution)/shard_map/all_gather | solution.py:526
  13.4 154.7 %all-gather.12.cloned.1.call-start = ((), (), s32[]{:S(2)}) async-start(), calls=%async_computation.5 | async-start | bytes 2359296 | tf_op jit(solution)/shard_map/all_gather | solution.py:526
  14.2 221.4 %all-gather.16.cloned.1.call-start = ((), (), s32[]{:S(2)}) async-start(), calls=%async_computation.7 | async-start | bytes 9437184 | tf_op jit(solution)/shard_map/all_gather | solution.py:526
  15.4 320.0 %reduce-scatter.2.cloned.1.call-start = ((), (), s32[]{:S(2)}) async-start(), calls=%async_computation.1 | async-start | bytes 9437184 | tf_op jit(solution)/shard_map/reduce_scatter | solution.py:912
  73.1 27.6 %collective-permute-start.3 = (f32[72,1024]{1,0:T(8,128)}, f32[72,1024]{1,0:T(8,128)S(1)}, u32[]{:S(2)}, u32[]{:S(2)}) collective-permute-start(f32[72,1024]{1,0:T(8,128)} %get-tuple-element.118.done_ref), channel_id=1, source_target_pairs={{0,16},{4,20},{8,24},{12,28},{1,17},{5,21},{9,25},{13,29},{2,18},{... | collective-permute-start | bytes 884744 | tf_op jit(solution)/shard_map/ppermute | solution.py:693
  230.1 43.6 %collective-permute-start.7 = (f32[72,1024]{1,0:T(8,128)}, f32[72,1024]{1,0:T(8,128)S(1)}, u32[]{:S(2)}, u32[]{:S(2)}) collective-permute-start(f32[72,1024]{1,0:T(8,128)} %get-tuple-element.127.done_ref), channel_id=1, source_target_pairs={{16,0},{20,4},{24,8},{28,12},{17,1},{21,5},{25,9},{29,13},{18,2},{... | collective-permute-start | bytes 884744 | tf_op jit(solution)/shard_map/ppermute | solution.py:744
  231.4 42.3 %collective-permute-start.6 = (f32[72,1024]{1,0:T(8,128)}, f32[72,1024]{1,0:T(8,128)S(1)}, u32[]{:S(2)}, u32[]{:S(2)}) collective-permute-start(f32[72,1024]{1,0:T(8,128)} %get-tuple-element.127.done_ref), channel_id=1, source_target_pairs={{12,0},{16,4},{20,8},{24,12},{28,16},{13,1},{17,5},{21,9},{25,13},... | collective-permute-start | bytes 884744 | tf_op jit(solution)/shard_map/ppermute | solution.py:744
  232.7 41.0 %collective-permute-start.5 = (f32[72,1024]{1,0:T(8,128)}, f32[72,1024]{1,0:T(8,128)S(1)}, u32[]{:S(2)}, u32[]{:S(2)}) collective-permute-start(f32[72,1024]{1,0:T(8,128)} %get-tuple-element.127.done_ref), channel_id=1, source_target_pairs={{8,0},{12,4},{16,8},{20,12},{24,16},{28,20},{9,1},{13,5},{17,9},{2... | collective-permute-start | bytes 884744 | tf_op jit(solution)/shard_map/ppermute | solution.py:744
  234.0 39.7 %collective-permute-start.4 = (f32[72,1024]{1,0:T(8,128)}, f32[72,1024]{1,0:T(8,128)S(1)}, u32[]{:S(2)}, u32[]{:S(2)}) collective-permute-start(f32[72,1024]{1,0:T(8,128)} %get-tuple-element.127.done_ref), channel_id=1, source_target_pairs={{4,0},{8,4},{12,8},{16,12},{20,16},{24,20},{28,24},{5,1},{9,5},{13... | collective-permute-start | bytes 884744 | tf_op jit(solution)/shard_map/ppermute | solution.py:744
  298.9 36.4 %collective-permute-start.8 = (f32[2,2,4,128,1024]{4,3,2,1,0:T(8,128)}, f32[2,2,4,128,1024]{4,3,2,1,0:T(8,128)}, u32[]{:S(2)}, u32[]{:S(2)}) collective-permute-start(f32[2,2,4,128,1024]{4,3,2,1,0:T(8,128)} %bitcast.201), channel_id=1, source_target_pairs={{0,4},{4,0},{8,12},{12,8},{16,20},{20,16},{24,28},{28,24},{1,5},{5... | collective-permute-start | bytes 25165832 | tf_op jit(solution)/shard_map/ppermute | solution.py:780
  300.1 25.3 %collective-permute-start.9 = (bf16[2,2,4,128,1024]{4,3,2,1,0:T(8,128)(2,1)}, bf16[2,2,4,128,1024]{4,3,2,1,0:T(8,128)(2,1)}, u32[]{:S(2)}, u32[]{:S(2)}) collective-permute-start(bf16[2,2,4,128,1024]{4,3,2,1,0:T(8,128)(2,1)} %bitcast.25), channel_id=1, source_target_pairs={{0,4},{4,0},{8,12},{12,8},{16,20},{20,16},{24,28},{28,24},{1,5},{5... | collective-permute-start | bytes 12582920 | tf_op jit(solution)/shard_map/ppermute | solution.py:780
  329.4 27.9 %collective-permute-start.13 = (bf16[2,2,128,1024]{3,2,1,0:T(8,128)(2,1)}, bf16[2,2,128,1024]{3,2,1,0:T(8,128)(2,1)S(1)}, u32[]{:S(2)}, u32[]{:S(2)}) collective-permute-start(bf16[2,2,128,1024]{3,2,1,0:T(8,128)(2,1)} %get-tuple-element.148), channel_id=1, source_target_pairs={{0,16},{4,20},{8,24},{12,28},{16,0},{20,4},{24,8},{28,12},{1,17},{... | collective-permute-start | bytes 3145736 | tf_op jit(solution)/shard_map/ppermute | solution.py:780
  333.8 26.4 %collective-permute-start.12 = (bf16[2,2,128,1024]{3,2,1,0:T(8,128)(2,1)}, bf16[2,2,128,1024]{3,2,1,0:T(8,128)(2,1)}, u32[]{:S(2)}, u32[]{:S(2)}) collective-permute-start(bf16[2,2,128,1024]{3,2,1,0:T(8,128)(2,1)} %get-tuple-element.142.refs_4_), channel_id=1, source_target_pairs={{0,8},{4,12},{8,0},{12,4},{16,24},{20,28},{24,16},{28,20},{1,9},{5... | collective-permute-start | bytes 3145736 | tf_op jit(solution)/shard_map/ppermute | solution.py:780
  341.0 100.0 %all-reduce.5.cloned.1.call-start = ((), (), s32[]{:S(2)}) async-start(), calls=%async_computation.2 | async-start | bytes 2097152 | tf_op jit(solution)/shard_map/psum | solution.py:913
  341.5 188.6 %all-reduce.7.cloned.1.call-start = ((), (), s32[]{:S(2)}) async-start(), calls=%async_computation.3 | async-start | bytes 2097152 | tf_op jit(solution)/shard_map/psum | solution.py:928
  342.8 55.4 %collective-permute-start.10 = (bf16[2,2,128,1024]{3,2,1,0:T(8,128)(2,1)}, bf16[2,2,128,1024]{3,2,1,0:T(8,128)(2,1)}, u32[]{:S(2)}, u32[]{:S(2)}) collective-permute-start(bf16[2,2,128,1024]{3,2,1,0:T(8,128)(2,1)} %get-tuple-element.144.refs_6_), channel_id=1, source_target_pairs={{0,8},{4,12},{8,0},{12,4},{16,24},{20,28},{24,16},{28,20},{1,9},{5... | collective-permute-start | bytes 3145736 | tf_op jit(solution)/shard_map/ppermute | solution.py:780
  363.9 28.8 %collective-permute-start.15 = (bf16[2,128,1024]{2,1,0:T(8,128)(2,1)}, bf16[2,128,1024]{2,1,0:T(8,128)(2,1)}, u32[]{:S(2)}, u32[]{:S(2)}) collective-permute-start(bf16[2,128,1024]{2,1,0:T(8,128)(2,1)} %get-tuple-element.150), channel_id=1, source_target_pairs={{0,8},{4,12},{8,0},{12,4},{16,24},{20,28},{24,16},{28,20},{1,9},{5... | collective-permute-start | bytes 1572872 | tf_op jit(solution)/shard_map/ppermute | solution.py:780
  365.5 32.7 %collective-permute-start.11 = (bf16[2,2,128,1024]{3,2,1,0:T(8,128)(2,1)}, bf16[2,2,128,1024]{3,2,1,0:T(8,128)(2,1)}, u32[]{:S(2)}, u32[]{:S(2)}) collective-permute-start(bf16[2,2,128,1024]{3,2,1,0:T(8,128)(2,1)} %get-tuple-element.147), channel_id=1, source_target_pairs={{0,16},{4,20},{8,24},{12,28},{16,0},{20,4},{24,8},{28,12},{1,17},{... | collective-permute-start | bytes 3145736 | tf_op jit(solution)/shard_map/ppermute | solution.py:780
  429.2 27.4 %collective-permute-start.18 = (bf16[4,32,1024]{2,1,0:T(8,128)(2,1)}, bf16[4,32,1024]{2,1,0:T(8,128)(2,1)S(1)}, u32[]{:S(2)}, u32[]{:S(2)}) collective-permute-start(bf16[4,32,1024]{2,1,0:T(8,128)(2,1)} %get-tuple-element.284), channel_id=1, source_target_pairs={{0,1},{1,2},{2,3},{3,0},{4,5},{5,6},{6,7},{7,4},{8,9},{9,10},{10,1... | collective-permute-start | bytes 786440 | tf_op jit(solution)/shard_map/ppermute | solution.py:894
  430.6 26.0 %collective-permute-start.19 = (bf16[4,32,1024]{2,1,0:T(8,128)(2,1)}, bf16[4,32,1024]{2,1,0:T(8,128)(2,1)}, u32[]{:S(2)}, u32[]{:S(2)}) collective-permute-start(bf16[4,32,1024]{2,1,0:T(8,128)(2,1)} %get-tuple-element.285), channel_id=1, source_target_pairs={{0,2},{1,3},{2,0},{3,1},{4,6},{5,7},{6,4},{7,5},{8,10},{9,11},{10,... | collective-permute-start | bytes 786440 | tf_op jit(solution)/shard_map/ppermute | solution.py:894
  458.1 54.1 %collective-permute-start.23 = (bf16[6,32,1024]{2,1,0:T(8,128)(2,1)S(1)}, bf16[6,32,1024]{2,1,0:T(8,128)(2,1)S(1)}, u32[]{:S(2)}, u32[]{:S(2)}) collective-permute-start(bf16[6,32,1024]{2,1,0:T(8,128)(2,1)S(1)} %pad_maximum_fusion.4), channel_id=1, source_target_pairs={{0,3},{1,0},{2,1},{3,2},{4,7},{5,4},{6,5},{7,6},{8,11},{9,8},{10,9... | collective-permute-start | bytes 1179656 | tf_op jit(solution)/shard_map/ppermute | solution.py:900
  461.4 50.7 %collective-permute-start.22 = (bf16[6,32,1024]{2,1,0:T(8,128)(2,1)S(1)}, bf16[6,32,1024]{2,1,0:T(8,128)(2,1)S(1)}, u32[]{:S(2)}, u32[]{:S(2)}) collective-permute-start(bf16[6,32,1024]{2,1,0:T(8,128)(2,1)S(1)} %pad_maximum_fusion.4), channel_id=1, source_target_pairs={{0,2},{1,3},{2,0},{3,1},{4,6},{5,7},{6,4},{7,5},{8,10},{9,11},{10,... | collective-permute-start | bytes 1179656 | tf_op jit(solution)/shard_map/ppermute | solution.py:900
  461.4 39.8 %collective-permute-start.21 = (bf16[6,32,1024]{2,1,0:T(8,128)(2,1)S(1)}, bf16[6,32,1024]{2,1,0:T(8,128)(2,1)S(1)}, u32[]{:S(2)}, u32[]{:S(2)}) collective-permute-start(bf16[6,32,1024]{2,1,0:T(8,128)(2,1)S(1)} %pad_maximum_fusion.4), channel_id=1, source_target_pairs={{0,1},{1,2},{2,3},{3,0},{4,5},{5,6},{6,7},{7,4},{8,9},{9,10},{10,1... | collective-permute-start | bytes 1179656 | tf_op jit(solution)/shard_map/ppermute | solution.py:900
  (53 other events, 670.9 us)
Sparse Core Ops, SparseCore 0:
  10.5 48.2 all-gather.9
  61.3 70.9 all-gather.13
  134.7 27.8 all-gather.11
  164.4 54.3 all-gather.15
  235.7 75.8 reduce-scatter.1
  344.0 50.6 all-reduce.4
  456.2 73.9 all-reduce.6

commit v3 on v2

--- a/solution.py
+++ b/solution.py
@@ -1,3 +1,4 @@
+import functools
 import math
 
 import jax
@@ -134,8 +135,12 @@
     return project - (SCALE * SCALE) * value * total
 
 
-def spread(state_ref, const_ref):
-    packed = state_ref[0:HEAD, :]
+def arrive(state_refs, weigh_ref):
+    return sum(ref[...] * weigh_ref[i] for i, ref in enumerate(state_refs))
+
+
+def spread(state, const_ref):
+    packed = state[0:HEAD, :]
     tall = jnp.concatenate([packed] * EACH, axis=0)
     return tall * const_ref[2].astype(f32)
 
@@ -176,15 +181,19 @@
     q_ref[...] = phi(query, const_ref, weight_ref).astype(bf16)
 
 
-def attend_kernel(
-    q_ref, k_ref, v_ref, vl_ref, uq_ref, s_ref, g_ref, wm_ref, table_ref, row_ref, marks_ref, const_ref, core_ref, done_ref,
-    mixed_ref, dq_ref, dk_ref, dv_ref, ds_ref, bias_ref, out_ref, send_ref, keep_ref,
-    dnum_ref, dlow_ref, dden_ref,
-):
+def attend_kernel(far, *refs):
+    state_refs, refs = refs[:far], refs[far:]
+    (
+        q_ref, k_ref, v_ref, vl_ref, uq_ref, weigh_ref, g_ref, wm_ref, table_ref, row_ref,
+        marks_ref, const_ref, core_ref,
+        dq_ref, dk_ref, dv_ref, ds_ref, bias_ref, out_ref, send_ref, keep_ref,
+        mixed_ref, dnum_ref, dlow_ref, dden_ref,
+    ) = refs
+    came = arrive(state_refs, weigh_ref)
     count = q_ref.shape[0] // CHUNK
     merge = flat(wm_ref[...])
-    state = spread(s_ref, const_ref)
-    total = s_ref[HEAD : HEAD + 1, :]
+    state = spread(came, const_ref)
+    total = came[HEAD : HEAD + 1, :]
     blocks = const_ref[2].astype(f32)
     masks = [head_mask(index, bf16) for index in range(EACH)]
     lower = lax.broadcasted_iota(jnp.int32, (CHUNK, CHUNK), 0) >= lax.broadcasted_iota(
@@ -302,17 +311,20 @@
     keep_ref[...], send_ref[...] = keep, send
 
 
-def finish_kernel(
-    k_ref, v_ref, vl_ref, uk_ref, dq_ref, dk_ref, dv_ref, ds_ref, table_ref, marks_ref, const_ref,
-    wq_ref, wk_ref, wv_ref, ht_ref, core_ref, sent_ref, kept_ref, done_ref,
-    bias_ref, dh_ref, send_ref, keep_ref,
-):
+def finish_kernel(far, *refs):
+    state_refs, refs = refs[:far], refs[far:]
+    (
+        k_ref, v_ref, vl_ref, uk_ref, dq_ref, dk_ref, dv_ref, weigh_ref, table_ref, marks_ref,
+        const_ref, wq_ref, wk_ref, wv_ref, ht_ref, core_ref, _, _, _,
+        bias_ref, dh_ref, send_ref, keep_ref,
+    ) = refs
+    came = arrive(state_refs, weigh_ref)
     segment = twice(table_ref[3])
     tail = jnp.where(segment == marks_ref[15:16, :], 1.0, 0.0)
-    high, low = halves(spread(ds_ref, const_ref))
+    high, low = halves(spread(came, const_ref))
     key, value = k_ref[...], v_ref[...]
     grad_key = dk_ref[...] + tail * (
-        dot_three(dot_nt, value, vl_ref[...], high, low) + ds_ref[HEAD : HEAD + 1, :]
+        dot_three(dot_nt, value, vl_ref[...], high, low) + came[HEAD : HEAD + 1, :]
     )
     grad_value = dv_ref[...] + tail * (dot_nn(key, high) + dot_nn(key, low))
     grad = phi_back(grad_key, key.astype(f32), uk_ref[...].astype(f32), const_ref)
@@ -404,6 +416,24 @@
     gradients(1, *right)
     accumulate(out_ref, forward + dot_nn(right[0], shrink[half:]))
     accumulate(dh_ref, backward + dot_nt(right[1], expand[:, half:]))
+
+
+def close_kernel(x_ref, g_ref, one_ref, mixed_ref, *refs):
+    feeds, (lines_ref, _, out_ref, grad_ref, sums_ref) = refs[:-5], refs[-5:]
+    half = len(feeds) // 2
+    inputs = x_ref[...].astype(f32)
+    result = inputs + mixed_ref[...] + lines_ref[2:3, :]
+    out_ref[...] = (result + sum(ref[...] for ref in feeds[:half])).astype(bf16)
+    normed, root = layer_parts(inputs)
+    one, two = one_ref[...], sum(ref[...] for ref in feeds[half:])
+    pulled = one * lines_ref[0:1, :] + two * lines_ref[1:2, :]
+    drop = jnp.mean(pulled, -1, keepdims=True)
+    lean = jnp.mean(pulled * normed, -1, keepdims=True)
+    outer = g_ref[...].astype(f32)
+    grad_ref[...] = (outer + root * (pulled - drop - normed * lean)).astype(bf16)
+    values = (one * normed, one, two * normed, two, outer)
+    rows = [jnp.sum(value, 0, keepdims=True) for value in values]
+    accumulate(sums_ref, jnp.concatenate(rows + [jnp.zeros((3, D), f32)], 0))
 
 
 def lamb_step(master, first, second, grad, mean_ref, square_ref, update_ref, norms_ref):
@@ -684,22 +714,21 @@
         name="queries",
     )(low_one, attend, biases, table, const, weighting, summary)
 
-    fed = [feed(0, query, False)]
-
     reaches = range(1, n // 2 + 1)
     own_before, own_final = label(device * rows - 1), segment[-1]
-    carried = jnp.zeros_like(summary)
+    carried, weights = [], []
     for far in reaches:
-        came = lax.ppermute(summary, "seq", [(e, e + far) for e in range(n - far)])
+        carried.append(lax.ppermute(summary, "seq", [(e, e + far) for e in range(n - far)]))
         same = (device >= far) & (label((device - far + 1) * rows - 1) == own_before)
-        carried = carried + jnp.where(same, came, 0.0)
-
-    _, grad_query, part_key, part_value, grad_carried, query_bias, attend_out, send, keep = pl.pallas_call(
-        attend_kernel,
+        weights.append(same.astype(f32))
+
+    grad_query, part_key, part_value, grad_carried, query_bias, attend_out, send, keep = pl.pallas_call(
+        functools.partial(attend_kernel, len(carried)),
         grid=(NGROUP,),
         in_specs=[
+            *[columns(STATE)] * len(carried),
             *[columns(rows)] * 5,
-            columns(STATE),
+            scalar(),
             whole((rows, D)),
             pl.BlockSpec((LANES // own, 1, own, D), lambda g: (g, 0, 0, 0)),
             whole((4, rows, 2 * HEAD)),
@@ -707,13 +736,11 @@
             whole((16, LANES)),
             whole((3, LANES, LANES)),
             scalar(),
-            pl.BlockSpec(memory_space=pl.ANY),
         ],
-        out_specs=[columns(rows)] * 4
+        out_specs=[columns(rows)] * 3
         + [columns(STATE), columns(8), total_of((rows, D))]
         + [pl.BlockSpec((LANES // own // 2, 1, own, D), lambda g: (g, 3, 0, 0))] * 2,
         out_shape=[
-            shaped((rows, D), bf16),
             shaped((rows, D), bf16),
             shaped((rows, D), f32),
             shaped((rows, D), f32),
@@ -723,7 +750,7 @@
             shaped((n // 2, 4, own, D), f32),
             shaped((n // 2, 4, own, D), f32),
         ],
-        scratch_shapes=[pltpu.VMEM((rows, LANES), kind) for kind in (bf16, bf16, f32)],
+        scratch_shapes=[pltpu.VMEM((rows, LANES), kind) for kind in (bf16, bf16, bf16, f32)],
         compiler_params=params(),
         cost_estimate=pl.CostEstimate(
             flops=2 * rows * D * D + 150 * rows * D * LANES,
@@ -732,25 +759,24 @@
         ),
         name="attend",
     )(
-        query, key, value, value_low, turned_query, carried,
-        grad_out, merge, table, row_table, marks, const, core_ref, fed[0][2],
-    )
-
-    for index in range(1, parts):
-        fed.append(feed(index, grad_carried, True))
-
-    returned = jnp.zeros_like(summary)
+        *carried, query, key, value, value_low, turned_query, jnp.stack(weights),
+        grad_out, merge, table, row_table, marks, const, core_ref,
+    )
+
+    returned, weights = [], []
     for far in reaches:
-        came = lax.ppermute(grad_carried, "seq", [(e + far, e) for e in range(n - far)])
+        returned.append(lax.ppermute(grad_carried, "seq", [(e + far, e) for e in range(n - far)]))
         same = (device + far < n) & (label((device + far) * rows - 1) == own_final)
-        returned = returned + jnp.where(same, came, 0.0)
+        weights.append(same.astype(f32))
+    fed = [feed(0, grad_carried, False)]
 
     sides = pl.BlockSpec((n // 2, 3, own, LANES), lambda g: (0, 0, 0, g))
     rest_bias, grad_one, send, keep = pl.pallas_call(
-        finish_kernel,
+        functools.partial(finish_kernel, len(returned)),
         grid=(NGROUP,),
-        in_specs=[columns(rows)] * 7
-        + [columns(STATE), *tables, whole((3, LANES, LANES))]
+        in_specs=[columns(STATE)] * len(returned)
+        + [columns(rows)] * 7
+        + [scalar(), *tables, whole((3, LANES, LANES))]
         + [projection(index) for index in range(3)]
         + [whole((D, rows)), scalar()]
         + [pl.BlockSpec(memory_space=pl.ANY)] * 3,
@@ -761,7 +787,7 @@
             shaped((n // 2, 4, own, D), f32),
             shaped((n // 2, 4, own, D), f32),
         ],
-        input_output_aliases={16: 2, 17: 3},
+        input_output_aliases={16 + len(returned): 2, 17 + len(returned): 3},
         compiler_params=params(),
         cost_estimate=pl.CostEstimate(
             flops=12 * rows * D * D + 24 * rows * D * LANES,
@@ -770,9 +796,11 @@
         ),
         name="finish",
     )(
-        key, value, value_low, turned_key, grad_query, part_key, part_value, returned,
-        table, marks, const, attend, attend, attend, flipped_one, core_ref, send, keep, fed[-1][2],
-    )
+        *returned, key, value, value_low, turned_key, grad_query, part_key, part_value,
+        jnp.stack(weights), table, marks, const, attend, attend, attend, flipped_one, core_ref, send, keep, fed[0][2],
+    )
+    for index in range(1, parts):
+        fed.append(feed(index, rest_bias, True))
 
     bits = n.bit_length() - 1
 
@@ -881,7 +909,7 @@
     groups = lax.axis_size("dp")
     group = lax.axis_index("dp")
 
-    def sum_groups(value, fine):
+    def sum_groups(value, fine, begun):
         blocks = value.shape[0]
         shares = value.reshape(blocks, groups, own // groups, D)
         rolls = {far: [(i, (i + far) % groups) for i in range(groups)] for far in range(1, groups)}
@@ -892,6 +920,7 @@
         total = share(group)
         for far, pairs in rolls.items():
             total = total + lax.ppermute(share(group + far).astype(bf16), "dp", pairs).astype(f32)
+        total = total + begun
         high = lax.reduce_precision(total, 8, 7)
         total = jnp.concatenate([high, (total - high)[:fine]], 0).astype(bf16)
         result = jnp.zeros((blocks + fine,) + shares.shape[1:], bf16)
@@ -899,7 +928,7 @@
         for far, pairs in rolls.items():
             came = lax.ppermute(total, "dp", pairs)
             result = lax.dynamic_update_index_in_dim(result, came, (group - far) % groups, 1)
-        return result.reshape(blocks + fine, own, D)
+        return result.reshape(blocks + fine, own, D), total
 
     def sum_all(value):
         for bit in range(bits):
@@ -917,50 +946,49 @@
         feed_came = exchange(feed_send, 0)
         send, keep = send.reshape(deep), keep.reshape(deep)
         came = exchange(send, 0)
-        begun, *feed_first = step_one(feed_keep, feed_came, [rest_bias])
-        started, *first = step_one(keep, came, [begun, first_part])
-        feed_second = step_two(feed_keep, feed_came, *feed_first, [started])
-        second = step_two(keep, came, *first, feed_second)
-        attend_part = step_three(keep, came, *first, *second, f32, [])
+        started, *first = step_one(keep, came, [fed[1][2], first_part])
+        arrived = first[0]
+        begun, *feed_first = step_one(feed_keep, feed_came, [started])
+        second = step_two(keep, came, *first, [begun])
+        feed_second = step_two(feed_keep, feed_came, *feed_first, [])
+        attend_part = step_three(
+            keep, came, *first, *second, f32, [*feed_second, feed_sums[0]]
+        )
         feed_part = step_three(
-            feed_keep, feed_came, *feed_first, *feed_second, bf16, [attend_part, feed_sums[0]]
+            feed_keep, feed_came, *feed_first, *feed_second, bf16, [attend_part]
         )
         feed_sums.append(lax.psum(feed_part, "dp"))
-        grad_one = grad_one + 0.0 * started[0, 0, 0, 0].astype(f32)
+        feed_sums_begun = 0.0 * feed_part[0, 0, 0].astype(f32)
     else:
         for index in range(1, parts):
             part = scatter(fed[index][4], exchange(fed[index][3], 0))
             feed_sums.append(lax.psum(part.astype(bf16), "dp"))
         attend_part = scatter(keep, exchange(send, 0))
-    attend_sum = sum_groups(attend_part, 2)
-
-    grad_float = grad_out.astype(f32)
-    result = inputs + attend_out + bias_merge + bias_shrink + sum(f[0] for f in fed)
-    block_output = result.astype(bf16)[None]
-    grad_two = sum(f[1] for f in fed)
-    grad_bias_out = jnp.sum(grad_float, 0)
-    pulled = grad_one * gain_one + grad_two * gain_two
-    drop = jnp.mean(pulled, -1, keepdims=True)
-    lean = jnp.mean(pulled * normed, -1, keepdims=True)
-    input_grad = (grad_float + root * (pulled - drop - normed * lean)).astype(bf16)[None]
+        feed_sums_begun, arrived = 0.0, attend_part
+    attend_sum, attend_share = sum_groups(attend_part, 2, feed_sums_begun)
+
+    strip = pl.BlockSpec((128, D), lambda g: (g, 0))
+    lines = jnp.stack([gain_one, gain_two, bias_merge + bias_shrink] + [gain_one] * 5)
+    block_output, input_grad, sums = pl.pallas_call(
+        close_kernel,
+        grid=(rows // 128,),
+        in_specs=[strip] * (4 + 2 * parts) + [whole((8, D)), pl.BlockSpec(memory_space=pl.ANY)],
+        out_specs=[strip, strip, total_of((8, D))],
+        out_shape=[shaped((rows, D), bf16), shaped((rows, D), bf16), shaped((8, D), f32)],
+        compiler_params=params(),
+        name="close",
+    )(
+        tokens[0], grad_out, grad_one, attend_out, *[f[0] for f in fed], *[f[1] for f in fed],
+        lines, arrived,
+    )
+    block_output, input_grad = block_output[None], input_grad[None]
     feed_bias = jnp.concatenate(
         [fed[p][2][0, j * sub : (j + 1) * sub] for j in range(n) for p in range(parts)]
     )
     grad_vector = jnp.concatenate(
-        [
-            jnp.sum(grad_one * normed, 0),
-            jnp.sum(grad_one, 0),
-            jnp.sum(grad_two * normed, 0),
-            jnp.sum(grad_two, 0),
-            query_bias[0],
-            rest_bias[0],
-            rest_bias[8],
-            grad_bias_out,
-            feed_bias,
-            grad_bias_out,
-        ]
-    )
-    grad_vector = grad_vector + 0.0 * attend_part[0, 0, 0].astype(f32)
+        [sums[0:4].reshape(-1), query_bias[0], rest_bias[0], rest_bias[8], sums[4], feed_bias, sums[4]]
+    )
+    grad_vector = grad_vector + 0.0 * attend_sum[0, 0, 0].astype(f32)
     vector_sum = sum_all(grad_vector.reshape(-1, 128)).reshape(-1)
     share = gains_biases.shape[0]
     own_vector = lax.dynamic_slice(vector_sum, (device * share,), (share,))
@@ -982,7 +1010,7 @@
             + [pl.BlockSpec((1, own, wide_cols), lambda g: (g // per, 0, g % per))]
             + [of_shrink] * 3
             + [pl.BlockSpec((sub // strips, D), lambda g: (strips + g, 0))]
-            + before_specs,
+            + (before_specs or [pl.BlockSpec(memory_space=pl.ANY)]),
             out_specs=[total_of((2, 8, wide_cols)), total_of((2, 8, D))]
             + [of_expand] * 3
             + [of_shrink] * 3,
@@ -995,7 +1023,7 @@
         )(
             expand_weight, expand_first, expand_second, feed_sums[index],
             shrink_weight, shrink_first, shrink_second, flat(feed_sums[index]),
-            *([] if held is None else held),
+            *([attend_share] if held is None else held),
         )
         expand_sums.append(jnp.sum(expand_norm, (1, 2)))
         shrink_sums.append(jnp.sum(shrink_norm, (1, 2)))

time: 583 us -> 561 us (0.962)
  local copies, waits for them, and re-layouts: 50.3 us -> 25.7 us
  other arithmetic: 38.2 us -> 24.6 us
  Pallas kernels: 246 us -> 257 us
  starting transfers between devices: 44.2 us -> 50.2 us
    ppermute x3, waiting for transfers between devices: 48.4 us -> 22.7 us  [sum_groups(): came = lax.ppermute(total, 'dp', pairs)]
    pallas_call x6 -> x0, local copies, waits for them, and re-layouts: 19.9 us -> none  [the longest x4 12.7 us: feed(): pl.pallas_call(feed_kernel, grid=(n // 2,), in_specs=[whole((rows, D)), w...]
    ppermute x13, waiting for transfers between devices: 49.7 us -> 33.5 us  [exchange(): return lax.ppermute(array, 'seq', [(i, i ^ 1 << bit) for i in range(n)])]
    reduce_scatter x1, waiting for transfers between devices: 0.01 us -> 13.9 us  [per_device(): lax.psum_scatter(fed[0][3], 'seq', scatter_dimension=0, tiled=False)]
    all_gather x4, waiting for transfers between devices: 34.5 us -> 20.8 us  [gather(): full = lax.all_gather(shard, 'seq', axis=0, tiled=False)]
    ppermute x4, waiting for transfers between devices: 0.01 us -> 12.2 us  [per_device(): lax.ppermute(grad_carried, 'seq', [(e + far, e) for e in range(n - far)])]
    reduce_sum x2 -> x0, other arithmetic: 11.8 us -> none  [the longest x1 6.16 us: per_device(): jnp.sum(grad_two, 0)]
    pallas_call x2 -> x3, Pallas kernels: 85.8 us -> 96.7 us  [the longest x1 61 us: per_device(): pl.pallas_call(functools.partial(attend_kernel, len(carried)), grid=(NGRO...]
  transfers between devices with their start and end apart: 36 -> 36, of which waited for: 15 -> 20; matrix products, arithmetic and copies ran while one was open for 13% -> 6% of each run, Pallas kernels for 40% -> 43%
where the time goes in v3:
time: 561 us; the launch traced here: 552 us
  Pallas kernels  257 us (46%)
  waiting for transfers between devices  144 us (26%)
  starting transfers between devices  50.2 us (9%)
  between operations  27 us (5%)
  local copies, waits for them, and re-layouts  25.7 us (5%)
  other arithmetic  24.6 us (4%)
  blocking collectives  24.5 us (4%)
    pallas_call x2, Pallas kernels, feed(): pl.pallas_call(feed_kernel, grid=(n // 2,), in_specs=[whole((rows, D)), w...  74.4 us
    pallas_call x1, Pallas kernels, per_device(): pl.pallas_call(functools.partial(attend_kernel, len(carried)), grid=(NGRO...  61 us
    ppermute x13, waiting for transfers between devices, exchange(): return lax.ppermute(array, 'seq', [(i, i ^ 1 << bit) for i in range(n)])  33.5 us
    pallas_call x6, Pallas kernels, add_step(): pl.pallas_call(kernel, grid_spec=pltpu.PrefetchScalarGridSpec(num_scalar_...  25.9 us
    pallas_call x1, Pallas kernels, per_device(): pl.pallas_call(functools.partial(finish_kernel, len(returned)), grid=(NGR...  24.5 us
    ppermute x3, waiting for transfers between devices, sum_groups(): came = lax.ppermute(total, 'dp', pairs)  22.7 us
    all_gather x4, waiting for transfers between devices, gather(): full = lax.all_gather(shard, 'seq', axis=0, tiled=False)  20.8 us
    pallas_call x2, Pallas kernels, per_device(): pl.pallas_call(lamb_feed_kernel, grid=(strips,), in_specs=[of_expand] * 3...  18.6 us
  transfers between devices with their start and end apart: 36, of which 20 were waited for; matrix products, arithmetic and copies ran while one was open for 6% of the time, Pallas kernels for 43%

profile of v3, /device:TPU:0, one launch (start us, length us, event | category | flops | bytes accessed | tf_op | source)
XLA Modules:
  0.0 552.3 jit_solution(8127391130973027347)
XLA Ops:
  15.1 10.6 %all-gather.4 = bf16[8,1,1664]{2,1,0:T(2,128)(2,1)S(1)} all-gather(bf16[1,1,1664]{2,1,0:T(2,128)(2,1)S(1)} %reshape.324), channel_id=1, replica_groups=mesh['seq'=8,'dp'=4] {'seq'}, dimensions={0}, use_global_device_ids=true | all-gather | bytes 29952 | tf_op jit(solution)/shard_map/all_gather | solution.py:575
  44.5 14.3 %all-gather.10.cloned.1.call-done = bf16[3072,1024]{1,0:T(8,128)(2,1)} async-done(((bf16[384,1024]{1,0:T(8,128)(2,1)}), bf16[3072,1024]{1,0:T(8,128)(2,1)}) %all-gather.10.cloned.1.call-update) | async-done | bytes 6291472 | tf_op jit(solution)/shard_map/all_gather | solution.py:556
  59.5 13.6 %keys.1 = (bf16[768,1024]{1,0:T(8,128)(2,1)}, bf16[768,1024]{1,0:T(8,128)(2,1)}, bf16[768,1024]{1,0:T(8,128)(2,1)}, bf16[768,1024]{1,0:T(8,128)(2,1)}, f32[72,1024]{1,0:T(8,128)}) custom-call(bf16[768,1024]{1,0:T(8,128)(2,1)} %get-tuple-element.210.h_ref, bf16[8,3,128,1024]{3,2,1,0:T(8,128)(2,1)} %bitcast.151, bf16[8,3,128,1024]{3,2,1,0:T(8,128)(2,1)} %bitcast.152, ...), custom_call_target="tpu_custom_call" | custom-call | flops 6039797760 | bytes 11010048 | tf_op jit(solution)/shard_map/keys/pallas_call | solution.py:675
  83.1 11.4 %queries.1 = (bf16[768,1024]{1,0:T(8,128)(2,1)}, bf16[768,1024]{1,0:T(8,128)(2,1)}) custom-call(bf16[768,1024]{1,0:T(8,128)(2,1)} %get-tuple-element.210.h_ref, bf16[8,3,128,1024]{3,2,1,0:T(8,128)(2,1)} %bitcast.153, f32[3,1024]{1,0:T(4,128)} %slice.295.b_ref, f32[4,768,128]{2,1,0:T(8,128)} %pad_maximum_fusion.table_ref.refs_12_, ...), custom_call_target="tpu_custom_call" | custom-call | flops 3221225472 | bytes 6291456 | tf_op jit(solution)/shard_map/queries/pallas_call | solution.py:695
  103.7 61.0 %attend.1 = (bf16[768,1024]{1,0:T(8,128)(2,1)}, f32[768,1024]{1,0:T(8,128)}, f32[768,1024]{1,0:T(8,128)}, f32[72,1024]{1,0:T(8,128)}, f32[8,1024]{1,0:T(8,128)},...) custom-call(f32[72,1024]{1,0:T(8,128)} %copy-done.40, f32[72,1024]{1,0:T(8,128)} %copy-done.41, ...), custom_call_target="tpu_custom_call" | custom-call | flops 31809601536 | bytes 18874368 | tf_op jit(solution)/shard_map/attend/pallas_call | solution.py:725
  164.7 36.3 %feed.2 = (f32[768,1024]{1,0:T(8,128)}, f32[768,1024]{1,0:T(8,128)}, f32[8,2048]{1,0:T(8,128)}, bf16[8,4,128,1024]{3,2,1,0:T(8,128)(2,1)}) custom-call(bf16[768,1024]{1,0:T(8,128)(2,1)} %copy-done.3, bf16[1024,768]{1,0:T(8,128)(2,1)} %copy.85.ht_ref, bf16[768,1024]{1,0:T(8,128)(2,1)} %bitcast.174, bf16[8,4,128,1024]{3,2,1,0:T(8,128)(2,1)} %bitcast.228, ...), custom_call_target="tpu_custom_call" | custom-call | flops 38654705664 | bytes 20971520 | tf_op jit(solution)/shard_map/feed/pallas_call | solution.py:632
  214.5 11.7 %collective-permute-done.5.refs_1_ = f32[72,1024]{1,0:T(8,128)S(1)} collective-permute-done((f32[72,1024]{1,0:T(8,128)S(1)}, f32[72,1024]{1,0:T(8,128)S(1)}, u32[]{:S(2)}, u32[]{:S(2)}) %collective-permute-start.5) | collective-permute-done | bytes 294944 | tf_op jit(solution)/shard_map/ppermute | solution.py:768
  227.5 24.5 %finish.1 = (f32[16,1024]{1,0:T(8,128)}, f32[768,1024]{1,0:T(8,128)}, f32[4,4,128,1024]{3,2,1,0:T(8,128)}, f32[4,4,128,1024]{3,2,1,0:T(8,128)}) custom-call(f32[72,1024]{1,0:T(8,128)} %copy-done.15, f32[72,1024]{1,0:T(8,128)} %copy-done.16, f32[72,1024]{1,0:T(8,128)} %copy-done.17, ...), custom_call_target="tpu_custom_call", output_to_operand_aliasing={{2}: (20, {}), {3}: (21, {})} | custom-call | flops 14495514624 | bytes 14155776 | tf_op jit(solution)/shard_map/finish/pallas_call | solution.py:774
  252.1 38.1 %feed.3 = (f32[768,1024]{1,0:T(8,128)}, f32[768,1024]{1,0:T(8,128)}, f32[8,2048]{1,0:T(8,128)}, bf16[4,4,128,1024]{3,2,1,0:T(8,128)(2,1)}, bf16[4,4,128,1024]{3,2,1,0:T(8,128)(2,1)}) custom-call(bf16[768,1024]{1,0:T(8,128)(2,1)} %copy-done.3, bf16[1024,768]{1,0:T(8,128)(2,1)} %copy.85.ht_ref, bf16[768,1024]{1,0:T(8,128)(2,1)} %bitcast.175, ...), custom_call_target="tpu_custom_call" | custom-call | flops 38654705664 | bytes 20971520 | tf_op jit(solution)/shard_map/feed/pallas_call | solution.py:632
  291.2 13.9 %reduce-scatter.2.cloned.1.call-done = bf16[1,4,128,1024]{3,2,1,0:T(8,128)(2,1)} async-done(((bf16[8,4,128,1024]{3,2,1,0:T(8,128)(2,1)}), bf16[1,4,128,1024]{3,2,1,0:T(8,128)(2,1)}) %reduce-scatter.2.cloned.1.call-update) | async-done | bytes 1048592 | tf_op jit(solution)/shard_map/reduce_scatter | solution.py:941
  323.0 14.3 %collective-permute-done.9.refs_5_.refs_2_ = bf16[2,2,128,1024]{3,2,1,0:T(8,128)(2,1)S(1)} collective-permute-done((bf16[2,2,128,1024]{3,2,1,0:T(8,128)(2,1)}, bf16[2,2,128,1024]{3,2,1,0:T(8,128)(2,1)S(1)}, u32[]{:S(2)}, u32[]{:S(2)}) %collective-permute-start.9) | collective-permute-done | bytes 1048608 | tf_op jit(solution)/shard_map/ppermute | solution.py:808
  338.3 11.2 %close.1 = (bf16[768,1024]{1,0:T(8,128)(2,1)}, bf16[768,1024]{1,0:T(8,128)(2,1)}, f32[8,1024]{1,0:T(8,128)}) custom-call(bf16[768,1024]{1,0:T(8,128)(2,1)} %bitcast.157, bf16[768,1024]{1,0:T(8,128)(2,1)} %bitcast.176, f32[768,1024]{1,0:T(8,128)} %get-tuple-element.135.one_ref, f32[768,1024]{1,0:T(8,128)} %get-tuple-element.136.mixed_ref, ...), custom_call_target="tpu_custom_call" | custom-call | tf_op jit(solution)/shard_map/close/pallas_call | solution.py:972
  366.9 8.0 %all-reduce.5.cloned.1.call-done.refs_10_.eg_ref = bf16[4,128,1024]{2,1,0:T(8,128)(2,1)} async-done(((bf16[4,128,1024]{2,1,0:T(8,128)(2,1)}), bf16[4,128,1024]{2,1,0:T(8,128)(2,1)}) %all-reduce.5.cloned.1.call-update) | async-done | bytes 1048592 | tf_op jit(solution)/shard_map/psum | solution.py:942
  374.9 7.2 %collective-permute-done.16.refs_8_.refs_3_ = bf16[2,128,1024]{2,1,0:T(8,128)(2,1)S(1)} collective-permute-done((bf16[2,128,1024]{2,1,0:T(8,128)(2,1)}, bf16[2,128,1024]{2,1,0:T(8,128)(2,1)S(1)}, u32[]{:S(2)}, u32[]{:S(2)}) %collective-permute-start.16) | collective-permute-done | bytes 524320 | tf_op jit(solution)/shard_map/ppermute | solution.py:808
  401.0 8.8 %collective-permute-done.19 = bf16[4,32,1024]{2,1,0:T(8,128)(2,1)S(1)} collective-permute-done((bf16[4,32,1024]{2,1,0:T(8,128)(2,1)S(1)}, bf16[4,32,1024]{2,1,0:T(8,128)(2,1)S(1)}, u32[]{:S(2)}, u32[]{:S(2)}) %collective-permute-start.19) | collective-permute-done | bytes 262176 | tf_op jit(solution)/shard_map/ppermute | solution.py:922
  420.1 8.4 %collective-permute-done.21 = bf16[6,32,1024]{2,1,0:T(8,128)(2,1)S(1)} collective-permute-done((bf16[6,32,1024]{2,1,0:T(8,128)(2,1)S(1)}, bf16[6,32,1024]{2,1,0:T(8,128)(2,1)S(1)}, u32[]{:S(2)}, u32[]{:S(2)}) %collective-permute-start.21) | collective-permute-done | bytes 393248 | tf_op jit(solution)/shard_map/ppermute | solution.py:929
  428.5 13.8 %collective-permute-done.22 = bf16[6,32,1024]{2,1,0:T(8,128)(2,1)S(1)} collective-permute-done((bf16[6,32,1024]{2,1,0:T(8,128)(2,1)S(1)}, bf16[6,32,1024]{2,1,0:T(8,128)(2,1)S(1)}, u32[]{:S(2)}, u32[]{:S(2)}) %collective-permute-start.22) | collective-permute-done | bytes 393248 | tf_op jit(solution)/shard_map/ppermute | solution.py:929
  453.9 8.8 %collective-permute-start.27 = (f32[104,128]{1,0:T(8,128)S(1)}, f32[104,128]{1,0:T(8,128)S(1)}, u32[]{:S(2)}, u32[]{:S(2)}) collective-permute-start(f32[104,128]{1,0:T(8,128)S(1)} %add.317), channel_id=1, source_target_pairs={{0,1},{1,0},{2,3},{3,2},{4,5},{5,4},{6,7},{7,6},{8,9},{9,8},{10,11... | collective-permute-start | bytes 159752 | tf_op jit(solution)/shard_map/ppermute | solution.py:938
  469.7 9.3 %lamb_feed.2 = (f32[2,8,256]{2,1,0:T(8,128)}, f32[2,8,1024]{2,1,0:T(8,128)}, f32[128,4096]{1,0:T(8,128)}, f32[128,4096]{1,0:T(8,128)}, f32[128,4096]{1,0:T(8,128...) custom-call(f32[128,4096]{1,0:T(8,128)} %refs_4_.1, f32[128,4096]{1,0:T(8,128)} %em_ref.3, ...), custom_call_target="tpu_custom_call" | custom-call | tf_op jit(solution)/shard_map/lamb_feed/pallas_call | solution.py:1006
  480.9 8.7 %lamb_attend.1 = (f32[2,8,1024]{2,1,0:T(8,128)}, f32[2,8,1024]{2,1,0:T(8,128)}, f32[128,3072]{1,0:T(8,128)}, f32[128,3072]{1,0:T(8,128)}, f32[128,3072]{1,0:T(8,...) custom-call(f32[128,3072]{1,0:T(8,128)} %refs_0_.1, f32[128,3072]{1,0:T(8,128)} %am_ref.1, ...), custom_call_target="tpu_custom_call" | custom-call | tf_op jit(solution)/shard_map/lamb_attend/pallas_call | solution.py:1032
  492.2 16.3 %all-reduce.7.cloned.1.call-done.eg_ref = bf16[4,128,1024]{2,1,0:T(8,128)(2,1)} async-done(((bf16[4,128,1024]{2,1,0:T(8,128)(2,1)}), bf16[4,128,1024]{2,1,0:T(8,128)(2,1)}) %all-reduce.7.cloned.1.call-update) | async-done | bytes 1048592 | tf_op jit(solution)/shard_map/psum | solution.py:960
  508.5 9.3 %lamb_feed.3 = (f32[2,8,256]{2,1,0:T(8,128)}, f32[2,8,1024]{2,1,0:T(8,128)}, f32[128,4096]{1,0:T(8,128)}, f32[128,4096]{1,0:T(8,128)}, f32[128,4096]{1,0:T(8,128...) custom-call(f32[128,4096]{1,0:T(8,128)} %refs_4_.1, ...), custom_call_target="tpu_custom_call", output_to_operand_aliasing={{2}: (8, {}), {3}: (9, {}), {4}: (10, {}), {5}: (11, {}), {... | custom-call | tf_op jit(solution)/shard_map/lamb_feed/pallas_call | solution.py:1006
  520.9 13.8 %psum.23.squares_ref = f32[10]{0:T(128)S(1)} all-reduce(f32[10]{0:T(128)S(1)} %concatenate.93), channel_id=1, replica_groups=mesh['seq'=8,'dp'=4] {'seq'}, use_global_device_ids=true, to_apply=%region_26.27 | all-reduce | flops 10 | bytes 80 | tf_op jit(solution)/shard_map/psum | solution.py:1059
  537.6 7.4 %renew.1 = (f32[128,3072]{1,0:T(8,128)}, f32[128,1024]{1,0:T(8,128)}, f32[128,4096]{1,0:T(8,128)}, f32[512,1024]{1,0:T(8,128)}) custom-call(f32[10]{0:T(128)} %copy-done.34, f32[128,3072]{1,0:T(8,128)} %refs_0_.1, f32[128,3072]{1,0:T(8,128)} %get-tuple-element.172.refs_1_, f32[128,1024]{1,0:T(8,128)} %refs_2_.1, f32[128,1024]{1,0:T(8,128)} %get-tuple-element.173.refs_3_, ...), custom_call_target="tpu_custom_call" | custom-call | tf_op jit(solution)/shard_map/renew/pallas_call | solution.py:1060
  (291 shorter events, 144.3 us)
Async XLA Ops:
  7.2 51.6 %all-gather.10.cloned.1.call-start = ((), (), s32[]{:S(2)}) async-start(), calls=%async_computation.4 | async-start | bytes 7077888 | tf_op jit(solution)/shard_map/all_gather | solution.py:556
  9.8 91.2 %all-gather.12.cloned.1.call-start = ((), (), s32[]{:S(2)}) async-start(), calls=%async_computation.5 | async-start | bytes 2359296 | tf_op jit(solution)/shard_map/all_gather | solution.py:556
  10.6 154.1 %all-gather.14.cloned.1.call-start = ((), (), s32[]{:S(2)}) async-start(), calls=%async_computation.6 | async-start | bytes 9437184 | tf_op jit(solution)/shard_map/all_gather | solution.py:556
  13.8 238.2 %all-gather.16.cloned.1.call-start = ((), (), s32[]{:S(2)}) async-start(), calls=%async_computation.7 | async-start | bytes 9437184 | tf_op jit(solution)/shard_map/all_gather | solution.py:556
  15.0 290.2 %reduce-scatter.2.cloned.1.call-start = ((), (), s32[]{:S(2)}) async-start(), calls=%async_computation.1 | async-start | bytes 9437184 | tf_op jit(solution)/shard_map/reduce_scatter | solution.py:941
  73.1 27.9 %collective-permute-start = (f32[72,1024]{1,0:T(8,128)}, f32[72,1024]{1,0:T(8,128)S(1)}, u32[]{:S(2)}, u32[]{:S(2)}) collective-permute-start(f32[72,1024]{1,0:T(8,128)} %get-tuple-element.121.done_ref), channel_id=1, source_target_pairs={{0,4},{4,8},{8,12},{12,16},{16,20},{20,24},{24,28},{1,5},{5,9},{9,... | collective-permute-start | bytes 884744 | tf_op jit(solution)/shard_map/ppermute | solution.py:721
  75.3 25.7 %collective-permute-start.1 = (f32[72,1024]{1,0:T(8,128)}, f32[72,1024]{1,0:T(8,128)S(1)}, u32[]{:S(2)}, u32[]{:S(2)}) collective-permute-start(f32[72,1024]{1,0:T(8,128)} %get-tuple-element.121.done_ref), channel_id=1, source_target_pairs={{0,8},{4,12},{8,16},{12,20},{16,24},{20,28},{1,9},{5,13},{9,17},{1... | collective-permute-start | bytes 884744 | tf_op jit(solution)/shard_map/ppermute | solution.py:721
  78.7 22.4 %collective-permute-start.2 = (f32[72,1024]{1,0:T(8,128)}, f32[72,1024]{1,0:T(8,128)S(1)}, u32[]{:S(2)}, u32[]{:S(2)}) collective-permute-start(f32[72,1024]{1,0:T(8,128)} %get-tuple-element.121.done_ref), channel_id=1, source_target_pairs={{0,12},{4,16},{8,20},{12,24},{16,28},{1,13},{5,17},{9,21},{13,25},... | collective-permute-start | bytes 884744 | tf_op jit(solution)/shard_map/ppermute | solution.py:721
  81.8 21.2 %collective-permute-start.3 = (f32[72,1024]{1,0:T(8,128)}, f32[72,1024]{1,0:T(8,128)S(1)}, u32[]{:S(2)}, u32[]{:S(2)}) collective-permute-start(f32[72,1024]{1,0:T(8,128)} %get-tuple-element.121.done_ref), channel_id=1, source_target_pairs={{0,16},{4,20},{8,24},{12,28},{1,17},{5,21},{9,25},{13,29},{2,18},{... | collective-permute-start | bytes 884744 | tf_op jit(solution)/shard_map/ppermute | solution.py:721
  203.2 23.0 %collective-permute-start.5 = (f32[72,1024]{1,0:T(8,128)S(1)}, f32[72,1024]{1,0:T(8,128)S(1)}, u32[]{:S(2)}, u32[]{:S(2)}) collective-permute-start(f32[72,1024]{1,0:T(8,128)S(1)} %copy-done.39), channel_id=1, source_target_pairs={{8,0},{12,4},{16,8},{20,12},{24,16},{28,20},{9,1},{13,5},{17,9},{2... | collective-permute-start | bytes 884744 | tf_op jit(solution)/shard_map/ppermute | solution.py:768
  204.5 22.2 %collective-permute-start.6 = (f32[72,1024]{1,0:T(8,128)S(1)}, f32[72,1024]{1,0:T(8,128)S(1)}, u32[]{:S(2)}, u32[]{:S(2)}) collective-permute-start(f32[72,1024]{1,0:T(8,128)S(1)} %copy-done.39), channel_id=1, source_target_pairs={{12,0},{16,4},{20,8},{24,12},{28,16},{13,1},{17,5},{21,9},{25,13},... | collective-permute-start | bytes 884744 | tf_op jit(solution)/shard_map/ppermute | solution.py:768
  205.8 20.9 %collective-permute-start.7 = (f32[72,1024]{1,0:T(8,128)S(1)}, f32[72,1024]{1,0:T(8,128)S(1)}, u32[]{:S(2)}, u32[]{:S(2)}) collective-permute-start(f32[72,1024]{1,0:T(8,128)S(1)} %copy-done.39), channel_id=1, source_target_pairs={{16,0},{20,4},{24,8},{28,12},{17,1},{21,5},{25,9},{29,13},{18,2},{... | collective-permute-start | bytes 884744 | tf_op jit(solution)/shard_map/ppermute | solution.py:768
  251.9 39.3 %collective-permute-start.8 = (f32[2,2,4,128,1024]{4,3,2,1,0:T(8,128)}, f32[2,2,4,128,1024]{4,3,2,1,0:T(8,128)}, u32[]{:S(2)}, u32[]{:S(2)}) collective-permute-start(f32[2,2,4,128,1024]{4,3,2,1,0:T(8,128)} %bitcast.162), channel_id=1, source_target_pairs={{0,4},{4,0},{8,12},{12,8},{16,20},{20,16},{24,28},{28,24},{1,5},{5... | collective-permute-start | bytes 25165832 | tf_op jit(solution)/shard_map/ppermute | solution.py:808
  290.2 24.3 %collective-permute-start.11 = (bf16[2,2,4,128,1024]{4,3,2,1,0:T(8,128)(2,1)}, bf16[2,2,4,128,1024]{4,3,2,1,0:T(8,128)(2,1)}, u32[]{:S(2)}, u32[]{:S(2)}) collective-permute-start(bf16[2,2,4,128,1024]{4,3,2,1,0:T(8,128)(2,1)} %bitcast.230), channel_id=1, source_target_pairs={{0,4},{4,0},{8,12},{12,8},{16,20},{20,16},{24,28},{28,24},{1,5},{5... | collective-permute-start | bytes 12582920 | tf_op jit(solution)/shard_map/ppermute | solution.py:808
  311.0 63.9 %all-reduce.5.cloned.1.call-start = ((), (), s32[]{:S(2)}) async-start(), calls=%async_computation.2 | async-start | bytes 2097152 | tf_op jit(solution)/shard_map/psum | solution.py:942
  311.0 26.3 %collective-permute-start.9 = (bf16[2,2,128,1024]{3,2,1,0:T(8,128)(2,1)}, bf16[2,2,128,1024]{3,2,1,0:T(8,128)(2,1)S(1)}, u32[]{:S(2)}, u32[]{:S(2)}) collective-permute-start(bf16[2,2,128,1024]{3,2,1,0:T(8,128)(2,1)} %get-tuple-element.146.refs_4_), channel_id=1, source_target_pairs={{0,8},{4,12},{8,0},{12,4},{16,24},{20,28},{24,16},{28,20},{1,9},{5... | collective-permute-start | bytes 3145736 | tf_op jit(solution)/shard_map/ppermute | solution.py:808
  312.4 37.8 %collective-permute-start.10 = (bf16[2,2,128,1024]{3,2,1,0:T(8,128)(2,1)}, bf16[2,2,128,1024]{3,2,1,0:T(8,128)(2,1)S(1)}, u32[]{:S(2)}, u32[]{:S(2)}) collective-permute-start(bf16[2,2,128,1024]{3,2,1,0:T(8,128)(2,1)} %get-tuple-element.149), channel_id=1, source_target_pairs={{0,16},{4,20},{8,24},{12,28},{16,0},{20,4},{24,8},{28,12},{1,17},{... | collective-permute-start | bytes 3145736 | tf_op jit(solution)/shard_map/ppermute | solution.py:808
  318.5 41.3 %collective-permute-start.14 = (bf16[2,2,128,1024]{3,2,1,0:T(8,128)(2,1)}, bf16[2,2,128,1024]{3,2,1,0:T(8,128)(2,1)S(1)}, u32[]{:S(2)}, u32[]{:S(2)}) collective-permute-start(bf16[2,2,128,1024]{3,2,1,0:T(8,128)(2,1)} %get-tuple-element.152.refs_6_), channel_id=1, source_target_pairs={{0,8},{4,12},{8,0},{12,4},{16,24},{20,28},{24,16},{28,20},{1,9},{5... | collective-permute-start | bytes 3145736 | tf_op jit(solution)/shard_map/ppermute | solution.py:808
  319.8 41.5 %collective-permute-start.15 = (bf16[2,2,128,1024]{3,2,1,0:T(8,128)(2,1)}, bf16[2,2,128,1024]{3,2,1,0:T(8,128)(2,1)}, u32[]{:S(2)}, u32[]{:S(2)}) collective-permute-start(bf16[2,2,128,1024]{3,2,1,0:T(8,128)(2,1)} %get-tuple-element.155), channel_id=1, source_target_pairs={{0,16},{4,20},{8,24},{12,28},{16,0},{20,4},{24,8},{28,12},{1,17},{... | collective-permute-start | bytes 3145736 | tf_op jit(solution)/shard_map/ppermute | solution.py:808
  355.4 19.6 %collective-permute-start.12 = (bf16[2,128,1024]{2,1,0:T(8,128)(2,1)}, bf16[2,128,1024]{2,1,0:T(8,128)(2,1)S(1)}, u32[]{:S(2)}, u32[]{:S(2)}) collective-permute-start(bf16[2,128,1024]{2,1,0:T(8,128)(2,1)} %get-tuple-element.153), channel_id=1, source_target_pairs={{0,16},{4,20},{8,24},{12,28},{16,0},{20,4},{24,8},{28,12},{1,17},{... | collective-permute-start | bytes 1572872 | tf_op jit(solution)/shard_map/ppermute | solution.py:808
  400.4 108.1 %all-reduce.7.cloned.1.call-start = ((), (), s32[]{:S(2)}) async-start(), calls=%async_computation.3 | async-start | bytes 2097152 | tf_op jit(solution)/shard_map/psum | solution.py:960
  417.4 24.9 %collective-permute-start.22 = (bf16[6,32,1024]{2,1,0:T(8,128)(2,1)S(1)}, bf16[6,32,1024]{2,1,0:T(8,128)(2,1)S(1)}, u32[]{:S(2)}, u32[]{:S(2)}) collective-permute-start(bf16[6,32,1024]{2,1,0:T(8,128)(2,1)S(1)} %pad_maximum_fusion.4.refs_0_), channel_id=1, source_target_pairs={{0,2},{1,3},{2,0},{3,1},{4,6},{5,7},{6,4},{7,5},{8,10},{9,11},{10,... | collective-permute-start | bytes 1179656 | tf_op jit(solution)/shard_map/ppermute | solution.py:929
  419.0 23.8 %collective-permute-start.23 = (bf16[6,32,1024]{2,1,0:T(8,128)(2,1)S(1)}, bf16[6,32,1024]{2,1,0:T(8,128)(2,1)S(1)}, u32[]{:S(2)}, u32[]{:S(2)}) collective-permute-start(bf16[6,32,1024]{2,1,0:T(8,128)(2,1)S(1)} %pad_maximum_fusion.4.refs_0_), channel_id=1, source_target_pairs={{0,3},{1,0},{2,1},{3,2},{4,7},{5,4},{6,5},{7,6},{8,11},{9,8},{10,9... | collective-permute-start | bytes 1179656 | tf_op jit(solution)/shard_map/ppermute | solution.py:929
  467.9 23.5 %collective-permute-start.28 = (f32[104,128]{1,0:T(8,128)S(1)}, f32[104,128]{1,0:T(8,128)S(1)}, u32[]{:S(2)}, u32[]{:S(2)}) collective-permute-start(f32[104,128]{1,0:T(8,128)S(1)} %add.318), channel_id=1, source_target_pairs={{0,2},{1,3},{2,0},{3,1},{4,6},{5,7},{6,4},{7,5},{8,10},{9,11},{10,... | collective-permute-start | bytes 159752 | tf_op jit(solution)/shard_map/ppermute | solution.py:938
  (57 other events, 542.3 us)
Sparse Core Ops, SparseCore 0:
  10.5 48.2 all-gather.9
  61.3 39.7 all-gather.11
  102.9 56.9 all-gather.13
  161.6 57.3 all-gather.15
  222.3 82.7 reduce-scatter.1
  323.1 51.8 all-reduce.4
  446.4 62.0 all-reduce.6
